TPU v7x, 128 devices: a whole 4x4x4 slice. The times are simulated.
128 devices in a mesh: space: 16 (over z, x), occ: 8 (over y, core).
Axes of the slice: x: 4, y: 4, z: 4, core: 2. Of those that a mesh axis runs over, the one named last changes fastest.
Arguments:
- factors: bfloat16 [48, 512, 8192], P('space', None, 'occ'), may hold values from -1.5 to 1.5
- pair_mask: int32 [48, 4], P('space'), may hold values from 0 to 1, as said below
Outputs:
- forward_k: float32 [48, 4, 512, 512], P('space', None, None, 'occ')
- backward_k: float32 [48, 4, 512, 512], P('space', None, 'occ')
Inputs may be any that keep to these rules, and one draw needn't show every extreme that they name: pair_mask[A, s] is 1 where the block pair (A, A + 1 + s) passed screening and 0 otherwise; it is 0 wherever A + 1 + s >= 48.
All inputs are finite; a program needn't handle non-finite values.
Results may differ from a plain program's by a relative error of at most 0.0003.
Values may be sent and summed in bfloat16 or wider, within the bound.
No kernel may reach another device: no remote copies, remote signals or barrier semaphores. Data moves between devices by JAX's collectives and lax.ppermute only.
A program may use at most 128 MiB of HBM per device.

v0:
```python
import jax
import jax.numpy as jnp
from jax import lax
from jax.sharding import PartitionSpec as P


def shifted(value, axis, by):
    size = lax.axis_size(axis)
    pairs = [(i, i + by) for i in range(size) if 0 <= i + by < size]
    return lax.ppermute(value, axis, pairs)


def on_device(factors, pair_mask):
    blocks, block_funcs, columns = factors.shape
    reach_slots = pair_mask.shape[1]
    ahead_count = -(-reach_slots // blocks)
    pieces = [factors]
    for step in range(1, ahead_count + 1):
        pieces.append(shifted(factors, "space", -step))
    window = jnp.concatenate(pieces, 0)
    partners = jnp.stack([window[1 + slot : 1 + slot + blocks] for slot in range(reach_slots)], 1)
    pair_terms = jnp.einsum("abk,asck->asbc", factors, partners, preferred_element_type=jnp.float32)
    pair_terms = pair_terms * pair_mask[:, :, None, None].astype(jnp.float32)
    forward = lax.psum_scatter(pair_terms, "occ", scatter_dimension=3, tiled=True)
    behind = []
    for step in range(ahead_count, 0, -1):
        behind.append(shifted(forward, "space", step))
    behind.append(forward)
    earlier = jnp.concatenate(behind, 0)
    anchor = ahead_count * blocks
    backs = []
    for slot in range(reach_slots):
        moved = earlier[anchor - 1 - slot : anchor - 1 - slot + blocks, slot]
        backs.append(jnp.swapaxes(moved, 1, 2))
    backward = jnp.stack(backs, 1)
    return (forward, backward)


def solution(mesh):
    in_specs = (P("space", None, "occ"), P("space", None))
    out_specs = (P("space", None, None, "occ"), P("space", None, "occ", None))
    return jax.shard_map(
        on_device, mesh=mesh, in_specs=in_specs, out_specs=out_specs, check_vma=False
    )
```

profile of v0, /device:TPU:96, one launch (start us, length us, event | category | flops | bytes accessed | tf_op | source)
XLA Modules:
  0.0 320.4 jit_solution(2940617533648007631)
XLA Ops:
  7.2 0.0 reduce-scatter.2.cloned.1.call-start
  7.2 4.5 %collective-permute-start = (bf16[3,512,1024]{2,1,0:T(8,128)(2,1)}, bf16[3,512,1024]{2,1,0:T(8,128)(2,1)S(1)}, u32[]{:S(2)}, u32[]{:S(2)}) collective-permute-start(bf16[3,512,1024]{2,1,0:T(8,128)(2,1)} %param.2), channel_id=1, source_target_pairs={{8,0},{16,8},{24,16},{32,24},{40,32},{48,40},{56,48},{64,56},{72,6... | collective-permute-start | bytes 9437192 | tf_op jit(solution)/shard_map/ppermute | solution.py:10
  11.7 2.7 collective-permute-start.1
  14.4 0.7 convert_element_type.4
  15.1 2.2 constant_dynamic-update-slice_fusion.1
  17.3 129.5 %collective-permute-done = bf16[3,512,1024]{2,1,0:T(8,128)(2,1)S(1)} collective-permute-done((bf16[3,512,1024]{2,1,0:T(8,128)(2,1)}, bf16[3,512,1024]{2,1,0:T(8,128)(2,1)S(1)}, u32[]{:S(2)}, u32[]{:S(2)}) %collective-permute-start) | collective-permute-done | bytes 3145760 | tf_op jit(solution)/shard_map/ppermute | solution.py:10
  146.8 0.0 collective-permute-done.1
  146.8 1.0 constant_dynamic-update-slice_fusion
  147.9 0.0 copy-start.1
  147.9 2.1 slice_bitcast_fusion.1
  150.0 0.8 copy-done.1
  150.8 10.5 %multiply_bitcast_fusion = f32[3,4,512,512]{2,3,1,0:T(8,128)} fusion(f32[3,4]{1,0:T(4,128)S(1)} %convert_element_type.4, bf16[3,1,512,1024]{3,2,1,0:T(8,128)(2,1)S(1)} %get-tuple-element.9, bf16[3,1,512,1024]{3,2,1,0:T(8,128)(2,1)S(1)} %bitcast.44, bf16[3,1,512,1024]{3,2,1,0:T(8,128)(2,1)} %get-tuple-element.5, ...), kind=kOutput, calls=%fused_computation.8 | convolution fusion | flops 6464471040 | bytes 28311600 | tf_op jit(solution)/shard_map/abk,asck->asbc/dot_general | solution.py:22
  161.3 0.0 reduce-scatter.2.cloned.1.call-update
  161.3 75.3 %reduce-scatter.2.cloned.1.call-done = f32[3,4,512,64]{2,3,1,0:T(8,128)} async-done(((f32[3,4,512,512]{2,3,1,0:T(8,128)}), f32[3,4,512,64]{2,3,1,0:T(8,128)}) %reduce-scatter.2.cloned.1.call-update) | async-done | bytes 1572880 | tf_op jit(solution)/shard_map/reduce_scatter | solution.py:24
  236.6 0.0 copy-start
  236.6 1.7 copy.7
  238.3 3.4 %collective-permute-start.2 = (f32[3,4,512,64]{2,3,0,1:T(8,128)S(1)}, f32[3,4,512,64]{2,3,0,1:T(8,128)S(1)}, u32[]{:S(2)}, u32[]{:S(2)}) collective-permute-start(f32[3,4,512,64]{2,3,0,1:T(8,128)S(1)} %copy.7), channel_id=1, source_target_pairs={{0,8},{8,16},{16,24},{24,32},{32,40},{40,48},{48,56},{56,64},{64,7... | collective-permute-start | bytes 4718600 | tf_op jit(solution)/shard_map/ppermute | solution.py:10
  241.7 0.0 copy-done
  241.7 4.6 %collective-permute-start.3 = (f32[3,4,512,64]{2,3,1,0:T(8,128)S(1)}, f32[3,4,512,64]{2,3,1,0:T(8,128)S(1)}, u32[]{:S(2)}, u32[]{:S(2)}) collective-permute-start(f32[3,4,512,64]{2,3,1,0:T(8,128)S(1)} %copy-done), channel_id=1, source_target_pairs={{0,16},{8,24},{16,32},{24,40},{32,48},{40,56},{48,64},{56,72},{64,... | collective-permute-start | bytes 4718600 | tf_op jit(solution)/shard_map/ppermute | solution.py:10
  246.3 33.1 %collective-permute-done.2 = f32[3,4,512,64]{2,3,0,1:T(8,128)S(1)} collective-permute-done((f32[3,4,512,64]{2,3,0,1:T(8,128)S(1)}, f32[3,4,512,64]{2,3,0,1:T(8,128)S(1)}, u32[]{:S(2)}, u32[]{:S(2)}) %collective-permute-start.2) | collective-permute-done | bytes 1572896 | tf_op jit(solution)/shard_map/ppermute | solution.py:10
  279.4 0.1 constant_dynamic-update-slice_fusion.3
  279.6 32.2 %collective-permute-done.3 = f32[3,4,512,64]{2,3,1,0:T(8,128)S(1)} collective-permute-done((f32[3,4,512,64]{2,3,1,0:T(8,128)S(1)}, f32[3,4,512,64]{2,3,1,0:T(8,128)S(1)}, u32[]{:S(2)}, u32[]{:S(2)}) %collective-permute-start.3) | collective-permute-done | bytes 1572896 | tf_op jit(solution)/shard_map/ppermute | solution.py:10
  311.8 0.1 constant_dynamic-update-slice_fusion.2
  312.0 0.1 slice_bitcast_fusion.4
  312.1 0.1 pad_maximum_fusion.1
  312.2 1.4 copy.10
  (1 shorter events, 0.0 us)
Async XLA Ops:
  7.2 229.4 %reduce-scatter.2.cloned.1.call-start = ((), (), s32[]{:S(2)}) async-start(), calls=%async_computation.1 | async-start | bytes 14155776 | tf_op jit(solution)/shard_map/reduce_scatter | solution.py:24
  7.2 139.6 %collective-permute-start = (bf16[3,512,1024]{2,1,0:T(8,128)(2,1)}, bf16[3,512,1024]{2,1,0:T(8,128)(2,1)S(1)}, u32[]{:S(2)}, u32[]{:S(2)}) collective-permute-start(bf16[3,512,1024]{2,1,0:T(8,128)(2,1)} %param.2), channel_id=1, source_target_pairs={{8,0},{16,8},{24,16},{32,24},{40,32},{48,40},{56,48},{64,56},{72,6... | collective-permute-start | bytes 9437192 | tf_op jit(solution)/shard_map/ppermute | solution.py:10
  11.7 135.1 %collective-permute-start.1 = (bf16[3,512,1024]{2,1,0:T(8,128)(2,1)}, bf16[3,512,1024]{2,1,0:T(8,128)(2,1)S(1)}, u32[]{:S(2)}, u32[]{:S(2)}) collective-permute-start(bf16[3,512,1024]{2,1,0:T(8,128)(2,1)} %param.2), channel_id=1, source_target_pairs={{16,0},{24,8},{32,16},{40,24},{48,32},{56,40},{64,48},{72,56},{80,... | collective-permute-start | bytes 9437192 | tf_op jit(solution)/shard_map/ppermute | solution.py:10
  147.9 2.9 copy-start.1
  236.6 5.1 %copy-start = (f32[3,4,512,64]{2,3,1,0:T(8,128)S(1)}, f32[3,4,512,64]{2,3,1,0:T(8,128)}, u32[]{:S(2)}) copy-start(f32[3,4,512,64]{2,3,1,0:T(8,128)} %reduce-scatter.2.cloned.1.call-done) | copy-start | bytes 4718596
  238.3 41.1 %collective-permute-start.2 = (f32[3,4,512,64]{2,3,0,1:T(8,128)S(1)}, f32[3,4,512,64]{2,3,0,1:T(8,128)S(1)}, u32[]{:S(2)}, u32[]{:S(2)}) collective-permute-start(f32[3,4,512,64]{2,3,0,1:T(8,128)S(1)} %copy.7), channel_id=1, source_target_pairs={{0,8},{8,16},{16,24},{24,32},{32,40},{40,48},{48,56},{56,64},{64,7... | collective-permute-start | bytes 4718600 | tf_op jit(solution)/shard_map/ppermute | solution.py:10
  241.7 70.1 %collective-permute-start.3 = (f32[3,4,512,64]{2,3,1,0:T(8,128)S(1)}, f32[3,4,512,64]{2,3,1,0:T(8,128)S(1)}, u32[]{:S(2)}, u32[]{:S(2)}) collective-permute-start(f32[3,4,512,64]{2,3,1,0:T(8,128)S(1)} %copy-done), channel_id=1, source_target_pairs={{0,16},{8,24},{16,32},{24,40},{32,48},{40,56},{48,64},{56,72},{64,... | collective-permute-start | bytes 4718600 | tf_op jit(solution)/shard_map/ppermute | solution.py:10
Sparse Core Ops, SparseCore 0:
  161.4 75.0 reduce-scatter.1
where the time goes:
time: 321 us; the launch traced here: 320 us
  waiting for transfers between devices  270 us (84%)
  starting transfers between devices  15.2 us (5%)
  between operations  14.1 us (4%)
  matrix products  10.5 us (3%)
  local copies, waits for them, and re-layouts  8.52 us (3%)
    ppermute x4, waiting for transfers between devices, shifted(): return lax.ppermute(value, axis, pairs)  195 us
    reduce_scatter x1, waiting for transfers between devices, on_device(): lax.psum_scatter(pair_terms, 'occ', scatter_dimension=3, tiled=True)  75.3 us
    ppermute x4, starting transfers between devices, shifted(): return lax.ppermute(value, axis, pairs)  15.2 us
    dot_general x1, matrix products, on_device(): jnp.einsum('abk,asck->asbc', factors, partners, preferred_element_type=jn...  10.5 us
  transfers between devices with their start and end apart: 5, of which 4 were waited for; matrix products, arithmetic and copies ran while one was open for 1% of the time, Pallas kernels for 0%

commit v1 on v0

v1 whole, which is shorter than its diff:
```python
import functools

import jax
import jax.numpy as jnp
from jax import lax
from jax.experimental import pallas as pl
from jax.experimental.pallas import tpu as pltpu
from jax.sharding import PartitionSpec as P

BF = 512
HALF = 256
SLICE = 64
CHIPS = 4
STEPS = 256.0
TOP = 32700.0
LN2 = 0.6931471805599453


def space_pairs(by):
    return [(i, i + by) for i in range(16) if 0 <= i + by < 16]


SIBLING = [(o, o ^ 1) for o in range(8)]
SAME_CORE = [[0, 2, 4, 6], [1, 3, 5, 7]]


def barrier(*values):
    return lax.optimization_barrier(values)


def half_rows(ref, index, core):
    return jnp.concatenate(
        [ref[index, pl.ds((2 * y + core) * SLICE, SLICE), :] for y in range(CHIPS)], 0
    )


def code(acc):
    parts = [acc[y * SLICE : (y + 1) * SLICE] for y in range(CHIPS)]
    tops = jnp.concatenate([jnp.max(jnp.abs(part), 0, keepdims=True) for part in parts], 0)
    level = jnp.ceil(jnp.log(jnp.maximum(tops, 1e-30) / TOP) * (STEPS / LN2))
    gain = jnp.exp(level * (-LN2 / STEPS))
    coded = [
        jnp.round(part * gain[y : y + 1]).astype(jnp.int32).astype(jnp.int16)
        for y, part in enumerate(parts)
    ]
    return coded, level.astype(jnp.int32)


def pair_kernel(pairs, names, core_ref, *refs):
    ins, (out_ref, *extra) = refs[: len(names)], refs[len(names) :]
    core = core_ref[0]
    by_name = dict(zip(names, ins))
    levels = []

    def left(name, index, other):
        return by_name[name + ("_sib" if other else "_own")][index]

    def right(name, index, other):
        if name == "half":
            return by_name["half"][int(other)]
        return half_rows(by_name[name + ("_sib" if other else "_own")], index, core)

    for p, (a, b) in enumerate(pairs):
        acc = None
        for other in (False, True):
            term = lax.dot_general(
                right(*b, other),
                left(*a, other),
                (((1,), (1,)), ((), ())),
                preferred_element_type=jnp.float32,
            )
            acc = term if acc is None else acc + term
        coded, level = code(acc)
        for y in range(CHIPS):
            out_ref[y, p * SLICE : (p + 1) * SLICE, :] = coded[y]
        levels.append(level)
    n = len(pairs)
    for y in range(CHIPS):
        rows = [level[y : y + 1] for level in levels]
        rows.append(jnp.zeros((16 - n, BF), jnp.int32))
        out_ref[y, n * SLICE : n * SLICE + 16, :] = jnp.concatenate(rows, 0).astype(jnp.int16)
    if extra:
        for other in (False, True):
            extra[0][int(other)] = right("mine", 1, other)


def pair_products(core, pairs, operands, with_half=False):
    names = list(operands)
    n = len(pairs)
    shapes = [jax.ShapeDtypeStruct((CHIPS, n * SLICE + 16, BF), jnp.int16)]
    if with_half:
        shapes.append(jax.ShapeDtypeStruct((2, HALF, 1024), jnp.bfloat16))
    out = pl.pallas_call(
        functools.partial(pair_kernel, pairs, names),
        out_shape=shapes,
        in_specs=[pl.BlockSpec(memory_space=pltpu.SMEM)]
        + [pl.BlockSpec(memory_space=pltpu.VMEM)] * len(names),
        out_specs=[pl.BlockSpec(memory_space=pltpu.VMEM)] * len(shapes),
        compiler_params=pltpu.CompilerParams(vmem_limit_bytes=40 << 20),
        cost_estimate=pl.CostEstimate(
            flops=n * 2 * HALF * BF * 2048, bytes_accessed=8 << 20, transcendentals=0
        ),
    )(core, *operands.values())
    return out if with_half else out[0]


def add_kernel(masks, got_ref, mask_ref, before_ref, *outs):
    n = len(masks)
    scales = [
        jnp.exp(got_ref[y, n * SLICE : n * SLICE + 16, :].astype(jnp.float32) * (LN2 / STEPS))
        for y in range(CHIPS)
    ]
    for p, ((before, block, slot), places) in enumerate(masks):
        total = None
        for y in range(CHIPS):
            part = got_ref[y, p * SLICE : (p + 1) * SLICE, :].astype(jnp.float32)
            part = part * scales[y][p : p + 1]
            total = part if total is None else total + part
        weight = (before_ref if before else mask_ref)[block, slot].astype(jnp.float32)
        total = total * weight
        for which, index in places:
            outs[which][index] = total


def add_parts(got, mask, before, masks, counts):
    return pl.pallas_call(
        functools.partial(add_kernel, masks),
        out_shape=[jax.ShapeDtypeStruct((k, SLICE, BF), jnp.float32) for k in counts],
        in_specs=[
            pl.BlockSpec(memory_space=pltpu.VMEM),
            pl.BlockSpec(memory_space=pltpu.SMEM),
            pl.BlockSpec(memory_space=pltpu.SMEM),
        ],
        out_specs=[pl.BlockSpec(memory_space=pltpu.VMEM)] * len(counts),
        compiler_params=pltpu.CompilerParams(vmem_limit_bytes=40 << 20),
        cost_estimate=pl.CostEstimate(flops=1 << 20, bytes_accessed=4 << 20, transcendentals=0),
    )(got, mask, before)


def finish_kernel(forward, backward, *refs):
    ins, (f_ref, b_ref) = refs[:-2], refs[-2:]
    for block in range(3):
        for slot in range(4):
            which, index = forward[block][slot]
            f_ref[block, slot] = ins[which][index].T
            which, index = backward[block][slot]
            b_ref[block, slot] = ins[which][index]


def finish(forward, backward, arrays):
    return pl.pallas_call(
        functools.partial(finish_kernel, forward, backward),
        out_shape=[
            jax.ShapeDtypeStruct((3, 4, BF, SLICE), jnp.float32),
            jax.ShapeDtypeStruct((3, 4, SLICE, BF), jnp.float32),
        ],
        in_specs=[pl.BlockSpec(memory_space=pltpu.VMEM)] * len(arrays),
        out_specs=[pl.BlockSpec(memory_space=pltpu.VMEM)] * 2,
        compiler_params=pltpu.CompilerParams(vmem_limit_bytes=40 << 20),
    )(*arrays)


def swap(value):
    return lax.ppermute(value, "occ", SIBLING)


def across(value):
    return lax.all_to_all(value, "occ", 0, 0, axis_index_groups=SAME_CORE)


def up(value):
    return lax.ppermute(value, "space", space_pairs(1))


def down(value):
    return lax.ppermute(value, "space", space_pairs(-1))


def on_device(own, mask):
    core = (lax.axis_index("occ") % 2).astype(jnp.int32).reshape(1)
    low = up(own[2:3])
    high = down(own[0:1])
    before = up(mask)
    own_sib = swap(own)
    mine = {"mine_own": own, "mine_sib": own_sib}
    M0, M1, M2 = ("mine", 0), ("mine", 1), ("mine", 2)
    coded0, half1 = pair_products(core, [(M0, M1), (M0, M2), (M1, M2)], mine, True)
    got0 = across(coded0)
    low, high, half1, middle = barrier(low, high, half1, own[1:2])
    low2 = up(middle)
    high2 = down(half1)
    low_sib, high_sib = swap((low, high))
    L, H = ("low", 0), ("high", 0)
    coded1 = pair_products(
        core,
        [(M0, H), (M1, H), (L, M0), (L, M1), (L, M2), (L, H)],
        mine | {"low_own": low, "low_sib": low_sib, "high_own": high, "high_sib": high_sib},
    )
    (sum0,) = add_parts(
        got0, mask, before, [((0, 0, 0), [(0, 0)]), ((0, 0, 1), [(0, 1)]), ((0, 1, 0), [(0, 2)])], [3]
    )
    got1 = across(coded1)
    low2_sib = swap(low2)
    coded2 = pair_products(
        core,
        [(M0, ("half", 0)), (M1, ("half", 0)), (L, M2)],
        mine | {"low_own": low2, "low_sib": low2_sib, "half": high2},
    )
    sum1, up1, down1 = add_parts(
        got1,
        mask,
        before,
        [
            ((0, 0, 2), [(0, 0), (1, 0)]),
            ((0, 1, 1), [(0, 1), (1, 1)]),
            ((1, 2, 0), [(0, 2), (2, 0)]),
            ((1, 2, 1), [(0, 3), (2, 1)]),
            ((1, 2, 2), [(0, 4), (2, 2)]),
            ((1, 2, 3), [(1, 2), (2, 3)]),
        ],
        [5, 3, 4],
    )
    below1 = up(up1)
    above1 = down(down1)
    got2 = across(coded2)
    sum2, up2, down2 = add_parts(
        got2,
        mask,
        before,
        [
            ((0, 0, 3), [(0, 0), (1, 0)]),
            ((0, 1, 2), [(0, 1), (1, 1)]),
            ((1, 1, 3), [(0, 2), (2, 0)]),
        ],
        [3, 2, 1],
    )
    below2 = up(up2)
    above2 = down(down2)
    S0, S1, S2, U1, D1, U2, D2 = range(7)
    forward = [
        [(S0, 0), (S0, 1), (S1, 0), (S2, 0)],
        [(S0, 2), (S1, 1), (S2, 1), (D2, 0)],
        [(D1, 0), (D1, 1), (D1, 2), (D1, 3)],
    ]
    backward = [
        [(S1, 2), (U1, 1), (U1, 0), (U1, 2)],
        [(S0, 0), (S1, 3), (U2, 1), (U2, 0)],
        [(S0, 2), (S0, 1), (S1, 4), (S2, 2)],
    ]
    return tuple(finish(forward, backward, [sum0, sum1, sum2, below1, above1, below2, above2]))


def solution(mesh):
    in_specs = (P("space", None, "occ"), P("space", None))
    out_specs = (P("space", None, None, "occ"), P("space", None, "occ", None))
    return jax.shard_map(
        on_device, mesh=mesh, in_specs=in_specs, out_specs=out_specs, check_vma=False
    )
```

time: 321 us -> 152 us (0.47)
  waiting for transfers between devices: 270 us -> 56 us
  starting transfers between devices: 15.2 us -> 37.4 us
  Pallas kernels: 0 us -> 21.5 us
  blocking collectives: 0 us -> 17.1 us
  between operations: 14.1 us -> 0.86 us
  matrix products: 10.5 us -> 0 us
  local copies, waits for them, and re-layouts: 8.52 us -> 17 us
    ppermute x4 -> x13, waiting for transfers between devices: 195 us -> 56 us  [the longest x4 31.4 us: down(): return lax.ppermute(value, 'space', space_pairs(-1))]
    reduce_scatter x1 -> x0, waiting for transfers between devices: 75.3 us -> none  [on_device(): lax.psum_scatter(pair_terms, 'occ', scatter_dimension=3, tiled=True)]
    pallas_call x0 -> x7, Pallas kernels: none -> 21.5 us  [the longest x3 14.3 us: pair_products(): pl.pallas_call(functools.partial(pair_kernel, pairs, names), out_shape=sh...]
    all_to_all x0 -> x1, blocking collectives: none -> 17.1 us  [across(): return lax.all_to_all(value, 'occ', 0, 0, axis_index_groups=SAME_CORE)]
    ppermute x4 -> x13, starting transfers between devices: 15.2 us -> 28.7 us  [the longest x4 17.9 us: down(): return lax.ppermute(value, 'space', space_pairs(-1))]
    dot_general x1 -> x0, matrix products: 10.5 us -> none  [on_device(): jnp.einsum('abk,asck->asbc', factors, partners, preferred_element_type=jn...]
    all_to_all x0 -> x2, starting transfers between devices: none -> 8.66 us  [across(): return lax.all_to_all(value, 'occ', 0, 0, axis_index_groups=SAME_CORE)]
    unnamed x7 -> x34, local copies, waits for them, and re-layouts: 4.43 us -> 11.2 us
  transfers between devices with their start and end apart: 5 -> 15, of which waited for: 4 -> 10; matrix products, arithmetic and copies ran while one was open for 1% -> 3% of each run, Pallas kernels for 0% -> 13%
where the time goes in v1:
time: 152 us; the launch traced here: 150 us
  waiting for transfers between devices  56 us (37%)
  starting transfers between devices  37.4 us (25%)
  Pallas kernels  21.5 us (14%)
  blocking collectives  17.1 us (11%)
  local copies, waits for them, and re-layouts  17 us (11%)
    ppermute x4, waiting for transfers between devices, down(): return lax.ppermute(value, 'space', space_pairs(-1))  31.4 us
    ppermute x5, waiting for transfers between devices, up(): return lax.ppermute(value, 'space', space_pairs(1))  22.7 us
    ppermute x4, starting transfers between devices, down(): return lax.ppermute(value, 'space', space_pairs(-1))  17.9 us
    all_to_all x1, blocking collectives, across(): return lax.all_to_all(value, 'occ', 0, 0, axis_index_groups=SAME_CORE)  17.1 us
    pallas_call x3, Pallas kernels, pair_products(): pl.pallas_call(functools.partial(pair_kernel, pairs, names), out_shape=sh...  14.3 us
    unnamed x34, local copies, waits for them, and re-layouts  11.2 us
    ppermute x5, starting transfers between devices, up(): return lax.ppermute(value, 'space', space_pairs(1))  10.3 us
    all_to_all x2, starting transfers between devices, across(): return lax.all_to_all(value, 'occ', 0, 0, axis_index_groups=SAME_CORE)  8.66 us
  transfers between devices with their start and end apart: 15, of which 10 were waited for; matrix products, arithmetic and copies ran while one was open for 3% of the time, Pallas kernels for 13%

profile of v1, /device:TPU:96, one launch (start us, length us, event | category | flops | bytes accessed | tf_op | source)
XLA Modules:
  0.0 149.8 jit_solution(13777897335153175029)
XLA Ops:
  0.7 3.8 %fusion = (bf16[1,512,1024]{2,1,0:T(8,128)(2,1)}, bf16[1,512,1024]{2,1,0:T(8,128)(2,1)}, bf16[1,512,1024]{2,1,0:T(8,128)(2,1)}) fusion(bf16[3,512,1024]{2,1,0:T(8,128)(2,1)} %refs_0_.5), kind=kLoop, calls=%fused_computation | loop fusion | bytes 6291456 | tf_op jit(solution)/shard_map/slice | solution.py:189
  4.5 4.5 %collective-permute-start.3 = (bf16[1,512,1024]{2,1,0:T(8,128)(2,1)}, bf16[1,512,1024]{2,1,0:T(8,128)(2,1)}, u32[]{:S(2)}, u32[]{:S(2)}) collective-permute-start(bf16[1,512,1024]{2,1,0:T(8,128)(2,1)} %get-tuple-element.29), channel_id=1, source_target_pairs={{8,0},{16,8},{24,16},{32,24},{40,32},{48,40},{56,48},{64,56},{72,6... | collective-permute-start | bytes 3145736 | tf_op jit(solution)/shard_map/ppermute | solution.py:176
  9.0 1.9 %collective-permute-start.2 = (bf16[1,512,1024]{2,1,0:T(8,128)(2,1)}, bf16[1,512,1024]{2,1,0:T(8,128)(2,1)}, u32[]{:S(2)}, u32[]{:S(2)}) collective-permute-start(bf16[1,512,1024]{2,1,0:T(8,128)(2,1)} %get-tuple-element.30), channel_id=1, source_target_pairs={{0,8},{8,16},{16,24},{24,32},{32,40},{40,48},{48,56},{56,64},{64,7... | collective-permute-start | bytes 3145736 | tf_op jit(solution)/shard_map/ppermute | solution.py:172
  11.0 3.9 %shard_map.41 = (s16[4,208,512]{2,1,0:T(8,128)(2,1)S(1)}, bf16[2,256,1024]{2,1,0:T(8,128)(2,1)S(1)}) custom-call(s32[1]{0:T(128)} %bitcast.core_ref, bf16[3,512,1024]{2,1,0:T(8,128)(2,1)S(1)} %copy-done, bf16[3,512,1024]{2,1,0:T(8,128)(2,1)} %collective-permute-done.refs_1_), custom_call_target="tpu_custom_call" | custom-call | flops 1610612736 | bytes 8388608 | tf_op jit(solution)/shard_map/pallas_call | solution.py:93
  14.9 17.5 %collective-permute-done.3.refs_4_ = bf16[1,512,1024]{2,1,0:T(8,128)(2,1)} collective-permute-done((bf16[1,512,1024]{2,1,0:T(8,128)(2,1)}, bf16[1,512,1024]{2,1,0:T(8,128)(2,1)}, u32[]{:S(2)}, u32[]{:S(2)}) %collective-permute-start.3) | collective-permute-done | bytes 1048608 | tf_op jit(solution)/shard_map/ppermute | solution.py:176
  32.4 6.2 %collective-permute-done.2.refs_2_ = bf16[1,512,1024]{2,1,0:T(8,128)(2,1)} collective-permute-done((bf16[1,512,1024]{2,1,0:T(8,128)(2,1)}, bf16[1,512,1024]{2,1,0:T(8,128)(2,1)}, u32[]{:S(2)}, u32[]{:S(2)}) %collective-permute-start.2) | collective-permute-done | bytes 1048608 | tf_op jit(solution)/shard_map/ppermute | solution.py:172
  39.1 1.9 %collective-permute-start.6 = (bf16[1,512,1024]{2,1,0:T(8,128)(2,1)}, bf16[1,512,1024]{2,1,0:T(8,128)(2,1)}, u32[]{:S(2)}, u32[]{:S(2)}) collective-permute-start(bf16[1,512,1024]{2,1,0:T(8,128)(2,1)} %get-tuple-element.19), channel_id=1, source_target_pairs={{0,8},{8,16},{16,24},{24,32},{32,40},{40,48},{48,56},{56,64},{64,7... | collective-permute-start | bytes 3145736 | tf_op jit(solution)/shard_map/ppermute | solution.py:172
  41.5 1.5 collective-permute-done.5.refs_5_
  43.0 6.2 %shard_map.43 = s16[4,400,512]{2,1,0:T(8,128)(2,1)S(1)} custom-call(s32[1]{0:T(128)} %bitcast.core_ref, bf16[3,512,1024]{2,1,0:T(8,128)(2,1)S(1)} %copy-done, bf16[3,512,1024]{2,1,0:T(8,128)(2,1)} %collective-permute-done.refs_1_, bf16[1,512,1024]{2,1,0:T(8,128)(2,1)} %collective-permute-done.2.refs_2_, ...), custom_call_target="tpu_custom_call" | custom-call | flops 3221225472 | bytes 8388608 | tf_op jit(solution)/shard_map/pallas_call | solution.py:93
  49.2 1.2 copy-done.1
  50.4 4.5 %all-to-all-start.1 = ((s16[4,400,512]{2,1,0:T(8,128)(2,1)}), s16[4,400,512]{2,1,0:T(8,128)(2,1)}, u32[]{:S(2)}, u32[]{:S(2)}) async-start(s16[4,400,512]{2,1,0:T(8,128)(2,1)} %copy-done.1), calls=%async_computation.1 | async-start | bytes 3276800 | tf_op jit(solution)/shard_map/all_to_all | solution.py:168
  54.9 4.1 %collective-permute-start.8 = (bf16[2,256,1024]{2,1,0:T(8,128)(2,1)}, bf16[2,256,1024]{2,1,0:T(8,128)(2,1)S(1)}, u32[]{:S(2)}, u32[]{:S(2)}) collective-permute-start(bf16[2,256,1024]{2,1,0:T(8,128)(2,1)} %copy-done.16), channel_id=1, source_target_pairs={{8,0},{16,8},{24,16},{32,24},{40,32},{48,40},{56,48},{64,56},{72,6... | collective-permute-start | bytes 3145736 | tf_op jit(solution)/shard_map/ppermute | solution.py:176
  59.0 9.5 %collective-permute-done.6.refs_2_ = bf16[1,512,1024]{2,1,0:T(8,128)(2,1)} collective-permute-done((bf16[1,512,1024]{2,1,0:T(8,128)(2,1)}, bf16[1,512,1024]{2,1,0:T(8,128)(2,1)}, u32[]{:S(2)}, u32[]{:S(2)}) %collective-permute-start.6) | collective-permute-done | bytes 1048608 | tf_op jit(solution)/shard_map/ppermute | solution.py:172
  68.5 13.6 %collective-permute-done.8.refs_4_ = bf16[2,256,1024]{2,1,0:T(8,128)(2,1)S(1)} collective-permute-done((bf16[2,256,1024]{2,1,0:T(8,128)(2,1)}, bf16[2,256,1024]{2,1,0:T(8,128)(2,1)S(1)}, u32[]{:S(2)}, u32[]{:S(2)}) %collective-permute-start.8) | collective-permute-done | bytes 1048608 | tf_op jit(solution)/shard_map/ppermute | solution.py:176
  82.1 4.2 %shard_map.45 = s16[4,208,512]{2,1,0:T(8,128)(2,1)S(1)} custom-call(s32[1]{0:T(128)} %bitcast.core_ref, bf16[3,512,1024]{2,1,0:T(8,128)(2,1)S(1)} %copy-done, bf16[3,512,1024]{2,1,0:T(8,128)(2,1)} %collective-permute-done.refs_1_, bf16[1,512,1024]{2,1,0:T(8,128)(2,1)} %collective-permute-done.6.refs_2_, ...), custom_call_target="tpu_custom_call" | custom-call | flops 1610612736 | bytes 8388608 | tf_op jit(solution)/shard_map/pallas_call | solution.py:93
  87.2 17.1 %all_to_all.15.got_ref = s16[4,208,512]{2,1,0:T(8,128)(2,1)} all-to-all(s16[4,208,512]{2,1,0:T(8,128)(2,1)} %copy-done.2), channel_id=1, replica_groups={{0,2,4,6},{1,3,5,7},{8,10,12,14},{9,11,13,15},{16,18,20,22},{17,19,21,2..., dimensions={0} | all-to-all | bytes 1703936 | tf_op jit(solution)/shard_map/all_to_all | solution.py:168
  104.2 4.2 %all-to-all-start = ((s16[4,208,512]{2,1,0:T(8,128)(2,1)}), s16[4,208,512]{2,1,0:T(8,128)(2,1)}, u32[]{:S(2)}, u32[]{:S(2)}) async-start(s16[4,208,512]{2,1,0:T(8,128)(2,1)} %copy-done.4), calls=%async_computation | async-start | bytes 1703936 | tf_op jit(solution)/shard_map/all_to_all | solution.py:168
  108.4 1.9 %collective-permute-start.1 = (s32[3,4]{1,0:T(4,128)S(1)}, s32[3,4]{1,0:T(4,128)S(1)}, u32[]{:S(2)}, u32[]{:S(2)}) collective-permute-start(s32[3,4]{1,0:T(4,128)S(1)} %copy-done.15), channel_id=1, source_target_pairs={{0,8},{8,16},{16,24},{24,32},{32,40},{40,48},{48,56},{56,64},{64,7... | collective-permute-start | bytes 152 | tf_op jit(solution)/shard_map/ppermute | solution.py:172
  110.4 5.7 %collective-permute-done.1.before_ref = s32[3,4]{1,0:T(4,128)S(1)} collective-permute-done((s32[3,4]{1,0:T(4,128)S(1)}, s32[3,4]{1,0:T(4,128)S(1)}, u32[]{:S(2)}, u32[]{:S(2)}) %collective-permute-start.1) | collective-permute-done | bytes 80 | tf_op jit(solution)/shard_map/ppermute | solution.py:172
  116.0 2.4 %shard_map.44 = (f32[5,64,512]{2,1,0:T(8,128)S(1)}, f32[3,64,512]{2,1,0:T(8,128)}, f32[4,64,512]{2,1,0:T(8,128)S(1)}) custom-call(s16[4,400,512]{2,1,0:T(8,128)(2,1)} %all-to-all-done.1.got_ref, s32[3,4]{1,0:T(4,128)S(1)} %copy-done.15, s32[3,4]{1,0:T(4,128)S(1)} %collective-permute-done.1.before_ref), custom_call_target="tpu_custom_call" | custom-call | flops 1048576 | bytes 4194304 | tf_op jit(solution)/shard_map/pallas_call | solution.py:126
  119.3 3.2 %collective-permute-start.10 = (f32[4,64,512]{2,1,0:T(8,128)S(1)}, f32[4,64,512]{2,1,0:T(8,128)S(1)}, u32[]{:S(2)}, u32[]{:S(2)}) collective-permute-start(f32[4,64,512]{2,1,0:T(8,128)S(1)} %get-tuple-element.23), channel_id=1, source_target_pairs={{8,0},{16,8},{24,16},{32,24},{40,32},{48,40},{56,48},{64,56},{72,6... | collective-permute-start | bytes 1572872 | tf_op jit(solution)/shard_map/ppermute | solution.py:176
  122.5 2.6 %collective-permute-start.9 = (f32[3,64,512]{2,1,0:T(8,128)}, f32[3,64,512]{2,1,0:T(8,128)S(1)}, u32[]{:S(2)}, u32[]{:S(2)}) collective-permute-start(f32[3,64,512]{2,1,0:T(8,128)} %get-tuple-element.22), channel_id=1, source_target_pairs={{0,8},{8,16},{16,24},{24,32},{32,40},{40,48},{48,56},{56,64},{64,7... | collective-permute-start | bytes 1179656 | tf_op jit(solution)/shard_map/ppermute | solution.py:172
  125.1 1.1 copy-done.3
  126.3 1.4 shard_map.46
  127.7 1.9 %collective-permute-start.11 = (f32[2,64,512]{2,1,0:T(8,128)S(1)}, f32[2,64,512]{2,1,0:T(8,128)S(1)}, u32[]{:S(2)}, u32[]{:S(2)}) collective-permute-start(f32[2,64,512]{2,1,0:T(8,128)S(1)} %get-tuple-element.24), channel_id=1, source_target_pairs={{0,8},{8,16},{16,24},{24,32},{32,40},{40,48},{48,56},{56,64},{64,7... | collective-permute-start | bytes 786440 | tf_op jit(solution)/shard_map/ppermute | solution.py:172
  129.6 6.0 %collective-permute-start.12 = (f32[1,64,512]{2,1,0:T(8,128)}, f32[1,64,512]{2,1,0:T(8,128)S(1)}, u32[]{:S(2)}, u32[]{:S(2)}) collective-permute-start(f32[1,64,512]{2,1,0:T(8,128)} %get-tuple-element.25), channel_id=1, source_target_pairs={{8,0},{16,8},{24,16},{32,24},{40,32},{48,40},{56,48},{64,56},{72,6... | collective-permute-start | bytes 393224 | tf_op jit(solution)/shard_map/ppermute | solution.py:176
  135.7 1.4 shard_map.42.refs_0_
  139.1 1.0 collective-permute-done.11.refs_5_
  140.8 1.1 copy-done.6
  141.9 1.0 copy-done.8
  145.8 2.0 %shard_map.47 = (f32[3,4,512,64]{3,2,1,0:T(8,128)S(1)}, f32[3,4,64,512]{3,2,1,0:T(8,128)}) custom-call(f32[3,64,512]{2,1,0:T(8,128)S(1)} %shard_map.42.refs_0_, f32[5,64,512]{2,1,0:T(8,128)S(1)} %copy-done.6, f32[3,64,512]{2,1,0:T(8,128)S(1)} %copy-done.10, f32[3,64,512]{2,1,0:T(8,128)S(1)} %collective-permute-done.9.refs_3_, f32[4,64,512]{2,1,0:T(8,128)S(1)} %copy-done.8, ...), custom_call_target="tpu_custom_call" | custom-call | tf_op jit(solution)/shard_map/pallas_call | solution.py:151
  147.8 2.0 %copy.4 = f32[3,4,512,64]{2,3,1,0:T(8,128)} copy(f32[3,4,512,64]{3,2,1,0:T(8,128)S(1)} %get-tuple-element.26) | data formatting | bytes 3145728 | tf_op jit(solution)/shard_map/pallas_call | solution.py:151
  (42 shorter events, 8.4 us)
Async XLA Ops:
  0.6 10.3 %copy-start = (bf16[3,512,1024]{2,1,0:T(8,128)(2,1)S(1)}, bf16[3,512,1024]{2,1,0:T(8,128)(2,1)}, u32[]{:S(2)}) copy-start(bf16[3,512,1024]{2,1,0:T(8,128)(2,1)} %refs_0_.5) | copy-start | bytes 9437188
  0.6 10.3 %collective-permute-start = (bf16[3,512,1024]{2,1,0:T(8,128)(2,1)}, bf16[3,512,1024]{2,1,0:T(8,128)(2,1)}, u32[]{:S(2)}, u32[]{:S(2)}) collective-permute-start(bf16[3,512,1024]{2,1,0:T(8,128)(2,1)} %refs_0_.5), channel_id=1, source_target_pairs={{0,1},{1,0},{2,3},{3,2},{4,5},{5,4},{6,7},{7,6},{8,9},{9,8},{10,11... | collective-permute-start | bytes 9437192 | tf_op jit(solution)/shard_map/ppermute | solution.py:164
  4.5 27.9 %collective-permute-start.3 = (bf16[1,512,1024]{2,1,0:T(8,128)(2,1)}, bf16[1,512,1024]{2,1,0:T(8,128)(2,1)}, u32[]{:S(2)}, u32[]{:S(2)}) collective-permute-start(bf16[1,512,1024]{2,1,0:T(8,128)(2,1)} %get-tuple-element.29), channel_id=1, source_target_pairs={{8,0},{16,8},{24,16},{32,24},{40,32},{48,40},{56,48},{64,56},{72,6... | collective-permute-start | bytes 3145736 | tf_op jit(solution)/shard_map/ppermute | solution.py:176
  9.0 29.6 %collective-permute-start.2 = (bf16[1,512,1024]{2,1,0:T(8,128)(2,1)}, bf16[1,512,1024]{2,1,0:T(8,128)(2,1)}, u32[]{:S(2)}, u32[]{:S(2)}) collective-permute-start(bf16[1,512,1024]{2,1,0:T(8,128)(2,1)} %get-tuple-element.30), channel_id=1, source_target_pairs={{0,8},{8,16},{16,24},{24,32},{32,40},{40,48},{48,56},{56,64},{64,7... | collective-permute-start | bytes 3145736 | tf_op jit(solution)/shard_map/ppermute | solution.py:172
  14.9 26.6 %copy-start.4 = (s16[4,208,512]{2,1,0:T(8,128)(2,1)}, s16[4,208,512]{2,1,0:T(8,128)(2,1)S(1)}, u32[]{:S(2)}) copy-start(s16[4,208,512]{2,1,0:T(8,128)(2,1)S(1)} %get-tuple-element.14) | copy-start | bytes 2555908
  14.9 26.6 %copy-start.16 = (bf16[2,256,1024]{2,1,0:T(8,128)(2,1)}, bf16[2,256,1024]{2,1,0:T(8,128)(2,1)S(1)}, u32[]{:S(2)}) copy-start(bf16[2,256,1024]{2,1,0:T(8,128)(2,1)S(1)} %get-tuple-element.20) | copy-start | bytes 3145732
  38.6 2.9 %collective-permute-start.4 = (bf16[1,512,1024]{2,1,0:T(8,128)(2,1)}, bf16[1,512,1024]{2,1,0:T(8,128)(2,1)S(1)}, u32[]{:S(2)}, u32[]{:S(2)}) collective-permute-start(bf16[1,512,1024]{2,1,0:T(8,128)(2,1)} %collective-permute-done.2.refs_2_), channel_id=1, source_target_pairs={{0,1},{1,0},{2,3},{3,2},{4,5},{5,4},{6,7},{7,6},{8,9},{9,8},{10,11... | collective-permute-start | bytes 3145736 | tf_op jit(solution)/shard_map/ppermute | solution.py:164
  38.6 4.4 %collective-permute-start.5 = (bf16[1,512,1024]{2,1,0:T(8,128)(2,1)}, bf16[1,512,1024]{2,1,0:T(8,128)(2,1)S(1)}, u32[]{:S(2)}, u32[]{:S(2)}) collective-permute-start(bf16[1,512,1024]{2,1,0:T(8,128)(2,1)} %collective-permute-done.3.refs_4_), channel_id=1, source_target_pairs={{0,1},{1,0},{2,3},{3,2},{4,5},{5,4},{6,7},{7,6},{8,9},{9,8},{10,11... | collective-permute-start | bytes 3145736 | tf_op jit(solution)/shard_map/ppermute | solution.py:164
  39.1 29.4 %collective-permute-start.6 = (bf16[1,512,1024]{2,1,0:T(8,128)(2,1)}, bf16[1,512,1024]{2,1,0:T(8,128)(2,1)}, u32[]{:S(2)}, u32[]{:S(2)}) collective-permute-start(bf16[1,512,1024]{2,1,0:T(8,128)(2,1)} %get-tuple-element.19), channel_id=1, source_target_pairs={{0,8},{8,16},{16,24},{24,32},{32,40},{40,48},{48,56},{56,64},{64,7... | collective-permute-start | bytes 3145736 | tf_op jit(solution)/shard_map/ppermute | solution.py:172
  49.2 1.2 copy-start.1
  50.4 36.8 %all-to-all-start.1 = ((s16[4,400,512]{2,1,0:T(8,128)(2,1)}), s16[4,400,512]{2,1,0:T(8,128)(2,1)}, u32[]{:S(2)}, u32[]{:S(2)}) async-start(s16[4,400,512]{2,1,0:T(8,128)(2,1)} %copy-done.1), calls=%async_computation.1 | async-start | bytes 3276800 | tf_op jit(solution)/shard_map/all_to_all | solution.py:168
  54.9 27.2 %collective-permute-start.8 = (bf16[2,256,1024]{2,1,0:T(8,128)(2,1)}, bf16[2,256,1024]{2,1,0:T(8,128)(2,1)S(1)}, u32[]{:S(2)}, u32[]{:S(2)}) collective-permute-start(bf16[2,256,1024]{2,1,0:T(8,128)(2,1)} %copy-done.16), channel_id=1, source_target_pairs={{8,0},{16,8},{24,16},{32,24},{40,32},{48,40},{56,48},{64,56},{72,6... | collective-permute-start | bytes 3145736 | tf_op jit(solution)/shard_map/ppermute | solution.py:176
  68.5 13.6 %collective-permute-start.7 = (bf16[1,512,1024]{2,1,0:T(8,128)(2,1)}, bf16[1,512,1024]{2,1,0:T(8,128)(2,1)S(1)}, u32[]{:S(2)}, u32[]{:S(2)}) collective-permute-start(bf16[1,512,1024]{2,1,0:T(8,128)(2,1)} %collective-permute-done.6.refs_2_), channel_id=1, source_target_pairs={{0,1},{1,0},{2,3},{3,2},{4,5},{5,4},{6,7},{7,6},{8,9},{9,8},{10,11... | collective-permute-start | bytes 3145736 | tf_op jit(solution)/shard_map/ppermute | solution.py:164
  86.3 0.9 copy-start.2
  87.2 21.3 %copy-start.15 = (s32[3,4]{1,0:T(4,128)S(1)}, s32[3,4]{1,0:T(4,128)}, u32[]{:S(2)}) copy-start(s32[3,4]{1,0:T(4,128)} %mask_ref.5) | copy-start | bytes 148
  104.2 31.4 %all-to-all-start = ((s16[4,208,512]{2,1,0:T(8,128)(2,1)}), s16[4,208,512]{2,1,0:T(8,128)(2,1)}, u32[]{:S(2)}, u32[]{:S(2)}) async-start(s16[4,208,512]{2,1,0:T(8,128)(2,1)} %copy-done.4), calls=%async_computation | async-start | bytes 1703936 | tf_op jit(solution)/shard_map/all_to_all | solution.py:168
  108.4 7.6 %collective-permute-start.1 = (s32[3,4]{1,0:T(4,128)S(1)}, s32[3,4]{1,0:T(4,128)S(1)}, u32[]{:S(2)}, u32[]{:S(2)}) collective-permute-start(s32[3,4]{1,0:T(4,128)S(1)} %copy-done.15), channel_id=1, source_target_pairs={{0,8},{8,16},{16,24},{24,32},{32,40},{40,48},{48,56},{56,64},{64,7... | collective-permute-start | bytes 152 | tf_op jit(solution)/shard_map/ppermute | solution.py:172
  118.4 0.8 copy-start.5
  119.3 18.0 %collective-permute-start.10 = (f32[4,64,512]{2,1,0:T(8,128)S(1)}, f32[4,64,512]{2,1,0:T(8,128)S(1)}, u32[]{:S(2)}, u32[]{:S(2)}) collective-permute-start(f32[4,64,512]{2,1,0:T(8,128)S(1)} %get-tuple-element.23), channel_id=1, source_target_pairs={{8,0},{16,8},{24,16},{32,24},{40,32},{48,40},{56,48},{64,56},{72,6... | collective-permute-start | bytes 1572872 | tf_op jit(solution)/shard_map/ppermute | solution.py:176
  122.5 14.8 %collective-permute-start.9 = (f32[3,64,512]{2,1,0:T(8,128)}, f32[3,64,512]{2,1,0:T(8,128)S(1)}, u32[]{:S(2)}, u32[]{:S(2)}) collective-permute-start(f32[3,64,512]{2,1,0:T(8,128)} %get-tuple-element.22), channel_id=1, source_target_pairs={{0,8},{8,16},{16,24},{24,32},{32,40},{40,48},{48,56},{56,64},{64,7... | collective-permute-start | bytes 1179656 | tf_op jit(solution)/shard_map/ppermute | solution.py:172
  125.1 1.2 copy-start.3
  127.7 13.1 %copy-start.9 = (f32[3,64,512]{2,1,0:T(8,128)}, f32[3,64,512]{2,1,0:T(8,128)S(1)}, u32[]{:S(2)}) copy-start(f32[3,64,512]{2,1,0:T(8,128)S(1)} %get-tuple-element.21.refs_2_) | copy-start | bytes 1179652
  127.7 12.4 %collective-permute-start.11 = (f32[2,64,512]{2,1,0:T(8,128)S(1)}, f32[2,64,512]{2,1,0:T(8,128)S(1)}, u32[]{:S(2)}, u32[]{:S(2)}) collective-permute-start(f32[2,64,512]{2,1,0:T(8,128)S(1)} %get-tuple-element.24), channel_id=1, source_target_pairs={{0,8},{8,16},{16,24},{24,32},{32,40},{40,48},{48,56},{56,64},{64,7... | collective-permute-start | bytes 786440 | tf_op jit(solution)/shard_map/ppermute | solution.py:172
  129.6 8.9 %collective-permute-start.12 = (f32[1,64,512]{2,1,0:T(8,128)}, f32[1,64,512]{2,1,0:T(8,128)S(1)}, u32[]{:S(2)}, u32[]{:S(2)}) collective-permute-start(f32[1,64,512]{2,1,0:T(8,128)} %get-tuple-element.25), channel_id=1, source_target_pairs={{8,0},{16,8},{24,16},{32,24},{40,32},{48,40},{56,48},{64,56},{72,6... | collective-permute-start | bytes 393224 | tf_op jit(solution)/shard_map/ppermute | solution.py:176
  137.3 0.8 copy-start.7
  138.5 0.7 copy-start.13
  140.1 0.7 copy-start.11
  140.8 1.1 copy-start.6
  141.9 1.0 copy-start.8
  142.9 1.0 copy-start.10
  143.9 0.9 copy-start.12
  144.9 0.9 copy-start.14

commit v2 on v0

v2 whole, which is shorter than its diff:
```python
import functools

import jax
import jax.numpy as jnp
from jax import lax
from jax.experimental import pallas as pl
from jax.experimental.pallas import tpu as pltpu
from jax.sharding import PartitionSpec as P

BF = 512
COLS = 1024
HALF = 256
SLICE = 64
CHIPS = 4
STEPS = 256.0
TOP = 32700.0
LN2 = 0.6931471805599453

VMEM = pl.BlockSpec(memory_space=pltpu.VMEM)
SMEM = pl.BlockSpec(memory_space=pltpu.SMEM)
HBM = pl.BlockSpec(memory_space=pltpu.HBM)
PARAMS = pltpu.CompilerParams(vmem_limit_bytes=18 << 20)
OUTS = [jax.ShapeDtypeStruct((3, 4, SLICE, BF), jnp.float32)] * 2


def coded_rows(count):
    return count * SLICE + 16


def code(values):
    tops = jnp.concatenate([jnp.max(jnp.abs(v), 0, keepdims=True) for v in values], 0)
    level = jnp.ceil(jnp.log(jnp.maximum(tops, 1e-30) / TOP) * (STEPS / LN2))
    gain = jnp.exp(level * (-LN2 / STEPS))
    coded = [
        jnp.round(v * gain[i : i + 1]).astype(jnp.int32).astype(jnp.int16)
        for i, v in enumerate(values)
    ]
    return coded, level.astype(jnp.int32)


def level_rows(levels):
    rows = list(levels) + [jnp.zeros((16 - len(levels), BF), jnp.int32)]
    return jnp.concatenate(rows, 0).astype(jnp.int16)


def scales_of(rows):
    return jnp.exp(rows.astype(jnp.float32) * (LN2 / STEPS))


def pair_kernel(pairs, blocks, halved, names, together, lines, place_ref, *refs):
    ins = dict(zip(names, refs))
    outs = refs[len(names) :]
    if lines:
        outs, lines_ref = outs[:-1], outs[-1]
        lines_ref[...] = ins[lines][0, HALF : HALF + 16, :BF].astype(jnp.float32)
    if together:
        outs = [outs[0].at[d] for d in range(CHIPS)]
    core, chip = place_ref[0], place_ref[1]
    order = [d if together else (chip + d) % CHIPS for d in range(CHIPS)]

    def read(piece, start, rows):
        name, index = piece
        return ins[name][index, pl.ds(start, rows), :]

    def slices(pieces):
        rows = []
        for o in order:
            if len(pieces) == 2:
                start = (2 * (o % 2) + core) * SLICE
                low, high = (read(piece, start, SLICE) for piece in pieces)
                rows.append(jnp.where(o < 2, low, high))
            elif ins[pieces[0][0]].shape[1] == HALF:
                rows.append(read(pieces[0], o * SLICE, SLICE))
            else:
                rows.append(read(pieces[0], (2 * o + core) * SLICE, SLICE))
        return jnp.concatenate(rows, 0)

    def both_slices(pieces):
        rows = [read(pieces[0], o * 2 * SLICE, 2 * SLICE) for o in order]
        return jnp.concatenate(rows, 0)

    levels = []
    for p, (a, b) in enumerate(pairs):
        acc = None
        shared = a in halved
        for part in range(2):
            right = (both_slices if shared else slices)(blocks[b][part])
            pieces = blocks[a][part]
            rows = (HALF if shared else BF) // len(pieces)
            term = [
                lax.dot_general(
                    right,
                    read(piece, 0, rows),
                    (((1,), (1,)), ((), ())),
                    preferred_element_type=jnp.float32,
                )
                for piece in pieces
            ]
            term = jnp.concatenate(term, 1)
            acc = term if acc is None else acc + term
        if shared:
            parts = [
                jnp.concatenate(
                    [acc[k * SLICE : (k + 1) * SLICE] for k in (2 * d, 2 * d + 1)], 1
                )
                for d in range(CHIPS)
            ]
        else:
            parts = [acc[d * SLICE : (d + 1) * SLICE] for d in range(CHIPS)]
        coded, level = code(parts)
        for d in range(CHIPS):
            outs[d][p * SLICE : (p + 1) * SLICE, :] = coded[d]
        levels.append(level)
    end = len(pairs) * SLICE
    for d in range(CHIPS):
        outs[d][end : end + 16, :] = level_rows([v[d : d + 1] for v in levels])


def pair_products(place, pairs, blocks, operands, halved=(), together=False, lines=None):
    names = list(operands)
    n = len(pairs)
    rows = coded_rows(n)
    shapes = [jax.ShapeDtypeStruct((rows, BF), jnp.int16)] * CHIPS
    if together:
        shapes = [jax.ShapeDtypeStruct((CHIPS, rows, BF), jnp.int16)]
    if lines:
        shapes.append(jax.ShapeDtypeStruct((16, BF), jnp.float32))
    return pl.pallas_call(
        functools.partial(pair_kernel, pairs, blocks, halved, names, together, lines),
        out_shape=shapes,
        in_specs=[SMEM] + [VMEM] * len(names),
        out_specs=[VMEM] * len(shapes),
        compiler_params=PARAMS,
        cost_estimate=pl.CostEstimate(flops=1 << 20, bytes_accessed=1 << 16, transcendentals=0),
    )(place, *operands.values())


def pieces_kernel(place_ref, low_ref, high_ref, low_a_ref, low_b_ref, other_ref):
    low_a_ref[0] = low_ref[0, :HALF, :]
    low_b_ref[0] = low_ref[0, HALF:, :]
    core = 1 - place_ref[0]
    for y in range(CHIPS):
        start = (2 * y + core) * SLICE
        other_ref[0, y * SLICE : (y + 1) * SLICE, :] = high_ref[0, pl.ds(start, SLICE), :]


def pieces_for_sibling(place, low, high):
    return pl.pallas_call(
        pieces_kernel,
        out_shape=[jax.ShapeDtypeStruct((1, HALF, COLS), jnp.bfloat16)] * 3,
        in_specs=[SMEM, VMEM, VMEM],
        out_specs=[VMEM] * 3,
        compiler_params=PARAMS,
        cost_estimate=pl.CostEstimate(flops=1 << 10, bytes_accessed=1 << 10, transcendentals=0),
    )(place, low, high)


def second_kernel(place_ref, mask_ref, own_ref, sib_ref, up_ref, down_ref):
    core = place_ref[0]
    lines = [
        jnp.full((1, COLS), mask_ref[k // 4, k % 4].astype(jnp.float32), jnp.float32)
        for k in range(12)
    ]
    lines.append(jnp.zeros((4, COLS), jnp.float32))
    lines = jnp.concatenate(lines, 0).astype(jnp.bfloat16)
    for i, source in enumerate((own_ref, sib_ref)):
        up_ref[i, :HALF, :] = source[1, pl.ds(core * HALF, HALF), :]
        up_ref[i, HALF:, :] = lines
        for y in range(CHIPS):
            down_ref[i, y * SLICE : (y + 1) * SLICE, :] = source[
                1, pl.ds((2 * y + core) * SLICE, SLICE), :
            ]


def second_factors(place, mask, own, sib):
    return pl.pallas_call(
        second_kernel,
        out_shape=[
            jax.ShapeDtypeStruct((2, HALF + 16, COLS), jnp.bfloat16),
            jax.ShapeDtypeStruct((2, HALF, COLS), jnp.bfloat16),
        ],
        in_specs=[SMEM, SMEM, VMEM, VMEM],
        out_specs=[VMEM] * 2,
        compiler_params=PARAMS,
        cost_estimate=pl.CostEstimate(flops=1 << 10, bytes_accessed=1 << 10, transcendentals=0),
    )(place, mask, own, sib)


def add_kernel(places, first, sizes, halves, n_gots, lined, place_ref, *refs):
    gots, refs = refs[:n_gots], refs[n_gots:]
    if n_gots == 1:
        gots = [gots[0].at[d] for d in range(CHIPS)]
    mask_ref, refs = refs[0], refs[1:]
    if lined:
        lines_ref, refs = refs[0], refs[1:]
    if not first:
        refs = refs[2:]
    (f_ref, b_ref), refs = refs[:2], refs[2:]
    messages, refs = refs[: len(sizes)], refs[len(sizes) :]
    if halves:
        (same_ref, cross_ref, kept_ref, swap_ref), refs = refs[:4], refs[4:]
    sums, sems = refs
    levels = [[None] * size for size in sizes]
    writes = []
    n = len(places)
    scales = [scales_of(gots[d][n * SLICE : n * SLICE + 16, :]) for d in range(CHIPS)]
    for p, ((theirs, block, slot), goals) in enumerate(places):
        total = None
        for d in range(CHIPS):
            part = gots[d][p * SLICE : (p + 1) * SLICE, :].astype(jnp.float32)
            part = part * scales[d][p : p + 1]
            total = part if total is None else total + part
        if theirs:
            line = lines_ref[block * 4 + slot : block * 4 + slot + 1, :]
            total = total * line
        else:
            total = total * mask_ref[block, slot].astype(jnp.float32)
        coded = None
        for kind, *goal in goals:
            if kind == "m":
                which, index = goal
                if coded is None:
                    (coded,), level = code([total])
                levels[which][index] = level
                messages[which][index * SLICE : (index + 1) * SLICE, :] = coded
            elif kind == "halves":
                first_core = place_ref[0] == 0
                low, high = total[:, :HALF], total[:, HALF:]
                kept = jnp.where(first_core, low, high)
                other = jnp.where(first_core, high, low)
                kept_ref[...] = kept
                swap_ref[...] = other
                for ref, half in ((same_ref, kept), (cross_ref, other)):
                    (coded_half,), level = code([half])
                    ref[:SLICE, :] = coded_half
                    zeros = jnp.zeros((15, HALF), jnp.int32)
                    ref[SLICE:, :] = jnp.concatenate([level, zeros], 0).astype(jnp.int16)
            else:
                sums[p] = total
                writes.append((p, (f_ref if kind == "f" else b_ref).at[goal[0], goal[1]]))
    for m, size in enumerate(sizes):
        messages[m][size * SLICE : size * SLICE + 16, :] = level_rows(levels[m])
    writes = [
        pltpu.make_async_copy(sums.at[p], target, sems.at[k])
        for k, (p, target) in enumerate(writes)
    ]
    for copy in writes:
        copy.start()
    for copy in writes:
        copy.wait()


def add_parts(place, gots, masks, outs, places, sizes=(), halves=False):
    n = len(places)
    first = outs is None
    earlier = [] if first else list(outs)
    at = 1 + len(gots) + len(masks)
    shapes = OUTS + [jax.ShapeDtypeStruct((coded_rows(k), BF), jnp.int16) for k in sizes]
    if halves:
        shapes += [jax.ShapeDtypeStruct((SLICE + 16, HALF), jnp.int16)] * 2
        shapes += [jax.ShapeDtypeStruct((SLICE, HALF), jnp.float32)] * 2
    return pl.pallas_call(
        functools.partial(add_kernel, places, first, sizes, halves, len(gots), len(masks) > 1),
        out_shape=shapes,
        in_specs=[SMEM] + [VMEM] * len(gots) + [SMEM, VMEM][: len(masks)] + [HBM] * len(earlier),
        out_specs=[HBM] * 2 + [VMEM] * (len(shapes) - 2),
        scratch_shapes=[
            pltpu.VMEM((n, SLICE, BF), jnp.float32),
            pltpu.SemaphoreType.DMA((2 * n,)),
        ],
        input_output_aliases={} if first else {at: 0, at + 1: 1},
        compiler_params=PARAMS,
        cost_estimate=pl.CostEstimate(flops=1 << 20, bytes_accessed=1 << 16, transcendentals=0),
    )(place, *gots, *masks, *earlier)


def place_kernel(places, pair_places, place_ref, *refs):
    n, n_pairs = len(places), len(pair_places)
    messages, refs = refs[:n], refs[n:]
    halves, refs = refs[: 2 * n_pairs], refs[2 * n_pairs :]
    f_ref, b_ref, sums, sems = refs[2:]
    results = []
    for m, goals in enumerate(places):
        size = len(goals)
        scales = scales_of(messages[m][size * SLICE : size * SLICE + 16, :])
        for p, goal in enumerate(goals):
            part = messages[m][p * SLICE : (p + 1) * SLICE, :].astype(jnp.float32)
            results.append((part * scales[p : p + 1], goal))
    for m, goal in enumerate(pair_places):
        parts = []
        for half in halves[2 * m : 2 * m + 2]:
            part = half[:SLICE, :].astype(jnp.float32)
            if half.dtype == jnp.int16:
                part = part * scales_of(half[SLICE : SLICE + 16, :])[:1]
            parts.append(part)
        first_core = place_ref[0] == 0
        low = jnp.where(first_core, parts[0], parts[1])
        high = jnp.where(first_core, parts[1], parts[0])
        results.append((jnp.concatenate([low, high], 1), goal))
    writes = []
    for k, (value, (kind, block, slot)) in enumerate(results):
        sums[k] = value
        target = (f_ref if kind == "f" else b_ref).at[block, slot]
        writes.append(pltpu.make_async_copy(sums.at[k], target, sems.at[k]))
    for copy in writes:
        copy.start()
    for copy in writes:
        copy.wait()


def place_results(place, messages, halves, outs, places, pair_places=()):
    ins = list(messages) + list(halves)
    total = sum(map(len, places)) + len(pair_places)
    return pl.pallas_call(
        functools.partial(place_kernel, places, pair_places),
        out_shape=OUTS,
        in_specs=[SMEM] + [VMEM] * len(ins) + [HBM] * 2,
        out_specs=[HBM] * 2,
        scratch_shapes=[
            pltpu.VMEM((total, SLICE, BF), jnp.float32),
            pltpu.SemaphoreType.DMA((total,)),
        ],
        input_output_aliases={1 + len(ins): 0, 2 + len(ins): 1},
        compiler_params=PARAMS,
        cost_estimate=pl.CostEstimate(flops=1 << 20, bytes_accessed=1 << 16, transcendentals=0),
    )(place, *ins, *outs)


def swap(value):
    return lax.ppermute(value, "occ", [(o, o ^ 1) for o in range(2 * CHIPS)])


def chips_on(value, by):
    pairs = [
        (2 * y + core, 2 * ((y + by) % CHIPS) + core) for y in range(CHIPS) for core in range(2)
    ]
    return lax.ppermute(value, "occ", pairs)


def across(value):
    groups = [[2 * y + core for y in range(CHIPS)] for core in range(2)]
    return lax.all_to_all(value, "occ", 0, 0, axis_index_groups=groups)


def to_chips(parts):
    return [parts[0]] + [chips_on(parts[d], d) for d in range(1, CHIPS)]


def along_space(value, by):
    size = lax.axis_size("space")
    return lax.ppermute(value, "space", [(i, i + by) for i in range(size) if 0 <= i + by < size])


def up(value):
    return along_space(value, 1)


def down(value):
    return along_space(value, -1)


def down_across(value):
    groups, members = lax.axis_size("space"), 2 * CHIPS
    pairs = [
        (g * members + o, (g - 1) * members + (o ^ 1)) for g in range(1, groups) for o in range(members)
    ]
    return lax.ppermute(value, ("space", "occ"), pairs)


def on_device(own, mask):
    index = lax.axis_index("occ")
    place = jnp.stack([index % 2, index // 2]).astype(jnp.int32)
    own_sib = swap(own)
    low = own[2:3]
    low, own_after = lax.optimization_barrier((low, own))
    high = own_after[0:1]
    low, high = up(low), down(high)
    mine = {"own": own, "sib": own_sib}
    blocks = {k: ([("own", k)], [("sib", k)]) for k in range(3)}
    low2, high2 = second_factors(place, mask, own, own_sib)
    low2, high2 = up(low2), down(high2)
    coded0 = pair_products(place, [(0, 1), (0, 2), (1, 2)], blocks, mine, together=True)
    got0 = [across(coded0[0])]
    low, high, got0 = lax.optimization_barrier((low, high, got0))
    low_a, low_b, other = pieces_for_sibling(place, low, high)
    low_as, low_bs, high_sib = swap((low_a, low_b, other))
    blocks["L"] = [("low", 0)], [("low_as", 0), ("low_bs", 0)]
    blocks["H"] = [("high", 0)], [("high_sib", 0)]
    coded1 = pair_products(
        place,
        [("L", 0), ("L", 1), ("L", 2), (0, "H"), (1, "H"), ("L", "H")],
        blocks,
        mine | {"low": low, "low_as": low_as, "low_bs": low_bs, "high": high, "high_sib": high_sib},
    )
    got1 = to_chips(coded1)
    outs = add_parts(
        place,
        got0,
        [mask],
        None,
        [
            ((0, 0, 0), [("f", 0, 0), ("b", 1, 0)]),
            ((0, 0, 1), [("f", 0, 1), ("b", 2, 1)]),
            ((0, 1, 0), [("f", 1, 0), ("b", 2, 0)]),
        ],
    )
    low2, high2, _, outs = lax.optimization_barrier((low2, high2, coded1[0], outs))
    blocks["H2"] = [("high2", 0)], [("high2", 1)]
    blocks["L2"] = [("low2", 0)], [("low2", 1)]
    *coded2, lines = pair_products(
        place,
        [(0, "H2"), (1, "H2"), ("L2", 2)],
        blocks,
        mine | {"high2": high2, "low2": low2},
        halved=("L2",),
        lines="low2",
    )
    got2 = to_chips(coded2)
    *outs, up1, down1 = add_parts(
        place,
        got1,
        [mask, lines],
        outs,
        [
            ((1, 2, 0), [("b", 0, 0), ("m", 1, 0)]),
            ((1, 2, 1), [("b", 1, 1), ("m", 1, 1)]),
            ((1, 2, 2), [("b", 2, 2), ("m", 1, 2)]),
            ((0, 0, 2), [("f", 0, 2), ("m", 0, 0)]),
            ((0, 1, 1), [("f", 1, 1), ("m", 0, 1)]),
            ((1, 2, 3), [("m", 0, 2), ("m", 1, 3)]),
        ],
        (3, 4),
    )
    below1, above1 = up(up1), down(down1)
    *outs, up2, same, cross, kept, other = add_parts(
        place,
        got2,
        [mask, lines],
        outs,
        [
            ((0, 0, 3), [("f", 0, 3), ("m", 0, 0)]),
            ((0, 1, 2), [("f", 1, 2), ("m", 0, 1)]),
            ((1, 1, 3), [("halves",)]),
        ],
        (2,),
        halves=True,
    )
    below2, same, cross = up(up2), down(same), down_across(cross)
    other = swap(other)
    outs = place_results(
        place,
        [below1, above1],
        [kept, other],
        outs,
        [
            [("b", 0, 2), ("b", 0, 1), ("b", 0, 3)],
            [("f", 2, 0), ("f", 2, 1), ("f", 2, 2), ("f", 2, 3)],
        ],
        [("b", 2, 3)],
    )
    forward, backward = place_results(
        place, [below2], [same, cross], outs, [[("b", 1, 3), ("b", 1, 2)]], [("f", 1, 3)]
    )
    return jnp.swapaxes(forward, 2, 3), backward


def solution(mesh):
    in_specs = (P("space", None, "occ"), P("space", None))
    out_specs = (P("space", None, None, "occ"), P("space", None, "occ", None))
    return jax.shard_map(
        on_device, mesh=mesh, in_specs=in_specs, out_specs=out_specs, check_vma=False
    )
```

time: 321 us -> 101 us (0.31)
  waiting for transfers between devices: 270 us -> 17.6 us
  starting transfers between devices: 15.2 us -> 47.4 us
  Pallas kernels: 0 us -> 28.4 us
  between operations: 14.1 us -> 0.88 us
  matrix products: 10.5 us -> 0 us
    ppermute x4 -> x20, waiting for transfers between devices: 195 us -> 17.6 us  [the longest x8 11.1 us: along_space(): lax.ppermute(value, 'space', [(i, i + by) for i in range(size) if 0 <= i...]
    reduce_scatter x1 -> x0, waiting for transfers between devices: 75.3 us -> none  [on_device(): lax.psum_scatter(pair_terms, 'occ', scatter_dimension=3, tiled=True)]
    pallas_call x0 -> x10, Pallas kernels: none -> 28.4 us  [the longest x3 14.5 us: pair_products(): pl.pallas_call(functools.partial(pair_kernel, pairs, blocks, halved, name...]
    ppermute x4 -> x20, starting transfers between devices: 15.2 us -> 42.8 us  [the longest x8 28.2 us: along_space(): lax.ppermute(value, 'space', [(i, i + by) for i in range(size) if 0 <= i...]
    dot_general x1 -> x0, matrix products: 10.5 us -> none  [on_device(): jnp.einsum('abk,asck->asbc', factors, partners, preferred_element_type=jn...]
    slice x0 -> x2, local copies, waits for them, and re-layouts: none -> 4.68 us  [the longest x1 2.41 us: on_device(): low = own[2:3]]
    all_to_all x0 -> x1, starting transfers between devices: none -> 4.59 us  [across(): return lax.all_to_all(value, 'occ', 0, 0, axis_index_groups=groups)]
    unnamed x7 -> x6, local copies, waits for them, and re-layouts: 4.43 us -> 0.92 us
  transfers between devices with their start and end apart: 5 -> 21, of which waited for: 4 -> 9; matrix products, arithmetic and copies ran while one was open for 1% -> 5% of each run, Pallas kernels for 0% -> 27%
where the time goes in v2:
time: 101 us; the launch traced here: 99.9 us
  starting transfers between devices  47.4 us (47%)
  Pallas kernels  28.4 us (28%)
  waiting for transfers between devices  17.6 us (17%)
  local copies, waits for them, and re-layouts  5.59 us (6%)
    ppermute x8, starting transfers between devices, along_space(): lax.ppermute(value, 'space', [(i, i + by) for i in range(size) if 0 <= i...  28.2 us
    pallas_call x3, Pallas kernels, pair_products(): pl.pallas_call(functools.partial(pair_kernel, pairs, blocks, halved, name...  14.5 us
    ppermute x6, starting transfers between devices, chips_on(): return lax.ppermute(value, 'occ', pairs)  11.8 us
    ppermute x8, waiting for transfers between devices, along_space(): lax.ppermute(value, 'space', [(i, i + by) for i in range(size) if 0 <= i...  11.1 us
    pallas_call x3, Pallas kernels, add_parts(): pl.pallas_call(functools.partial(add_kernel, places, first, sizes, halves...  5.77 us
    all_to_all x1, starting transfers between devices, across(): return lax.all_to_all(value, 'occ', 0, 0, axis_index_groups=groups)  4.59 us
    pallas_call x1, Pallas kernels, second_factors(): pl.pallas_call(second_kernel, out_shape=[jax.ShapeDtypeStruct((2, HALF +...  3.43 us
    pallas_call x2, Pallas kernels, place_results(): pl.pallas_call(functools.partial(place_kernel, places, pair_places), out_...  3.04 us
  transfers between devices with their start and end apart: 21, of which 9 were waited for; matrix products, arithmetic and copies ran while one was open for 5% of the time, Pallas kernels for 27%

profile of v2, /device:TPU:96, one launch (start us, length us, event | category | flops | bytes accessed | tf_op | source)
XLA Modules:
  0.0 99.9 jit_solution(9305685951653636770)
XLA Ops:
  0.7 2.4 %slice.6 = bf16[1,512,1024]{2,1,0:T(8,128)(2,1)} slice(bf16[3,512,1024]{2,1,0:T(8,128)(2,1)} %refs_0_.5), slice={[2:3], [0:512], [0:1024]} | slice | bytes 2097152 | tf_op jit(solution)/shard_map/slice | solution.py:374
  3.1 2.3 %slice.7 = bf16[1,512,1024]{2,1,0:T(8,128)(2,1)} slice(bf16[3,512,1024]{2,1,0:T(8,128)(2,1)} %refs_0_.5), slice={[0:1], [0:512], [0:1024]} | slice | bytes 2097152 | tf_op jit(solution)/shard_map/slice | solution.py:376
  5.4 4.5 %collective-permute-start.4 = (bf16[1,512,1024]{2,1,0:T(8,128)(2,1)}, bf16[1,512,1024]{2,1,0:T(8,128)(2,1)}, u32[]{:S(2)}, u32[]{:S(2)}) collective-permute-start(bf16[1,512,1024]{2,1,0:T(8,128)(2,1)} %slice.7), channel_id=1, source_target_pairs={{8,0},{16,8},{24,16},{32,24},{40,32},{48,40},{56,48},{64,56},{72,6... | collective-permute-start | bytes 3145736 | tf_op jit(solution)/shard_map/ppermute | solution.py:351
  9.9 1.9 %collective-permute-start.3 = (bf16[1,512,1024]{2,1,0:T(8,128)(2,1)}, bf16[1,512,1024]{2,1,0:T(8,128)(2,1)}, u32[]{:S(2)}, u32[]{:S(2)}) collective-permute-start(bf16[1,512,1024]{2,1,0:T(8,128)(2,1)} %slice.6), channel_id=1, source_target_pairs={{0,8},{8,16},{16,24},{24,32},{32,40},{40,48},{48,56},{56,64},{64,7... | collective-permute-start | bytes 3145736 | tf_op jit(solution)/shard_map/ppermute | solution.py:351
  11.9 3.9 %shard_map.42 = s16[4,208,512]{2,1,0:T(8,128)(2,1)S(1)} custom-call(s32[2]{0:T(128)S(1)} %pad_add_fusion.place_ref, bf16[3,512,1024]{2,1,0:T(8,128)(2,1)S(1)} %copy-done, bf16[3,512,1024]{2,1,0:T(8,128)(2,1)} %collective-permute-done.sib_ref.refs_1_), custom_call_target="tpu_custom_call" | custom-call | flops 1048576 | bytes 65536 | tf_op jit(solution)/shard_map/pallas_call | solution.py:128
  16.7 4.6 %all-to-all-start = ((s16[4,208,512]{2,1,0:T(8,128)(2,1)}), s16[4,208,512]{2,1,0:T(8,128)(2,1)}, u32[]{:S(2)}, u32[]{:S(2)}) async-start(s16[4,208,512]{2,1,0:T(8,128)(2,1)} %copy-done.1), calls=%async_computation | async-start | bytes 1703936 | tf_op jit(solution)/shard_map/all_to_all | solution.py:342
  21.3 3.4 %shard_map.41 = (bf16[2,272,1024]{2,1,0:T(8,128)(2,1)}, bf16[2,256,1024]{2,1,0:T(8,128)(2,1)}) custom-call(s32[2]{0:T(128)S(1)} %pad_add_fusion.place_ref, s32[3,4]{1,0:T(4,128)S(1)} %copy-done.2, bf16[3,512,1024]{2,1,0:T(8,128)(2,1)S(1)} %copy-done, bf16[3,512,1024]{2,1,0:T(8,128)(2,1)} %collective-permute-done.sib_ref.refs_1_), custom_call_target="tpu_custom_call" | custom-call | flops 1024 | bytes 1024 | tf_op jit(solution)/shard_map/pallas_call | solution.py:176
  24.8 2.8 %collective-permute-start.1 = (bf16[2,272,1024]{2,1,0:T(8,128)(2,1)}, bf16[2,272,1024]{2,1,0:T(8,128)(2,1)}, u32[]{:S(2)}, u32[]{:S(2)}) collective-permute-start(bf16[2,272,1024]{2,1,0:T(8,128)(2,1)} %get-tuple-element.42), channel_id=1, source_target_pairs={{0,8},{8,16},{16,24},{24,32},{32,40},{40,48},{48,56},{56,64},{64,7... | collective-permute-start | bytes 3342344 | tf_op jit(solution)/shard_map/ppermute | solution.py:351
  27.6 5.1 %collective-permute-start.2 = (bf16[2,256,1024]{2,1,0:T(8,128)(2,1)}, bf16[2,256,1024]{2,1,0:T(8,128)(2,1)}, u32[]{:S(2)}, u32[]{:S(2)}) collective-permute-start(bf16[2,256,1024]{2,1,0:T(8,128)(2,1)} %get-tuple-element.43), channel_id=1, source_target_pairs={{8,0},{16,8},{24,16},{32,24},{40,32},{48,40},{56,48},{64,56},{72,6... | collective-permute-start | bytes 3145736 | tf_op jit(solution)/shard_map/ppermute | solution.py:351
  33.7 6.6 %collective-permute-done.3.low_ref.refs_2_ = bf16[1,512,1024]{2,1,0:T(8,128)(2,1)} collective-permute-done((bf16[1,512,1024]{2,1,0:T(8,128)(2,1)}, bf16[1,512,1024]{2,1,0:T(8,128)(2,1)}, u32[]{:S(2)}, u32[]{:S(2)}) %collective-permute-start.3) | collective-permute-done | bytes 1048608 | tf_op jit(solution)/shard_map/ppermute | solution.py:351
  40.2 1.7 %shard_map.43 = (bf16[1,256,1024]{2,1,0:T(8,128)(2,1)S(1)}, bf16[1,256,1024]{2,1,0:T(8,128)(2,1)S(1)}, bf16[1,256,1024]{2,1,0:T(8,128)(2,1)S(1)}) custom-call(s32[2]{0:T(128)S(1)} %pad_add_fusion.place_ref, bf16[1,512,1024]{2,1,0:T(8,128)(2,1)} %collective-permute-done.3.low_ref.refs_2_, bf16[1,512,1024]{2,1,0:T(8,128)(2,1)} %collective-permute-done.4.high_ref.refs_5_), custom_call_target="tpu_custom_call" | custom-call | flops 1024 | bytes 1024 | tf_op jit(solution)/shard_map/pallas_call | solution.py:148
  45.4 6.2 %shard_map.44 = (s16[400,512]{1,0:T(8,128)(2,1)S(1)}, s16[400,512]{1,0:T(8,128)(2,1)S(1)}, s16[400,512]{1,0:T(8,128)(2,1)S(1)}, s16[400,512]{1,0:T(8,128)(2,1)S(1)}) custom-call(s32[2]{0:T(128)S(1)} %pad_add_fusion.place_ref, bf16[3,512,1024]{2,1,0:T(8,128)(2,1)S(1)} %copy-done, bf16[3,512,1024]{2,1,0:T(8,128)(2,1)} %collective-permute-done.sib_ref.refs_1_, ...), custom_call_target="tpu_custom_call" | custom-call | flops 1048576 | bytes 65536 | tf_op jit(solution)/shard_map/pallas_call | solution.py:128
  51.6 1.6 %collective-permute-start.11 = (s16[400,512]{1,0:T(8,128)(2,1)S(1)}, s16[400,512]{1,0:T(8,128)(2,1)S(1)}, u32[]{:S(2)}, u32[]{:S(2)}) collective-permute-start(s16[400,512]{1,0:T(8,128)(2,1)S(1)} %get-tuple-element.62), channel_id=1, source_target_pairs={{0,2},{1,3},{2,4},{3,5},{4,6},{5,7},{6,0},{7,1},{8,10},{9,11},{10,... | collective-permute-start | bytes 1228808 | tf_op jit(solution)/shard_map/ppermute | solution.py:337
  53.2 2.9 %collective-permute-start.12 = (s16[400,512]{1,0:T(8,128)(2,1)S(1)}, s16[400,512]{1,0:T(8,128)(2,1)S(1)}, u32[]{:S(2)}, u32[]{:S(2)}) collective-permute-start(s16[400,512]{1,0:T(8,128)(2,1)S(1)} %get-tuple-element.63), channel_id=1, source_target_pairs={{0,4},{1,5},{2,6},{3,7},{4,0},{5,1},{6,2},{7,3},{8,12},{9,13},{10,... | collective-permute-start | bytes 1228808 | tf_op jit(solution)/shard_map/ppermute | solution.py:337
  56.1 1.3 %collective-permute-start.13 = (s16[400,512]{1,0:T(8,128)(2,1)S(1)}, s16[400,512]{1,0:T(8,128)(2,1)S(1)}, u32[]{:S(2)}, u32[]{:S(2)}) collective-permute-start(s16[400,512]{1,0:T(8,128)(2,1)S(1)} %get-tuple-element.64), channel_id=1, source_target_pairs={{0,6},{1,7},{2,0},{3,1},{4,2},{5,3},{6,4},{7,5},{8,14},{9,15},{10,... | collective-permute-start | bytes 1228808 | tf_op jit(solution)/shard_map/ppermute | solution.py:337
  57.5 2.3 %shard_map.45 = (f32[3,4,64,512]{3,2,1,0:T(8,128)}, f32[3,4,64,512]{3,2,1,0:T(8,128)}) custom-call(s32[2]{0:T(128)S(1)} %pad_add_fusion.place_ref, s16[4,208,512]{2,1,0:T(8,128)(2,1)} %all-to-all-done.refs_0_, s32[3,4]{1,0:T(4,128)S(1)} %copy-done.2), custom_call_target="tpu_custom_call" | custom-call | flops 1048576 | bytes 65536 | tf_op jit(solution)/shard_map/pallas_call | solution.py:262
  59.8 3.6 %collective-permute-done.1.refs_3_ = bf16[2,272,1024]{2,1,0:T(8,128)(2,1)} collective-permute-done((bf16[2,272,1024]{2,1,0:T(8,128)(2,1)}, bf16[2,272,1024]{2,1,0:T(8,128)(2,1)}, u32[]{:S(2)}, u32[]{:S(2)}) %collective-permute-start.1) | collective-permute-done | bytes 1114144 | tf_op jit(solution)/shard_map/ppermute | solution.py:351
  63.4 4.5 %shard_map.46 = (s16[208,512]{1,0:T(8,128)(2,1)S(1)}, s16[208,512]{1,0:T(8,128)(2,1)S(1)}, s16[208,512]{1,0:T(8,128)(2,1)S(1)}, s16[208,512]{1,0:T(8,128)(2,1)S(1)}, f32[16,512]{1,0:T(8,128)S(1)}) custom-call(s32[2]{0:T(128)S(1)} %pad_add_fusion.place_ref, bf16[3,512,1024]{2,1,0:T(8,128)(2,1)S(1)} %copy-done, ...), custom_call_target="tpu_custom_call" | custom-call | flops 1048576 | bytes 65536 | tf_op jit(solution)/shard_map/pallas_call | solution.py:128
  67.9 1.6 %collective-permute-start.8 = (s16[208,512]{1,0:T(8,128)(2,1)S(1)}, s16[208,512]{1,0:T(8,128)(2,1)S(1)}, u32[]{:S(2)}, u32[]{:S(2)}) collective-permute-start(s16[208,512]{1,0:T(8,128)(2,1)S(1)} %get-tuple-element.58), channel_id=1, source_target_pairs={{0,2},{1,3},{2,4},{3,5},{4,6},{5,7},{6,0},{7,1},{8,10},{9,11},{10,... | collective-permute-start | bytes 638984 | tf_op jit(solution)/shard_map/ppermute | solution.py:337
  69.5 2.9 %collective-permute-start.9 = (s16[208,512]{1,0:T(8,128)(2,1)S(1)}, s16[208,512]{1,0:T(8,128)(2,1)S(1)}, u32[]{:S(2)}, u32[]{:S(2)}) collective-permute-start(s16[208,512]{1,0:T(8,128)(2,1)S(1)} %get-tuple-element.59), channel_id=1, source_target_pairs={{0,4},{1,5},{2,6},{3,7},{4,0},{5,1},{6,2},{7,3},{8,12},{9,13},{10,... | collective-permute-start | bytes 638984 | tf_op jit(solution)/shard_map/ppermute | solution.py:337
  72.4 1.3 %collective-permute-start.10 = (s16[208,512]{1,0:T(8,128)(2,1)S(1)}, s16[208,512]{1,0:T(8,128)(2,1)S(1)}, u32[]{:S(2)}, u32[]{:S(2)}) collective-permute-start(s16[208,512]{1,0:T(8,128)(2,1)S(1)} %get-tuple-element.60), channel_id=1, source_target_pairs={{0,6},{1,7},{2,0},{3,1},{4,2},{5,3},{6,4},{7,5},{8,14},{9,15},{10,... | collective-permute-start | bytes 638984 | tf_op jit(solution)/shard_map/ppermute | solution.py:337
  73.8 1.5 %collective-permute-done.12.refs_2_ = s16[400,512]{1,0:T(8,128)(2,1)S(1)} collective-permute-done((s16[400,512]{1,0:T(8,128)(2,1)S(1)}, s16[400,512]{1,0:T(8,128)(2,1)S(1)}, u32[]{:S(2)}, u32[]{:S(2)}) %collective-permute-start.12) | collective-permute-done | bytes 409632 | tf_op jit(solution)/shard_map/ppermute | solution.py:337
  75.2 2.0 %shard_map.47 = (f32[3,4,64,512]{3,2,1,0:T(8,128)}, f32[3,4,64,512]{3,2,1,0:T(8,128)}, s16[208,512]{1,0:T(8,128)(2,1)S(1)}, s16[272,512]{1,0:T(8,128)(2,1)S(1)}) custom-call(s32[2]{0:T(128)S(1)} %pad_add_fusion.place_ref, s16[400,512]{1,0:T(8,128)(2,1)S(1)} %get-tuple-element.51.refs_0_, ...), custom_call_target="tpu_custom_call", output_to_operand_aliasing={{0}: (7, {}), {1}: (8, {})} | custom-call | flops 1048576 | bytes 65536 | tf_op jit(solution)/shard_map/pallas_call | solution.py:262
  77.2 1.9 %collective-permute-start.18 = (s16[272,512]{1,0:T(8,128)(2,1)S(1)}, s16[272,512]{1,0:T(8,128)(2,1)S(1)}, u32[]{:S(2)}, u32[]{:S(2)}) collective-permute-start(s16[272,512]{1,0:T(8,128)(2,1)S(1)} %get-tuple-element.73), channel_id=1, source_target_pairs={{8,0},{16,8},{24,16},{32,24},{40,32},{48,40},{56,48},{64,56},{72,6... | collective-permute-start | bytes 835592 | tf_op jit(solution)/shard_map/ppermute | solution.py:351
  79.1 3.9 %collective-permute-start.17 = (s16[208,512]{1,0:T(8,128)(2,1)S(1)}, s16[208,512]{1,0:T(8,128)(2,1)S(1)}, u32[]{:S(2)}, u32[]{:S(2)}) collective-permute-start(s16[208,512]{1,0:T(8,128)(2,1)S(1)} %get-tuple-element.72), channel_id=1, source_target_pairs={{0,8},{8,16},{16,24},{24,32},{32,40},{40,48},{48,56},{56,64},{64,7... | collective-permute-start | bytes 638984 | tf_op jit(solution)/shard_map/ppermute | solution.py:351
  83.5 1.5 %shard_map.48 = (f32[3,4,64,512]{3,2,1,0:T(8,128)}, f32[3,4,64,512]{3,2,1,0:T(8,128)}, s16[144,512]{1,0:T(8,128)(2,1)S(1)}, s16[80,256]{1,0:T(8,128)(2,1)S(1)}, ...) custom-call(s32[2]{0:T(128)S(1)} %pad_add_fusion.place_ref, ...), custom_call_target="tpu_custom_call", output_to_operand_aliasing={{0}: (7, {}), {1}: (8, {})} | custom-call | flops 1048576 | bytes 65536 | tf_op jit(solution)/shard_map/pallas_call | solution.py:262
  85.0 1.9 %collective-permute-start.14 = (s16[144,512]{1,0:T(8,128)(2,1)S(1)}, s16[144,512]{1,0:T(8,128)(2,1)S(1)}, u32[]{:S(2)}, u32[]{:S(2)}) collective-permute-start(s16[144,512]{1,0:T(8,128)(2,1)S(1)} %get-tuple-element.69), channel_id=1, source_target_pairs={{0,8},{8,16},{16,24},{24,32},{32,40},{40,48},{48,56},{56,64},{64,7... | collective-permute-start | bytes 442376 | tf_op jit(solution)/shard_map/ppermute | solution.py:351
  87.1 6.0 %collective-permute-start.15 = (s16[80,256]{1,0:T(8,128)(2,1)S(1)}, s16[80,256]{1,0:T(8,128)(2,1)S(1)}, u32[]{:S(2)}, u32[]{:S(2)}) collective-permute-start(s16[80,256]{1,0:T(8,128)(2,1)S(1)} %get-tuple-element.70), channel_id=1, source_target_pairs={{8,0},{16,8},{24,16},{32,24},{40,32},{48,40},{56,48},{64,56},{72,6... | collective-permute-start | bytes 122888 | tf_op jit(solution)/shard_map/ppermute | solution.py:351
  93.1 2.0 %collective-permute-start.16 = (s16[80,256]{1,0:T(8,128)(2,1)S(1)}, s16[80,256]{1,0:T(8,128)(2,1)S(1)}, u32[]{:S(2)}, u32[]{:S(2)}) collective-permute-start(s16[80,256]{1,0:T(8,128)(2,1)S(1)} %get-tuple-element.71), channel_id=1, source_target_pairs={{8,1},{9,0},{10,3},{11,2},{12,5},{13,4},{14,7},{15,6},{16,9},{17,8... | collective-permute-start | bytes 122888 | tf_op jit(solution)/shard_map/ppermute | solution.py:367
  95.2 1.7 %shard_map.49 = (f32[3,4,64,512]{3,2,1,0:T(8,128)}, f32[3,4,64,512]{3,2,1,0:T(8,128)}) custom-call(s32[2]{0:T(128)S(1)} %pad_add_fusion.place_ref, s16[208,512]{1,0:T(8,128)(2,1)S(1)} %collective-permute-done.17.refs_0_, s16[272,512]{1,0:T(8,128)(2,1)S(1)} %collective-permute-done.18.refs_1_, ...), custom_call_target="tpu_custom_call", output_to_operand_aliasing={{0}: (5, {}), {1}: (6, {})} | custom-call | flops 1048576 | bytes 65536 | tf_op jit(solution)/shard_map/pallas_call | solution.py:314
  96.9 1.7 %collective-permute-done.16.refs_2_ = s16[80,256]{1,0:T(8,128)(2,1)S(1)} collective-permute-done((s16[80,256]{1,0:T(8,128)(2,1)S(1)}, s16[80,256]{1,0:T(8,128)(2,1)S(1)}, u32[]{:S(2)}, u32[]{:S(2)}) %collective-permute-start.16) | collective-permute-done | bytes 40992 | tf_op jit(solution)/shard_map/ppermute | solution.py:367
  98.6 1.4 %shard_map.50 = (f32[3,4,64,512]{3,2,1,0:T(8,128)}, f32[3,4,64,512]{3,2,1,0:T(8,128)}) custom-call(s32[2]{0:T(128)S(1)} %pad_add_fusion.place_ref, s16[144,512]{1,0:T(8,128)(2,1)S(1)} %collective-permute-done.14.refs_0_, s16[80,256]{1,0:T(8,128)(2,1)S(1)} %collective-permute-done.15.refs_1_, ...), custom_call_target="tpu_custom_call", output_to_operand_aliasing={{0}: (4, {}), {1}: (5, {})} | custom-call | flops 1048576 | bytes 65536 | tf_op jit(solution)/shard_map/pallas_call | solution.py:314
  (29 shorter events, 6.1 us)
Async XLA Ops:
  0.6 11.3 %collective-permute-start = (bf16[3,512,1024]{2,1,0:T(8,128)(2,1)}, bf16[3,512,1024]{2,1,0:T(8,128)(2,1)}, u32[]{:S(2)}, u32[]{:S(2)}) collective-permute-start(bf16[3,512,1024]{2,1,0:T(8,128)(2,1)} %refs_0_.5), channel_id=1, source_target_pairs={{0,1},{1,0},{2,3},{3,2},{4,5},{5,4},{6,7},{7,6},{8,9},{9,8},{10,11... | collective-permute-start | bytes 9437192 | tf_op jit(solution)/shard_map/ppermute | solution.py:330
  0.7 11.2 %copy-start = (bf16[3,512,1024]{2,1,0:T(8,128)(2,1)S(1)}, bf16[3,512,1024]{2,1,0:T(8,128)(2,1)}, u32[]{:S(2)}) copy-start(bf16[3,512,1024]{2,1,0:T(8,128)(2,1)} %refs_0_.5) | copy-start | bytes 9437188
  5.4 28.3 %collective-permute-start.4 = (bf16[1,512,1024]{2,1,0:T(8,128)(2,1)}, bf16[1,512,1024]{2,1,0:T(8,128)(2,1)}, u32[]{:S(2)}, u32[]{:S(2)}) collective-permute-start(bf16[1,512,1024]{2,1,0:T(8,128)(2,1)} %slice.7), channel_id=1, source_target_pairs={{8,0},{16,8},{24,16},{32,24},{40,32},{48,40},{56,48},{64,56},{72,6... | collective-permute-start | bytes 3145736 | tf_op jit(solution)/shard_map/ppermute | solution.py:351
  9.9 30.3 %collective-permute-start.3 = (bf16[1,512,1024]{2,1,0:T(8,128)(2,1)}, bf16[1,512,1024]{2,1,0:T(8,128)(2,1)}, u32[]{:S(2)}, u32[]{:S(2)}) collective-permute-start(bf16[1,512,1024]{2,1,0:T(8,128)(2,1)} %slice.6), channel_id=1, source_target_pairs={{0,8},{8,16},{16,24},{24,32},{32,40},{40,48},{48,56},{56,64},{64,7... | collective-permute-start | bytes 3145736 | tf_op jit(solution)/shard_map/ppermute | solution.py:351
  15.8 0.9 copy-start.1
  16.7 4.6 %copy-start.2 = (s32[3,4]{1,0:T(4,128)S(1)}, s32[3,4]{1,0:T(4,128)}, u32[]{:S(2)}) copy-start(s32[3,4]{1,0:T(4,128)} %refs_4_.3) | copy-start | bytes 148
  16.7 23.5 %all-to-all-start = ((s16[4,208,512]{2,1,0:T(8,128)(2,1)}), s16[4,208,512]{2,1,0:T(8,128)(2,1)}, u32[]{:S(2)}, u32[]{:S(2)}) async-start(s16[4,208,512]{2,1,0:T(8,128)(2,1)} %copy-done.1), calls=%async_computation | async-start | bytes 1703936 | tf_op jit(solution)/shard_map/all_to_all | solution.py:342
  24.8 38.6 %collective-permute-start.1 = (bf16[2,272,1024]{2,1,0:T(8,128)(2,1)}, bf16[2,272,1024]{2,1,0:T(8,128)(2,1)}, u32[]{:S(2)}, u32[]{:S(2)}) collective-permute-start(bf16[2,272,1024]{2,1,0:T(8,128)(2,1)} %get-tuple-element.42), channel_id=1, source_target_pairs={{0,8},{8,16},{16,24},{24,32},{32,40},{40,48},{48,56},{56,64},{64,7... | collective-permute-start | bytes 3342344 | tf_op jit(solution)/shard_map/ppermute | solution.py:351
  27.6 32.2 %collective-permute-start.2 = (bf16[2,256,1024]{2,1,0:T(8,128)(2,1)}, bf16[2,256,1024]{2,1,0:T(8,128)(2,1)}, u32[]{:S(2)}, u32[]{:S(2)}) collective-permute-start(bf16[2,256,1024]{2,1,0:T(8,128)(2,1)} %get-tuple-element.43), channel_id=1, source_target_pairs={{8,0},{16,8},{24,16},{32,24},{40,32},{48,40},{56,48},{64,56},{72,6... | collective-permute-start | bytes 3145736 | tf_op jit(solution)/shard_map/ppermute | solution.py:351
  41.9 2.0 %collective-permute-start.5 = (bf16[1,256,1024]{2,1,0:T(8,128)(2,1)S(1)}, bf16[1,256,1024]{2,1,0:T(8,128)(2,1)S(1)}, u32[]{:S(2)}, u32[]{:S(2)}) collective-permute-start(bf16[1,256,1024]{2,1,0:T(8,128)(2,1)S(1)} %get-tuple-element.48), channel_id=1, source_target_pairs={{0,1},{1,0},{2,3},{3,2},{4,5},{5,4},{6,7},{7,6},{8,9},{9,8},{10,11... | collective-permute-start | bytes 1572872 | tf_op jit(solution)/shard_map/ppermute | solution.py:330
  42.0 2.6 %collective-permute-start.6 = (bf16[1,256,1024]{2,1,0:T(8,128)(2,1)S(1)}, bf16[1,256,1024]{2,1,0:T(8,128)(2,1)S(1)}, u32[]{:S(2)}, u32[]{:S(2)}) collective-permute-start(bf16[1,256,1024]{2,1,0:T(8,128)(2,1)S(1)} %get-tuple-element.49), channel_id=1, source_target_pairs={{0,1},{1,0},{2,3},{3,2},{4,5},{5,4},{6,7},{7,6},{8,9},{9,8},{10,11... | collective-permute-start | bytes 1572872 | tf_op jit(solution)/shard_map/ppermute | solution.py:330
  42.5 2.9 %collective-permute-start.7 = (bf16[1,256,1024]{2,1,0:T(8,128)(2,1)S(1)}, bf16[1,256,1024]{2,1,0:T(8,128)(2,1)S(1)}, u32[]{:S(2)}, u32[]{:S(2)}) collective-permute-start(bf16[1,256,1024]{2,1,0:T(8,128)(2,1)S(1)} %get-tuple-element.50), channel_id=1, source_target_pairs={{0,1},{1,0},{2,3},{3,2},{4,5},{5,4},{6,7},{7,6},{8,9},{9,8},{10,11... | collective-permute-start | bytes 1572872 | tf_op jit(solution)/shard_map/ppermute | solution.py:330
  51.6 20.9 %collective-permute-start.11 = (s16[400,512]{1,0:T(8,128)(2,1)S(1)}, s16[400,512]{1,0:T(8,128)(2,1)S(1)}, u32[]{:S(2)}, u32[]{:S(2)}) collective-permute-start(s16[400,512]{1,0:T(8,128)(2,1)S(1)} %get-tuple-element.62), channel_id=1, source_target_pairs={{0,2},{1,3},{2,4},{3,5},{4,6},{5,7},{6,0},{7,1},{8,10},{9,11},{10,... | collective-permute-start | bytes 1228808 | tf_op jit(solution)/shard_map/ppermute | solution.py:337
  53.2 22.0 %collective-permute-start.12 = (s16[400,512]{1,0:T(8,128)(2,1)S(1)}, s16[400,512]{1,0:T(8,128)(2,1)S(1)}, u32[]{:S(2)}, u32[]{:S(2)}) collective-permute-start(s16[400,512]{1,0:T(8,128)(2,1)S(1)} %get-tuple-element.63), channel_id=1, source_target_pairs={{0,4},{1,5},{2,6},{3,7},{4,0},{5,1},{6,2},{7,3},{8,12},{9,13},{10,... | collective-permute-start | bytes 1228808 | tf_op jit(solution)/shard_map/ppermute | solution.py:337
  56.1 19.1 %collective-permute-start.13 = (s16[400,512]{1,0:T(8,128)(2,1)S(1)}, s16[400,512]{1,0:T(8,128)(2,1)S(1)}, u32[]{:S(2)}, u32[]{:S(2)}) collective-permute-start(s16[400,512]{1,0:T(8,128)(2,1)S(1)} %get-tuple-element.64), channel_id=1, source_target_pairs={{0,6},{1,7},{2,0},{3,1},{4,2},{5,3},{6,4},{7,5},{8,14},{9,15},{10,... | collective-permute-start | bytes 1228808 | tf_op jit(solution)/shard_map/ppermute | solution.py:337
  67.9 15.2 %collective-permute-start.8 = (s16[208,512]{1,0:T(8,128)(2,1)S(1)}, s16[208,512]{1,0:T(8,128)(2,1)S(1)}, u32[]{:S(2)}, u32[]{:S(2)}) collective-permute-start(s16[208,512]{1,0:T(8,128)(2,1)S(1)} %get-tuple-element.58), channel_id=1, source_target_pairs={{0,2},{1,3},{2,4},{3,5},{4,6},{5,7},{6,0},{7,1},{8,10},{9,11},{10,... | collective-permute-start | bytes 638984 | tf_op jit(solution)/shard_map/ppermute | solution.py:337
  69.5 14.0 %collective-permute-start.9 = (s16[208,512]{1,0:T(8,128)(2,1)S(1)}, s16[208,512]{1,0:T(8,128)(2,1)S(1)}, u32[]{:S(2)}, u32[]{:S(2)}) collective-permute-start(s16[208,512]{1,0:T(8,128)(2,1)S(1)} %get-tuple-element.59), channel_id=1, source_target_pairs={{0,4},{1,5},{2,6},{3,7},{4,0},{5,1},{6,2},{7,3},{8,12},{9,13},{10,... | collective-permute-start | bytes 638984 | tf_op jit(solution)/shard_map/ppermute | solution.py:337
  72.4 11.1 %collective-permute-start.10 = (s16[208,512]{1,0:T(8,128)(2,1)S(1)}, s16[208,512]{1,0:T(8,128)(2,1)S(1)}, u32[]{:S(2)}, u32[]{:S(2)}) collective-permute-start(s16[208,512]{1,0:T(8,128)(2,1)S(1)} %get-tuple-element.60), channel_id=1, source_target_pairs={{0,6},{1,7},{2,0},{3,1},{4,2},{5,3},{6,4},{7,5},{8,14},{9,15},{10,... | collective-permute-start | bytes 638984 | tf_op jit(solution)/shard_map/ppermute | solution.py:337
  77.2 18.0 %collective-permute-start.18 = (s16[272,512]{1,0:T(8,128)(2,1)S(1)}, s16[272,512]{1,0:T(8,128)(2,1)S(1)}, u32[]{:S(2)}, u32[]{:S(2)}) collective-permute-start(s16[272,512]{1,0:T(8,128)(2,1)S(1)} %get-tuple-element.73), channel_id=1, source_target_pairs={{8,0},{16,8},{24,16},{32,24},{40,32},{48,40},{56,48},{64,56},{72,6... | collective-permute-start | bytes 835592 | tf_op jit(solution)/shard_map/ppermute | solution.py:351
  79.1 16.0 %collective-permute-start.17 = (s16[208,512]{1,0:T(8,128)(2,1)S(1)}, s16[208,512]{1,0:T(8,128)(2,1)S(1)}, u32[]{:S(2)}, u32[]{:S(2)}) collective-permute-start(s16[208,512]{1,0:T(8,128)(2,1)S(1)} %get-tuple-element.72), channel_id=1, source_target_pairs={{0,8},{8,16},{16,24},{24,32},{32,40},{40,48},{48,56},{56,64},{64,7... | collective-permute-start | bytes 638984 | tf_op jit(solution)/shard_map/ppermute | solution.py:351
  85.0 13.5 %collective-permute-start.14 = (s16[144,512]{1,0:T(8,128)(2,1)S(1)}, s16[144,512]{1,0:T(8,128)(2,1)S(1)}, u32[]{:S(2)}, u32[]{:S(2)}) collective-permute-start(s16[144,512]{1,0:T(8,128)(2,1)S(1)} %get-tuple-element.69), channel_id=1, source_target_pairs={{0,8},{8,16},{16,24},{24,32},{32,40},{40,48},{48,56},{56,64},{64,7... | collective-permute-start | bytes 442376 | tf_op jit(solution)/shard_map/ppermute | solution.py:351
  87.0 6.1 %collective-permute-start.19 = (f32[64,256]{1,0:T(8,128)S(1)}, f32[64,256]{1,0:T(8,128)S(1)}, u32[]{:S(2)}, u32[]{:S(2)}) collective-permute-start(f32[64,256]{1,0:T(8,128)S(1)} %get-tuple-element.75), channel_id=1, source_target_pairs={{0,1},{1,0},{2,3},{3,2},{4,5},{5,4},{6,7},{7,6},{8,9},{9,8},{10,11... | collective-permute-start | bytes 196616 | tf_op jit(solution)/shard_map/ppermute | solution.py:330
  87.1 9.8 %collective-permute-start.15 = (s16[80,256]{1,0:T(8,128)(2,1)S(1)}, s16[80,256]{1,0:T(8,128)(2,1)S(1)}, u32[]{:S(2)}, u32[]{:S(2)}) collective-permute-start(s16[80,256]{1,0:T(8,128)(2,1)S(1)} %get-tuple-element.70), channel_id=1, source_target_pairs={{8,0},{16,8},{24,16},{32,24},{40,32},{48,40},{56,48},{64,56},{72,6... | collective-permute-start | bytes 122888 | tf_op jit(solution)/shard_map/ppermute | solution.py:351
  93.1 5.5 %collective-permute-start.16 = (s16[80,256]{1,0:T(8,128)(2,1)S(1)}, s16[80,256]{1,0:T(8,128)(2,1)S(1)}, u32[]{:S(2)}, u32[]{:S(2)}) collective-permute-start(s16[80,256]{1,0:T(8,128)(2,1)S(1)} %get-tuple-element.71), channel_id=1, source_target_pairs={{8,1},{9,0},{10,3},{11,2},{12,5},{13,4},{14,7},{15,6},{16,9},{17,8... | collective-permute-start | bytes 122888 | tf_op jit(solution)/shard_map/ppermute | solution.py:367

commit v3 on v2

v3 whole, which is shorter than its diff:
```python
import functools

import jax
import jax.numpy as jnp
from jax import lax
from jax.experimental import pallas as pl
from jax.experimental.pallas import tpu as pltpu
from jax.sharding import PartitionSpec as P

BF = 512
COLS = 1024
HALF = 256
SLICE = 64
CHIPS = 4
STEPS = 256.0
TOP = 32700.0
LN2 = 0.6931471805599453

VMEM = pl.BlockSpec(memory_space=pltpu.VMEM)
SMEM = pl.BlockSpec(memory_space=pltpu.SMEM)
HBM = pl.BlockSpec(memory_space=pltpu.HBM)
PARAMS = pltpu.CompilerParams(vmem_limit_bytes=18 << 20)
FAR = pltpu.CompilerParams(vmem_limit_bytes=62 << 20)
OUTS = [jax.ShapeDtypeStruct((3, 4, SLICE, BF), jnp.float32)] * 2


def coded_rows(count):
    return count * SLICE + 16


def code(values):
    tops = jnp.concatenate([jnp.max(jnp.abs(v), 0, keepdims=True) for v in values], 0)
    level = jnp.ceil(jnp.log(jnp.maximum(tops, 1e-30) / TOP) * (STEPS / LN2))
    gain = jnp.exp(level * (-LN2 / STEPS))
    coded = [
        jnp.round(v * gain[i : i + 1]).astype(jnp.int32).astype(jnp.int16)
        for i, v in enumerate(values)
    ]
    return coded, level.astype(jnp.int32)


def level_rows(levels):
    rows = list(levels) + [jnp.zeros((16 - len(levels), BF), jnp.int32)]
    return jnp.concatenate(rows, 0).astype(jnp.int16)


def scales_of(rows):
    return jnp.exp(rows.astype(jnp.float32) * (LN2 / STEPS))


def pair_kernel(pairs, blocks, halved, names, together, late, with_second, place_ref, *refs):
    ins = dict(zip(names, refs))
    outs = refs[len(names) :]
    if with_second:
        outs, mask_ref, second = outs[1:-2], outs[0], outs[-2:]
        put_second(place_ref, mask_ref, (ins["own"], ins["sib"]), *second)
    if late:
        *outs, lines_ref = outs
        first_ref, second_ref = ins["first"], ins["second"]

        def work(low_ref, high_ref):
            ins.update({"low2": low_ref, "high2": high_ref})
            lines_ref[...] = low_ref[0, HALF : HALF + 16, :BF].astype(jnp.float32)
            pair_work(pairs, blocks, halved, ins, outs, together, place_ref)

        @pl.when(place_ref[2] == 1)
        def _():
            work(second_ref, first_ref)

        @pl.when(place_ref[2] == 0)
        def _():
            work(first_ref, second_ref)

        return
    pair_work(pairs, blocks, halved, ins, outs, together, place_ref)


def pair_work(pairs, blocks, halved, ins, outs, together, place_ref):
    if together:
        outs = [outs[0].at[d] for d in range(CHIPS)]
    core, chip = place_ref[0], place_ref[1]
    order = [d if together else (chip + d) % CHIPS for d in range(CHIPS)]

    def read(piece, start, rows):
        name, index = piece
        return ins[name][index, pl.ds(start, rows), :]

    def slices(pieces):
        rows = []
        for o in order:
            if len(pieces) == 2:
                start = (2 * (o % 2) + core) * SLICE
                low, high = (read(piece, start, SLICE) for piece in pieces)
                rows.append(jnp.where(o < 2, low, high))
            elif ins[pieces[0][0]].shape[1] < BF:
                rows.append(read(pieces[0], o * SLICE, SLICE))
            else:
                rows.append(read(pieces[0], (2 * o + core) * SLICE, SLICE))
        return jnp.concatenate(rows, 0)

    def both_slices(pieces):
        rows = [read(pieces[0], o * 2 * SLICE, 2 * SLICE) for o in order]
        return jnp.concatenate(rows, 0)

    def term(a, b, part):
        shared = a in halved
        right = (both_slices if shared else slices)(blocks[b][part])
        pieces = blocks[a][part]
        rows = (HALF if shared else BF) // len(pieces)
        values = [
            lax.dot_general(
                right,
                read(piece, 0, rows),
                (((1,), (1,)), ((), ())),
                preferred_element_type=jnp.float32,
            )
            for piece in pieces
        ]
        return jnp.concatenate(values, 1)

    levels = []
    for p, (a, b) in enumerate(pairs):
        shared = a in halved
        acc = term(a, b, 0) + term(a, b, 1)
        if shared:
            parts = [
                jnp.concatenate(
                    [acc[k * SLICE : (k + 1) * SLICE] for k in (2 * d, 2 * d + 1)], 1
                )
                for d in range(CHIPS)
            ]
        else:
            parts = [acc[d * SLICE : (d + 1) * SLICE] for d in range(CHIPS)]
        coded, level = code(parts)
        for d in range(CHIPS):
            outs[d][p * SLICE : (p + 1) * SLICE, :] = coded[d]
        levels.append(level)
    end = len(pairs) * SLICE
    for d in range(CHIPS):
        outs[d][end : end + 16, :] = level_rows([v[d : d + 1] for v in levels])


def put_second(place_ref, mask_ref, sources, first_ref, second_ref):
    core = place_ref[0]
    lines = [
        jnp.full((1, COLS), mask_ref[k // 4, k % 4].astype(jnp.float32), jnp.float32)
        for k in range(12)
    ]
    lines.append(jnp.zeros((4, COLS), jnp.float32))
    lines = jnp.concatenate(lines, 0).astype(jnp.bfloat16)

    def put(up_ref, down_ref):
        for i, source in enumerate(sources):
            up_ref[i, :HALF, :] = source[1, pl.ds(core * HALF, HALF), :]
            up_ref[i, HALF:, :] = lines
            for y in range(CHIPS):
                down_ref[i, y * SLICE : (y + 1) * SLICE, :] = source[
                    1, pl.ds((2 * y + core) * SLICE, SLICE), :
                ]
            down_ref[i, HALF:, :] = lines

    @pl.when(place_ref[2] == 1)
    def _():
        put(first_ref, second_ref)

    @pl.when(place_ref[2] == 0)
    def _():
        put(second_ref, first_ref)


def pair_products(place, pairs, blocks, operands, halved=(), together=False, late=False, mask=None):
    names = list(operands)
    n = len(pairs)
    rows = coded_rows(n)
    shapes = [jax.ShapeDtypeStruct((rows, BF), jnp.int16)] * CHIPS
    if together:
        shapes = [jax.ShapeDtypeStruct((CHIPS, rows, BF), jnp.int16)]
    if late:
        shapes.append(jax.ShapeDtypeStruct((16, BF), jnp.float32))
    second = mask is not None
    if second:
        shapes += [jax.ShapeDtypeStruct((2, HALF + 16, COLS), jnp.bfloat16)] * 2
    return pl.pallas_call(
        functools.partial(pair_kernel, pairs, blocks, halved, names, together, late, second),
        out_shape=shapes,
        in_specs=[SMEM] + [VMEM] * len(names) + [SMEM] * second,
        out_specs=[VMEM] * len(shapes),
        compiler_params=FAR if together else PARAMS,
        cost_estimate=pl.CostEstimate(flops=1 << 20, bytes_accessed=1 << 16, transcendentals=0),
    )(place, *operands.values(), *([mask] if second else []))


def first_kernel(own_ref, first_ref, second_ref, held, sems):
    n = 4
    rows = BF // n
    odd = lax.axis_index("space") % 2
    copies = []
    for k in range(2 * n):
        at = pl.ds((k % n) * rows, rows)
        block, target = ((2 * odd, first_ref), (2 - 2 * odd, second_ref))[k // n]
        copies.append(
            (
                pltpu.make_async_copy(own_ref.at[block, at], held.at[k], sems.at[0, k]),
                pltpu.make_async_copy(held.at[k], target.at[0, at], sems.at[1, k]),
            )
        )
    for load, _ in copies:
        load.start()
    for load, store in copies:
        load.wait()
        store.start()
    for _, store in copies:
        store.wait()


def first_factors(own):
    return pl.pallas_call(
        first_kernel,
        out_shape=[jax.ShapeDtypeStruct((1, BF, COLS), jnp.bfloat16)] * 2,
        in_specs=[HBM],
        out_specs=[HBM] * 2,
        scratch_shapes=[
            pltpu.VMEM((8, BF // 4, COLS), jnp.bfloat16),
            pltpu.SemaphoreType.DMA((2, 8)),
        ],
        compiler_params=FAR,
        cost_estimate=pl.CostEstimate(flops=1 << 10, bytes_accessed=1 << 10, transcendentals=0),
    )(own)


def bring_kernel(ref, out_ref, sem):
    copy = pltpu.make_async_copy(ref, out_ref, sem)
    copy.start()
    copy.wait()


def bring(value):
    return pl.pallas_call(
        bring_kernel,
        out_shape=jax.ShapeDtypeStruct(value.shape, value.dtype),
        in_specs=[HBM],
        out_specs=VMEM,
        scratch_shapes=[pltpu.SemaphoreType.DMA],
        compiler_params=PARAMS,
        cost_estimate=pl.CostEstimate(flops=1 << 10, bytes_accessed=1 << 10, transcendentals=0),
    )(value)


def arrived_kernel(place_ref, first_ref, second_ref, low_a_ref, low_b_ref, mine_ref, other_ref):
    def put(low_ref, high_ref):
        low_a_ref[0] = low_ref[0, :HALF, :]
        low_b_ref[0] = low_ref[0, HALF:, :]
        for core, target in ((place_ref[0], mine_ref), (1 - place_ref[0], other_ref)):
            for y in range(CHIPS):
                start = (2 * y + core) * SLICE
                target[0, y * SLICE : (y + 1) * SLICE, :] = high_ref[0, pl.ds(start, SLICE), :]

    @pl.when(place_ref[2] == 1)
    def _():
        put(second_ref, first_ref)

    @pl.when(place_ref[2] == 0)
    def _():
        put(first_ref, second_ref)


def arrived(place, first, second):
    return pl.pallas_call(
        arrived_kernel,
        out_shape=[jax.ShapeDtypeStruct((1, HALF, COLS), jnp.bfloat16)] * 4,
        in_specs=[SMEM, VMEM, VMEM],
        out_specs=[VMEM] * 4,
        compiler_params=PARAMS,
        cost_estimate=pl.CostEstimate(flops=1 << 10, bytes_accessed=1 << 10, transcendentals=0),
    )(place, first, second)


def put_messages(place_ref, refs, held):
    def put(refs):
        for ref, blocks in zip(refs, held):
            for k, (coded, _) in enumerate(blocks):
                ref[k * SLICE : (k + 1) * SLICE, :] = coded
            end = ref.shape[0] - 16
            ref[end : end + 16, :] = level_rows([level for _, level in blocks])

    if len(refs) < 2:
        put(refs)
        return

    @pl.when(place_ref[2] == 1)
    def _():
        put(refs)

    @pl.when(place_ref[2] == 0)
    def _():
        put(refs[::-1])


def add_kernel(places, first, sizes, halves, n_gots, lined, place_ref, *refs):
    gots, refs = refs[:n_gots], refs[n_gots:]
    if n_gots == 1:
        gots = [gots[0].at[d] for d in range(CHIPS)]
    mask_ref, refs = refs[0], refs[1:]
    if lined:
        lines_ref, refs = refs[0], refs[1:]
    if not first:
        refs = refs[2:]
    (f_ref, b_ref), refs = refs[:2], refs[2:]
    messages, refs = refs[: len(sizes)], refs[len(sizes) :]
    if halves:
        (kept_ref, swap_ref), refs = refs[:2], refs[2:]
    sums, sems = refs
    held = [[] for _ in sizes]
    writes = []
    n = len(places)
    scales = [scales_of(gots[d][n * SLICE : n * SLICE + 16, :]) for d in range(CHIPS)]
    for p, ((theirs, block, slot), goals) in enumerate(places):
        total = None
        for d in range(CHIPS):
            part = gots[d][p * SLICE : (p + 1) * SLICE, :].astype(jnp.float32)
            part = part * scales[d][p : p + 1]
            total = part if total is None else total + part
        if theirs:
            line = lines_ref[block * 4 + slot : block * 4 + slot + 1, :]
            total = total * line
        else:
            total = total * mask_ref[block, slot].astype(jnp.float32)
        coded = None
        for kind, *goal in goals:
            if kind == "m":
                which, index = goal
                if coded is None:
                    (coded,), level = code([total])
                assert index == len(held[which])
                held[which].append((coded, level))
            elif kind == "halves":
                first_core = place_ref[0] == 0
                low, high = total[:, :HALF], total[:, HALF:]
                kept_ref[...] = jnp.where(first_core, low, high)
                swap_ref[...] = jnp.where(first_core, high, low)
            else:
                sums[p] = total
                writes.append((p, (f_ref if kind == "f" else b_ref).at[goal[0], goal[1]]))
    put_messages(place_ref, messages, held)
    writes = [
        pltpu.make_async_copy(sums.at[p], target, sems.at[k])
        for k, (p, target) in enumerate(writes)
    ]
    for copy in writes:
        copy.start()
    for copy in writes:
        copy.wait()


def add_parts(place, gots, masks, outs, places, sizes=(), halves=False):
    n = len(places)
    first = outs is None
    earlier = [] if first else list(outs)
    at = 1 + len(gots) + len(masks)
    shapes = OUTS + [jax.ShapeDtypeStruct((coded_rows(max(sizes, default=0)), BF), jnp.int16) for _ in sizes]
    if halves:
        shapes += [jax.ShapeDtypeStruct((SLICE, HALF), jnp.float32)] * 2
    return pl.pallas_call(
        functools.partial(add_kernel, places, first, sizes, halves, len(gots), len(masks) > 1),
        out_shape=shapes,
        in_specs=[SMEM] + [VMEM] * len(gots) + [SMEM, VMEM][: len(masks)] + [HBM] * len(earlier),
        out_specs=[HBM] * 2 + [VMEM] * (len(shapes) - 2),
        scratch_shapes=[
            pltpu.VMEM((n, SLICE, BF), jnp.float32),
            pltpu.SemaphoreType.DMA((2 * n,)),
        ],
        input_output_aliases={} if first else {at: 0, at + 1: 1},
        compiler_params=PARAMS,
        cost_estimate=pl.CostEstimate(flops=1 << 20, bytes_accessed=1 << 16, transcendentals=0),
    )(place, *gots, *masks, *earlier)


def place_kernel(below_places, above_places, block_places, place_ref, first_ref, second_ref, *refs):
    blocks, refs = refs[: len(block_places)], refs[len(block_places) + 2 :]
    f_ref, b_ref, sums, sems = refs
    goals = below_places + above_places + block_places

    def take(*messages):
        k = 0
        for ref, count in zip(messages, (len(below_places), len(above_places))):
            end = ref.shape[0] - 16
            scales = scales_of(ref[end : end + 16, :])
            for p in range(count):
                part = ref[p * SLICE : (p + 1) * SLICE, :].astype(jnp.float32)
                sums[k] = part * scales[p : p + 1]
                k += 1

    @pl.when(place_ref[2] == 1)
    def _():
        take(second_ref, first_ref)

    @pl.when(place_ref[2] == 0)
    def _():
        take(first_ref, second_ref)

    for k, block in enumerate(blocks):
        sums[len(goals) - len(blocks) + k] = block[...]
    writes = []
    for k, (kind, block, slot) in enumerate(goals):
        target = (f_ref if kind == "f" else b_ref).at[block, slot]
        writes.append(pltpu.make_async_copy(sums.at[k], target, sems.at[k]))
    for copy in writes:
        copy.start()
    for copy in writes:
        copy.wait()


def place_results(place, first, second, outs, below_places, above_places, blocks=(), block_places=()):
    total = len(below_places) + len(above_places) + len(blocks)
    n = 3 + len(blocks)
    return pl.pallas_call(
        functools.partial(place_kernel, below_places, above_places, list(block_places)),
        out_shape=OUTS,
        in_specs=[SMEM] + [VMEM] * (n - 1) + [HBM] * 2,
        out_specs=[HBM] * 2,
        scratch_shapes=[
            pltpu.VMEM((total, SLICE, BF), jnp.float32),
            pltpu.SemaphoreType.DMA((total,)),
        ],
        input_output_aliases={n: 0, n + 1: 1},
        compiler_params=PARAMS,
        cost_estimate=pl.CostEstimate(flops=1 << 20, bytes_accessed=1 << 16, transcendentals=0),
    )(place, first, second, *blocks, *outs)


def join_kernel(place_ref, mine_ref, other_ref, up_ref, block_ref, *refs):
    first_core = place_ref[0] == 0
    mine, other = mine_ref[...], other_ref[...]
    low, high = jnp.where(first_core, mine, other), jnp.where(first_core, other, mine)
    total = jnp.concatenate([low, high], 1)
    block_ref[...] = total
    (coded,), level = code([total])

    def put(up_to, down_to):
        up_to[...] = up_ref[...]
        end = down_to.shape[0] - 16
        down_to[:SLICE, :] = coded
        down_to[end:, :] = level_rows([level])

    @pl.when(place_ref[2] == 1)
    def _():
        put(*refs)

    @pl.when(place_ref[2] == 0)
    def _():
        put(*refs[::-1])


def join_halves(place, mine, other, up):
    return pl.pallas_call(
        join_kernel,
        out_shape=[
            jax.ShapeDtypeStruct((SLICE, BF), jnp.float32),
            jax.ShapeDtypeStruct(up.shape, jnp.int16),
            jax.ShapeDtypeStruct(up.shape, jnp.int16),
        ],
        in_specs=[SMEM, VMEM, VMEM, VMEM],
        out_specs=[VMEM] * 3,
        compiler_params=PARAMS,
        cost_estimate=pl.CostEstimate(flops=1 << 10, bytes_accessed=1 << 10, transcendentals=0),
    )(place, mine, other, up)


def swap(value):
    return lax.ppermute(value, "occ", [(o, o ^ 1) for o in range(2 * CHIPS)])


def chips_on(value, by):
    pairs = [
        (2 * y + core, 2 * ((y + by) % CHIPS) + core) for y in range(CHIPS) for core in range(2)
    ]
    return lax.ppermute(value, "occ", pairs)


def across(value):
    groups = [[2 * y + core for y in range(CHIPS)] for core in range(2)]
    return lax.all_to_all(value, "occ", 0, 0, axis_index_groups=groups)


def to_chips(parts):
    return [parts[0]] + [chips_on(parts[d], d) for d in range(1, CHIPS)]


def pairwise(first, second):
    size = lax.axis_size("space")
    done = []
    for value, start in ((first, 1), (second, 0)):
        pairs = [(i, i + 1) for i in range(start, size - 1, 2)]
        pairs += [(j, i) for i, j in pairs]
        done.append(lax.ppermute(value, "space", sorted(pairs)))
    return done


def on_device(own, mask):
    index = lax.axis_index("occ")
    place = jnp.stack([index % 2, index // 2, lax.axis_index("space") % 2]).astype(jnp.int32)
    own_sib = swap(own)
    first, second = pairwise(*first_factors(own))
    mine = {"own": own, "sib": own_sib}
    blocks = {k: ([("own", k)], [("sib", k)]) for k in range(3)}
    coded0, first2, second2 = pair_products(
        place, [(0, 1), (0, 2), (1, 2)], blocks, mine, together=True, mask=mask
    )
    first2, second2 = pairwise(first2, second2)
    got0 = [across(coded0)]
    first, second, got0 = lax.optimization_barrier((first, second, got0))
    low_a, low_b, high, other = arrived(place, first, second)
    low_as, low_bs, high_sib = swap((low_a, low_b, other))
    blocks["L"] = [("low_a", 0), ("low_b", 0)], [("low_as", 0), ("low_bs", 0)]
    blocks["H"] = [("high", 0)], [("high_sib", 0)]
    coded1 = pair_products(
        place,
        [("L", 0), ("L", 1), ("L", 2), (0, "H"), (1, "H"), ("L", "H")],
        blocks,
        mine
        | {"low_a": low_a, "low_b": low_b, "low_as": low_as, "low_bs": low_bs}
        | {"high": high, "high_sib": high_sib},
    )
    got1 = to_chips(coded1)
    outs = add_parts(
        place,
        got0,
        [mask],
        None,
        [
            ((0, 0, 0), [("f", 0, 0), ("b", 1, 0)]),
            ((0, 0, 1), [("f", 0, 1), ("b", 2, 1)]),
            ((0, 1, 0), [("f", 1, 0), ("b", 2, 0)]),
        ],
    )
    near, _ = lax.optimization_barrier((own_sib, coded1[0]))
    near = bring(near)
    first2, second2, _, outs, near = lax.optimization_barrier((first2, second2, coded1[0], outs, near))
    blocks["H2"] = [("high2", 0)], [("high2", 1)]
    blocks["L2"] = [("low2", 0)], [("low2", 1)]
    *coded2, lines = pair_products(
        place,
        [(0, "H2"), (1, "H2"), ("L2", 2)],
        blocks,
        {"own": own, "sib": near} | {"first": first2, "second": second2},
        halved=("L2",),
        late=True,
    )
    got2 = to_chips(coded2)
    *outs, up1, down1 = add_parts(
        place,
        got1,
        [mask, lines],
        outs,
        [
            ((1, 2, 0), [("b", 0, 0), ("m", 1, 0)]),
            ((1, 2, 1), [("b", 1, 1), ("m", 1, 1)]),
            ((1, 2, 2), [("b", 2, 2), ("m", 1, 2)]),
            ((0, 0, 2), [("f", 0, 2), ("m", 0, 0)]),
            ((0, 1, 1), [("f", 1, 1), ("m", 0, 1)]),
            ((1, 2, 3), [("m", 0, 2), ("m", 1, 3)]),
        ],
        (3, 4),
    )
    first3, second3 = pairwise(up1, down1)
    *outs, up2, mine_half, other_half = add_parts(
        place,
        got2,
        [mask, lines],
        outs,
        [
            ((0, 0, 3), [("f", 0, 3), ("m", 0, 0)]),
            ((0, 1, 2), [("f", 1, 2), ("m", 0, 1)]),
            ((1, 1, 3), [("halves",)]),
        ],
        (2,),
        halves=True,
    )
    block, first4, second4 = join_halves(place, mine_half, swap(other_half), up2)
    first4, second4 = pairwise(first4, second4)
    outs = place_results(
        place,
        first3,
        second3,
        outs,
        [("b", 0, 2), ("b", 0, 1), ("b", 0, 3)],
        [("f", 2, 0), ("f", 2, 1), ("f", 2, 2), ("f", 2, 3)],
        [block],
        [("b", 2, 3)],
    )
    forward, backward = place_results(
        place, first4, second4, outs, [("b", 1, 3), ("b", 1, 2)], [("f", 1, 3)]
    )
    return jnp.swapaxes(forward, 2, 3), backward


def solution(mesh):
    in_specs = (P("space", None, "occ"), P("space", None))
    out_specs = (P("space", None, None, "occ"), P("space", None, "occ", None))
    return jax.shard_map(
        on_device, mesh=mesh, in_specs=in_specs, out_specs=out_specs, check_vma=False
    )
```

time: 101 us -> 92.5 us (0.916)
  starting transfers between devices: 47.4 us -> 33.9 us
  waiting for transfers between devices: 17.6 us -> 25.3 us
  local copies, waits for them, and re-layouts: 5.59 us -> 0.01 us
  Pallas kernels: 28.4 us -> 30.9 us
    ppermute x9 -> x8, starting transfers between devices: 30.2 us -> 16.6 us  [pairwise(): done.append(lax.ppermute(value, 'space', sorted(pairs)))]
    slice x2 -> x0, local copies, waits for them, and re-layouts: 4.68 us -> none  [the longest x1 2.41 us: on_device(): low = own[2:3]]
    ppermute x9 -> x8, waiting for transfers between devices: 12.8 us -> 17.4 us  [pairwise(): done.append(lax.ppermute(value, 'space', sorted(pairs)))]
    ppermute x6, waiting for transfers between devices: 1.94 us -> 3.92 us  [chips_on(): return lax.ppermute(value, 'occ', pairs)]
    pallas_call x4 -> x6, Pallas kernels: 8.12 us -> 9.66 us  [the longest x2 3.06 us: place_results(): pl.pallas_call(functools.partial(place_kernel, below_places, above_places...]
    ppermute x5, waiting for transfers between devices: 2.81 us -> 4.05 us  [swap(): return lax.ppermute(value, 'occ', [(o, o ^ 1) for o in range(2 * CHIPS)])]
  transfers between devices with their start and end apart: 21 -> 20, of which waited for: 9 -> 11; matrix products, arithmetic and copies ran while one was open for 5% -> 1% of each run, Pallas kernels for 27% -> 32%
where the time goes in v3:
time: 92.5 us; the launch traced here: 91.8 us
  starting transfers between devices  33.9 us (37%)
  Pallas kernels  30.9 us (33%)
  waiting for transfers between devices  25.3 us (27%)
  between operations  0.98 us (1%)
    ppermute x8, waiting for transfers between devices, pairwise(): done.append(lax.ppermute(value, 'space', sorted(pairs)))  17.4 us
    ppermute x8, starting transfers between devices, pairwise(): done.append(lax.ppermute(value, 'space', sorted(pairs)))  16.6 us
    pallas_call x3, Pallas kernels, pair_products(): pl.pallas_call(functools.partial(pair_kernel, pairs, blocks, halved, name...  15.3 us
    ppermute x6, starting transfers between devices, chips_on(): return lax.ppermute(value, 'occ', pairs)  11.8 us
    pallas_call x3, Pallas kernels, add_parts(): pl.pallas_call(functools.partial(add_kernel, places, first, sizes, halves...  5.93 us
    all_to_all x1, starting transfers between devices, across(): return lax.all_to_all(value, 'occ', 0, 0, axis_index_groups=groups)  4.73 us
    ppermute x5, waiting for transfers between devices, swap(): return lax.ppermute(value, 'occ', [(o, o ^ 1) for o in range(2 * CHIPS)])  4.05 us
    ppermute x6, waiting for transfers between devices, chips_on(): return lax.ppermute(value, 'occ', pairs)  3.92 us
  transfers between devices with their start and end apart: 20, of which 11 were waited for; matrix products, arithmetic and copies ran while one was open for 1% of the time, Pallas kernels for 32%

profile of v3, /device:TPU:96, one launch (start us, length us, event | category | flops | bytes accessed | tf_op | source)
XLA Modules:
  0.0 91.8 jit_solution(2306727212436005911)
XLA Ops:
  0.7 2.4 %shard_map.42 = (bf16[1,512,1024]{2,1,0:T(8,128)(2,1)}, bf16[1,512,1024]{2,1,0:T(8,128)(2,1)}) custom-call(bf16[3,512,1024]{2,1,0:T(8,128)(2,1)} %refs_0_.5), custom_call_target="tpu_custom_call" | custom-call | flops 1024 | bytes 1024 | tf_op jit(solution)/shard_map/pallas_call | solution.py:217
  3.1 4.5 %collective-permute-start.3 = (bf16[1,512,1024]{2,1,0:T(8,128)(2,1)}, bf16[1,512,1024]{2,1,0:T(8,128)(2,1)}, u32[]{:S(2)}, u32[]{:S(2)}) collective-permute-start(bf16[1,512,1024]{2,1,0:T(8,128)(2,1)} %get-tuple-element.49), channel_id=1, source_target_pairs={{8,16},{16,8},{24,32},{32,24},{40,48},{48,40},{56,64},{64,56},{72,... | collective-permute-start | bytes 3145736 | tf_op jit(solution)/shard_map/ppermute | solution.py:495
  8.1 0.7 pad_add_fusion.place_ref
  8.8 5.9 %shard_map.41 = (s16[4,208,512]{2,1,0:T(8,128)(2,1)}, bf16[2,272,1024]{2,1,0:T(8,128)(2,1)}, bf16[2,272,1024]{2,1,0:T(8,128)(2,1)}) custom-call(s32[3]{0:T(128)} %pad_add_fusion.place_ref, bf16[3,512,1024]{2,1,0:T(8,128)(2,1)} %refs_0_.5, bf16[3,512,1024]{2,1,0:T(8,128)(2,1)} %collective-permute-done.refs_1_.ref, s32[3,4]{1,0:T(4,128)} %refs_4_.3), custom_call_target="tpu_custom_call" | custom-call | flops 1048576 | bytes 65536 | tf_op jit(solution)/shard_map/pallas_call | solution.py:183
  14.7 4.7 %all-to-all-start = ((s16[4,208,512]{2,1,0:T(8,128)(2,1)}), s16[4,208,512]{2,1,0:T(8,128)(2,1)}, u32[]{:S(2)}, u32[]{:S(2)}) async-start(s16[4,208,512]{2,1,0:T(8,128)(2,1)} %get-tuple-element.51), calls=%async_computation | async-start | bytes 1703936 | tf_op jit(solution)/shard_map/all_to_all | solution.py:482
  19.4 3.1 %collective-permute-start.1 = (bf16[2,272,1024]{2,1,0:T(8,128)(2,1)}, bf16[2,272,1024]{2,1,0:T(8,128)(2,1)}, u32[]{:S(2)}, u32[]{:S(2)}) collective-permute-start(bf16[2,272,1024]{2,1,0:T(8,128)(2,1)} %get-tuple-element.47), channel_id=1, source_target_pairs={{8,16},{16,8},{24,32},{32,24},{40,48},{48,40},{56,64},{64,56},{72,... | collective-permute-start | bytes 3342344 | tf_op jit(solution)/shard_map/ppermute | solution.py:495
  23.1 10.4 %collective-permute-done.3.first_ref = bf16[1,512,1024]{2,1,0:T(8,128)(2,1)} collective-permute-done((bf16[1,512,1024]{2,1,0:T(8,128)(2,1)}, bf16[1,512,1024]{2,1,0:T(8,128)(2,1)}, u32[]{:S(2)}, u32[]{:S(2)}) %collective-permute-start.3) | collective-permute-done | bytes 1048608 | tf_op jit(solution)/shard_map/ppermute | solution.py:495
  34.1 1.7 %shard_map.43 = (bf16[1,256,1024]{2,1,0:T(8,128)(2,1)S(1)}, bf16[1,256,1024]{2,1,0:T(8,128)(2,1)S(1)}, bf16[1,256,1024]{2,1,0:T(8,128)(2,1)S(1)}, bf16[1,256,1024]{2,1,0:T(8,128)(2,1)S(1)}) custom-call(s32[3]{0:T(128)S(1)} %copy-done.1, bf16[1,512,1024]{2,1,0:T(8,128)(2,1)} %collective-permute-done.3.first_ref, ...), custom_call_target="tpu_custom_call" | custom-call | flops 1024 | bytes 1024 | tf_op jit(solution)/shard_map/pallas_call | solution.py:268
  36.4 1.3 %collective-permute-done.7.refs_7_ = bf16[1,256,1024]{2,1,0:T(8,128)(2,1)S(1)} collective-permute-done((bf16[1,256,1024]{2,1,0:T(8,128)(2,1)S(1)}, bf16[1,256,1024]{2,1,0:T(8,128)(2,1)S(1)}, u32[]{:S(2)}, u32[]{:S(2)}) %collective-permute-start.7) | collective-permute-done | bytes 524320 | tf_op jit(solution)/shard_map/ppermute | solution.py:470
  37.8 0.7 collective-permute-done.5.refs_4_
  38.5 0.7 collective-permute-done.6.refs_5_
  39.3 5.6 %shard_map.44 = (s16[400,512]{1,0:T(8,128)(2,1)S(1)}, s16[400,512]{1,0:T(8,128)(2,1)S(1)}, s16[400,512]{1,0:T(8,128)(2,1)S(1)}, s16[400,512]{1,0:T(8,128)(2,1)S(1)}) custom-call(s32[3]{0:T(128)S(1)} %copy-done.1, bf16[3,512,1024]{2,1,0:T(8,128)(2,1)S(1)} %copy-done, bf16[3,512,1024]{2,1,0:T(8,128)(2,1)} %collective-permute-done.refs_1_.ref, ...), custom_call_target="tpu_custom_call" | custom-call | flops 1048576 | bytes 65536 | tf_op jit(solution)/shard_map/pallas_call | solution.py:183
  44.9 1.7 %collective-permute-start.11 = (s16[400,512]{1,0:T(8,128)(2,1)S(1)}, s16[400,512]{1,0:T(8,128)(2,1)S(1)}, u32[]{:S(2)}, u32[]{:S(2)}) collective-permute-start(s16[400,512]{1,0:T(8,128)(2,1)S(1)} %get-tuple-element.71), channel_id=1, source_target_pairs={{0,2},{1,3},{2,4},{3,5},{4,6},{5,7},{6,0},{7,1},{8,10},{9,11},{10,... | collective-permute-start | bytes 1228808 | tf_op jit(solution)/shard_map/ppermute | solution.py:477
  46.6 2.9 %collective-permute-start.12 = (s16[400,512]{1,0:T(8,128)(2,1)S(1)}, s16[400,512]{1,0:T(8,128)(2,1)S(1)}, u32[]{:S(2)}, u32[]{:S(2)}) collective-permute-start(s16[400,512]{1,0:T(8,128)(2,1)S(1)} %get-tuple-element.72), channel_id=1, source_target_pairs={{0,4},{1,5},{2,6},{3,7},{4,0},{5,1},{6,2},{7,3},{8,12},{9,13},{10,... | collective-permute-start | bytes 1228808 | tf_op jit(solution)/shard_map/ppermute | solution.py:477
  49.5 1.3 %collective-permute-start.13 = (s16[400,512]{1,0:T(8,128)(2,1)S(1)}, s16[400,512]{1,0:T(8,128)(2,1)S(1)}, u32[]{:S(2)}, u32[]{:S(2)}) collective-permute-start(s16[400,512]{1,0:T(8,128)(2,1)S(1)} %get-tuple-element.73), channel_id=1, source_target_pairs={{0,6},{1,7},{2,0},{3,1},{4,2},{5,3},{6,4},{7,5},{8,14},{9,15},{10,... | collective-permute-start | bytes 1228808 | tf_op jit(solution)/shard_map/ppermute | solution.py:477
  50.8 2.3 %shard_map.45 = (f32[3,4,64,512]{3,2,1,0:T(8,128)}, f32[3,4,64,512]{3,2,1,0:T(8,128)}) custom-call(s32[3]{0:T(128)S(1)} %copy-done.1, s16[4,208,512]{2,1,0:T(8,128)(2,1)} %all-to-all-done.refs_0_, s32[3,4]{1,0:T(4,128)S(1)} %copy-done.2), custom_call_target="tpu_custom_call" | custom-call | flops 1048576 | bytes 65536 | tf_op jit(solution)/shard_map/pallas_call | solution.py:363
  53.1 1.9 %shard_map.46.refs_1_ = bf16[3,512,1024]{2,1,0:T(8,128)(2,1)S(1)} custom-call(bf16[3,512,1024]{2,1,0:T(8,128)(2,1)} %collective-permute-done.refs_1_.ref), custom_call_target="tpu_custom_call" | custom-call | flops 1024 | bytes 1024 | tf_op jit(solution)/shard_map/pallas_call | solution.py:238
  55.0 1.8 %collective-permute-done.1.refs_2_ = bf16[2,272,1024]{2,1,0:T(8,128)(2,1)} collective-permute-done((bf16[2,272,1024]{2,1,0:T(8,128)(2,1)}, bf16[2,272,1024]{2,1,0:T(8,128)(2,1)}, u32[]{:S(2)}, u32[]{:S(2)}) %collective-permute-start.1) | collective-permute-done | bytes 1114144 | tf_op jit(solution)/shard_map/ppermute | solution.py:495
  57.2 3.8 %shard_map.47 = (s16[208,512]{1,0:T(8,128)(2,1)S(1)}, s16[208,512]{1,0:T(8,128)(2,1)S(1)}, s16[208,512]{1,0:T(8,128)(2,1)S(1)}, s16[208,512]{1,0:T(8,128)(2,1)S(1)}, f32[16,512]{1,0:T(8,128)S(1)}) custom-call(s32[3]{0:T(128)S(1)} %copy-done.1, bf16[3,512,1024]{2,1,0:T(8,128)(2,1)S(1)} %copy-done, bf16[3,512,1024]{2,1,0:T(8,128)(2,1)S(1)} %shard_map.46.refs_1_, ...), custom_call_target="tpu_custom_call" | custom-call | flops 1048576 | bytes 65536 | tf_op jit(solution)/shard_map/pallas_call | solution.py:183
  61.0 1.6 %collective-permute-start.8 = (s16[208,512]{1,0:T(8,128)(2,1)S(1)}, s16[208,512]{1,0:T(8,128)(2,1)S(1)}, u32[]{:S(2)}, u32[]{:S(2)}) collective-permute-start(s16[208,512]{1,0:T(8,128)(2,1)S(1)} %get-tuple-element.67), channel_id=1, source_target_pairs={{0,2},{1,3},{2,4},{3,5},{4,6},{5,7},{6,0},{7,1},{8,10},{9,11},{10,... | collective-permute-start | bytes 638984 | tf_op jit(solution)/shard_map/ppermute | solution.py:477
  62.6 2.9 %collective-permute-start.9 = (s16[208,512]{1,0:T(8,128)(2,1)S(1)}, s16[208,512]{1,0:T(8,128)(2,1)S(1)}, u32[]{:S(2)}, u32[]{:S(2)}) collective-permute-start(s16[208,512]{1,0:T(8,128)(2,1)S(1)} %get-tuple-element.68), channel_id=1, source_target_pairs={{0,4},{1,5},{2,6},{3,7},{4,0},{5,1},{6,2},{7,3},{8,12},{9,13},{10,... | collective-permute-start | bytes 638984 | tf_op jit(solution)/shard_map/ppermute | solution.py:477
  65.5 1.3 %collective-permute-start.10 = (s16[208,512]{1,0:T(8,128)(2,1)S(1)}, s16[208,512]{1,0:T(8,128)(2,1)S(1)}, u32[]{:S(2)}, u32[]{:S(2)}) collective-permute-start(s16[208,512]{1,0:T(8,128)(2,1)S(1)} %get-tuple-element.69), channel_id=1, source_target_pairs={{0,6},{1,7},{2,0},{3,1},{4,2},{5,3},{6,4},{7,5},{8,14},{9,15},{10,... | collective-permute-start | bytes 638984 | tf_op jit(solution)/shard_map/ppermute | solution.py:477
  66.9 1.7 %collective-permute-done.12.refs_2_ = s16[400,512]{1,0:T(8,128)(2,1)S(1)} collective-permute-done((s16[400,512]{1,0:T(8,128)(2,1)S(1)}, s16[400,512]{1,0:T(8,128)(2,1)S(1)}, u32[]{:S(2)}, u32[]{:S(2)}) %collective-permute-start.12) | collective-permute-done | bytes 409632 | tf_op jit(solution)/shard_map/ppermute | solution.py:477
  68.6 2.1 %shard_map.48 = (f32[3,4,64,512]{3,2,1,0:T(8,128)}, f32[3,4,64,512]{3,2,1,0:T(8,128)}, s16[272,512]{1,0:T(8,128)(2,1)S(1)}, s16[272,512]{1,0:T(8,128)(2,1)S(1)}) custom-call(s32[3]{0:T(128)S(1)} %copy-done.1, s16[400,512]{1,0:T(8,128)(2,1)S(1)} %get-tuple-element.58.refs_0_, ...), custom_call_target="tpu_custom_call", output_to_operand_aliasing={{0}: (7, {}), {1}: (8, {})} | custom-call | flops 1048576 | bytes 65536 | tf_op jit(solution)/shard_map/pallas_call | solution.py:363
  70.7 3.9 %collective-permute-start.17 = (s16[272,512]{1,0:T(8,128)(2,1)S(1)}, s16[272,512]{1,0:T(8,128)(2,1)S(1)}, u32[]{:S(2)}, u32[]{:S(2)}) collective-permute-start(s16[272,512]{1,0:T(8,128)(2,1)S(1)} %get-tuple-element.83), channel_id=1, source_target_pairs={{8,16},{16,8},{24,32},{32,24},{40,48},{48,40},{56,64},{64,56},{72,... | collective-permute-start | bytes 835592 | tf_op jit(solution)/shard_map/ppermute | solution.py:495
  74.7 2.2 %collective-permute-done.9.refs_2_ = s16[208,512]{1,0:T(8,128)(2,1)S(1)} collective-permute-done((s16[208,512]{1,0:T(8,128)(2,1)S(1)}, s16[208,512]{1,0:T(8,128)(2,1)S(1)}, u32[]{:S(2)}, u32[]{:S(2)}) %collective-permute-start.9) | collective-permute-done | bytes 213024 | tf_op jit(solution)/shard_map/ppermute | solution.py:477
  76.9 1.5 %shard_map.49 = (f32[3,4,64,512]{3,2,1,0:T(8,128)}, f32[3,4,64,512]{3,2,1,0:T(8,128)}, s16[144,512]{1,0:T(8,128)(2,1)S(1)}, f32[64,256]{1,0:T(8,128)S(1)}, f32[64,256]{1,0:T(8,128)S(1)}) custom-call(s32[3]{0:T(128)S(1)} %copy-done.1, s16[208,512]{1,0:T(8,128)(2,1)S(1)} %get-tuple-element.66.refs_0_, ...), custom_call_target="tpu_custom_call", output_to_operand_aliasing={{0}: (7, {}), {1}: (8, {})} | custom-call | flops 1048576 | bytes 65536 | tf_op jit(solution)/shard_map/pallas_call | solution.py:363
  78.5 1.2 %collective-permute-done.14.other_ref = f32[64,256]{1,0:T(8,128)S(1)} collective-permute-done((f32[64,256]{1,0:T(8,128)S(1)}, f32[64,256]{1,0:T(8,128)S(1)}, u32[]{:S(2)}, u32[]{:S(2)}) %collective-permute-start.14) | collective-permute-done | bytes 65568 | tf_op jit(solution)/shard_map/ppermute | solution.py:470
  80.3 3.9 %collective-permute-start.15 = (s16[144,512]{1,0:T(8,128)(2,1)S(1)}, s16[144,512]{1,0:T(8,128)(2,1)S(1)}, u32[]{:S(2)}, u32[]{:S(2)}) collective-permute-start(s16[144,512]{1,0:T(8,128)(2,1)S(1)} %get-tuple-element.81), channel_id=1, source_target_pairs={{8,16},{16,8},{24,32},{32,24},{40,48},{48,40},{56,64},{64,56},{72,... | collective-permute-start | bytes 442376 | tf_op jit(solution)/shard_map/ppermute | solution.py:495
  84.4 1.7 %shard_map.51 = (f32[3,4,64,512]{3,2,1,0:T(8,128)}, f32[3,4,64,512]{3,2,1,0:T(8,128)}) custom-call(s32[3]{0:T(128)S(1)} %copy-done.1, s16[272,512]{1,0:T(8,128)(2,1)S(1)} %collective-permute-done.17.first_ref, s16[272,512]{1,0:T(8,128)(2,1)S(1)} %collective-permute-done.18.second_ref, ...), custom_call_target="tpu_custom_call", output_to_operand_aliasing={{0}: (4, {}), {1}: (5, {})} | custom-call | flops 1048576 | bytes 65536 | tf_op jit(solution)/shard_map/pallas_call | solution.py:416
  86.1 4.2 %collective-permute-done.15.first_ref = s16[144,512]{1,0:T(8,128)(2,1)S(1)} collective-permute-done((s16[144,512]{1,0:T(8,128)(2,1)S(1)}, s16[144,512]{1,0:T(8,128)(2,1)S(1)}, u32[]{:S(2)}, u32[]{:S(2)}) %collective-permute-start.15) | collective-permute-done | bytes 147488 | tf_op jit(solution)/shard_map/ppermute | solution.py:495
  90.3 1.4 %shard_map.52 = (f32[3,4,64,512]{3,2,1,0:T(8,128)}, f32[3,4,64,512]{3,2,1,0:T(8,128)}) custom-call(s32[3]{0:T(128)S(1)} %copy-done.1, s16[144,512]{1,0:T(8,128)(2,1)S(1)} %collective-permute-done.15.first_ref, s16[144,512]{1,0:T(8,128)(2,1)S(1)} %collective-permute-done.16.second_ref, ...), custom_call_target="tpu_custom_call", output_to_operand_aliasing={{0}: (3, {}), {1}: (4, {})} | custom-call | flops 1048576 | bytes 65536 | tf_op jit(solution)/shard_map/pallas_call | solution.py:416
  (27 shorter events, 3.6 us)
Async XLA Ops:
  0.6 8.1 %collective-permute-start = (bf16[3,512,1024]{2,1,0:T(8,128)(2,1)}, bf16[3,512,1024]{2,1,0:T(8,128)(2,1)}, u32[]{:S(2)}, u32[]{:S(2)}) collective-permute-start(bf16[3,512,1024]{2,1,0:T(8,128)(2,1)} %refs_0_.5), channel_id=1, source_target_pairs={{0,1},{1,0},{2,3},{3,2},{4,5},{5,4},{6,7},{7,6},{8,9},{9,8},{10,11... | collective-permute-start | bytes 9437192 | tf_op jit(solution)/shard_map/ppermute | solution.py:470
  3.1 30.3 %collective-permute-start.3 = (bf16[1,512,1024]{2,1,0:T(8,128)(2,1)}, bf16[1,512,1024]{2,1,0:T(8,128)(2,1)}, u32[]{:S(2)}, u32[]{:S(2)}) collective-permute-start(bf16[1,512,1024]{2,1,0:T(8,128)(2,1)} %get-tuple-element.49), channel_id=1, source_target_pairs={{8,16},{16,8},{24,32},{32,24},{40,48},{48,40},{56,64},{64,56},{72,... | collective-permute-start | bytes 3145736 | tf_op jit(solution)/shard_map/ppermute | solution.py:495
  7.7 26.4 %collective-permute-start.4 = (bf16[1,512,1024]{2,1,0:T(8,128)(2,1)}, bf16[1,512,1024]{2,1,0:T(8,128)(2,1)}, u32[]{:S(2)}, u32[]{:S(2)}) collective-permute-start(bf16[1,512,1024]{2,1,0:T(8,128)(2,1)} %get-tuple-element.50), channel_id=1, source_target_pairs={{0,8},{8,0},{16,24},{24,16},{32,40},{40,32},{48,56},{56,48},{64,72... | collective-permute-start | bytes 3145736 | tf_op jit(solution)/shard_map/ppermute | solution.py:495
  14.7 19.4 %copy-start.1 = (s32[3]{0:T(128)S(1)}, s32[3]{0:T(128)}, u32[]{:S(2)}) copy-start(s32[3]{0:T(128)} %pad_add_fusion.place_ref) | copy-start | bytes 40
  14.7 24.6 %copy-start = (bf16[3,512,1024]{2,1,0:T(8,128)(2,1)S(1)}, bf16[3,512,1024]{2,1,0:T(8,128)(2,1)}, u32[]{:S(2)}) copy-start(bf16[3,512,1024]{2,1,0:T(8,128)(2,1)} %refs_0_.5) | copy-start | bytes 9437188
  14.7 19.4 %all-to-all-start = ((s16[4,208,512]{2,1,0:T(8,128)(2,1)}), s16[4,208,512]{2,1,0:T(8,128)(2,1)}, u32[]{:S(2)}, u32[]{:S(2)}) async-start(s16[4,208,512]{2,1,0:T(8,128)(2,1)} %get-tuple-element.51), calls=%async_computation | async-start | bytes 1703936 | tf_op jit(solution)/shard_map/all_to_all | solution.py:482
  19.4 37.5 %collective-permute-start.1 = (bf16[2,272,1024]{2,1,0:T(8,128)(2,1)}, bf16[2,272,1024]{2,1,0:T(8,128)(2,1)}, u32[]{:S(2)}, u32[]{:S(2)}) collective-permute-start(bf16[2,272,1024]{2,1,0:T(8,128)(2,1)} %get-tuple-element.47), channel_id=1, source_target_pairs={{8,16},{16,8},{24,32},{32,24},{40,48},{48,40},{56,64},{64,56},{72,... | collective-permute-start | bytes 3342344 | tf_op jit(solution)/shard_map/ppermute | solution.py:495
  22.5 34.7 %collective-permute-start.2 = (bf16[2,272,1024]{2,1,0:T(8,128)(2,1)}, bf16[2,272,1024]{2,1,0:T(8,128)(2,1)}, u32[]{:S(2)}, u32[]{:S(2)}) collective-permute-start(bf16[2,272,1024]{2,1,0:T(8,128)(2,1)} %get-tuple-element.48), channel_id=1, source_target_pairs={{0,8},{8,0},{16,24},{24,16},{32,40},{40,32},{48,56},{56,48},{64,72... | collective-permute-start | bytes 3342344 | tf_op jit(solution)/shard_map/ppermute | solution.py:495
  35.8 2.0 %collective-permute-start.7 = (bf16[1,256,1024]{2,1,0:T(8,128)(2,1)S(1)}, bf16[1,256,1024]{2,1,0:T(8,128)(2,1)S(1)}, u32[]{:S(2)}, u32[]{:S(2)}) collective-permute-start(bf16[1,256,1024]{2,1,0:T(8,128)(2,1)S(1)} %get-tuple-element.57), channel_id=1, source_target_pairs={{0,1},{1,0},{2,3},{3,2},{4,5},{5,4},{6,7},{7,6},{8,9},{9,8},{10,11... | collective-permute-start | bytes 1572872 | tf_op jit(solution)/shard_map/ppermute | solution.py:470
  35.9 2.6 %collective-permute-start.5 = (bf16[1,256,1024]{2,1,0:T(8,128)(2,1)S(1)}, bf16[1,256,1024]{2,1,0:T(8,128)(2,1)S(1)}, u32[]{:S(2)}, u32[]{:S(2)}) collective-permute-start(bf16[1,256,1024]{2,1,0:T(8,128)(2,1)S(1)} %get-tuple-element.54.refs_2_), channel_id=1, source_target_pairs={{0,1},{1,0},{2,3},{3,2},{4,5},{5,4},{6,7},{7,6},{8,9},{9,8},{10,11... | collective-permute-start | bytes 1572872 | tf_op jit(solution)/shard_map/ppermute | solution.py:470
  36.4 2.9 %collective-permute-start.6 = (bf16[1,256,1024]{2,1,0:T(8,128)(2,1)S(1)}, bf16[1,256,1024]{2,1,0:T(8,128)(2,1)S(1)}, u32[]{:S(2)}, u32[]{:S(2)}) collective-permute-start(bf16[1,256,1024]{2,1,0:T(8,128)(2,1)S(1)} %get-tuple-element.55.refs_3_), channel_id=1, source_target_pairs={{0,1},{1,0},{2,3},{3,2},{4,5},{5,4},{6,7},{7,6},{8,9},{9,8},{10,11... | collective-permute-start | bytes 1572872 | tf_op jit(solution)/shard_map/ppermute | solution.py:470
  39.3 11.6 %copy-start.2 = (s32[3,4]{1,0:T(4,128)S(1)}, s32[3,4]{1,0:T(4,128)}, u32[]{:S(2)}) copy-start(s32[3,4]{1,0:T(4,128)} %refs_4_.3) | copy-start | bytes 148
  44.9 20.6 %collective-permute-start.11 = (s16[400,512]{1,0:T(8,128)(2,1)S(1)}, s16[400,512]{1,0:T(8,128)(2,1)S(1)}, u32[]{:S(2)}, u32[]{:S(2)}) collective-permute-start(s16[400,512]{1,0:T(8,128)(2,1)S(1)} %get-tuple-element.71), channel_id=1, source_target_pairs={{0,2},{1,3},{2,4},{3,5},{4,6},{5,7},{6,0},{7,1},{8,10},{9,11},{10,... | collective-permute-start | bytes 1228808 | tf_op jit(solution)/shard_map/ppermute | solution.py:477
  46.6 22.0 %collective-permute-start.12 = (s16[400,512]{1,0:T(8,128)(2,1)S(1)}, s16[400,512]{1,0:T(8,128)(2,1)S(1)}, u32[]{:S(2)}, u32[]{:S(2)}) collective-permute-start(s16[400,512]{1,0:T(8,128)(2,1)S(1)} %get-tuple-element.72), channel_id=1, source_target_pairs={{0,4},{1,5},{2,6},{3,7},{4,0},{5,1},{6,2},{7,3},{8,12},{9,13},{10,... | collective-permute-start | bytes 1228808 | tf_op jit(solution)/shard_map/ppermute | solution.py:477
  49.5 19.1 %collective-permute-start.13 = (s16[400,512]{1,0:T(8,128)(2,1)S(1)}, s16[400,512]{1,0:T(8,128)(2,1)S(1)}, u32[]{:S(2)}, u32[]{:S(2)}) collective-permute-start(s16[400,512]{1,0:T(8,128)(2,1)S(1)} %get-tuple-element.73), channel_id=1, source_target_pairs={{0,6},{1,7},{2,0},{3,1},{4,2},{5,3},{6,4},{7,5},{8,14},{9,15},{10,... | collective-permute-start | bytes 1228808 | tf_op jit(solution)/shard_map/ppermute | solution.py:477
  61.0 13.7 %collective-permute-start.8 = (s16[208,512]{1,0:T(8,128)(2,1)S(1)}, s16[208,512]{1,0:T(8,128)(2,1)S(1)}, u32[]{:S(2)}, u32[]{:S(2)}) collective-permute-start(s16[208,512]{1,0:T(8,128)(2,1)S(1)} %get-tuple-element.67), channel_id=1, source_target_pairs={{0,2},{1,3},{2,4},{3,5},{4,6},{5,7},{6,0},{7,1},{8,10},{9,11},{10,... | collective-permute-start | bytes 638984 | tf_op jit(solution)/shard_map/ppermute | solution.py:477
  62.6 14.3 %collective-permute-start.9 = (s16[208,512]{1,0:T(8,128)(2,1)S(1)}, s16[208,512]{1,0:T(8,128)(2,1)S(1)}, u32[]{:S(2)}, u32[]{:S(2)}) collective-permute-start(s16[208,512]{1,0:T(8,128)(2,1)S(1)} %get-tuple-element.68), channel_id=1, source_target_pairs={{0,4},{1,5},{2,6},{3,7},{4,0},{5,1},{6,2},{7,3},{8,12},{9,13},{10,... | collective-permute-start | bytes 638984 | tf_op jit(solution)/shard_map/ppermute | solution.py:477
  65.5 11.4 %collective-permute-start.10 = (s16[208,512]{1,0:T(8,128)(2,1)S(1)}, s16[208,512]{1,0:T(8,128)(2,1)S(1)}, u32[]{:S(2)}, u32[]{:S(2)}) collective-permute-start(s16[208,512]{1,0:T(8,128)(2,1)S(1)} %get-tuple-element.69), channel_id=1, source_target_pairs={{0,6},{1,7},{2,0},{3,1},{4,2},{5,3},{6,4},{7,5},{8,14},{9,15},{10,... | collective-permute-start | bytes 638984 | tf_op jit(solution)/shard_map/ppermute | solution.py:477
  70.7 13.7 %collective-permute-start.17 = (s16[272,512]{1,0:T(8,128)(2,1)S(1)}, s16[272,512]{1,0:T(8,128)(2,1)S(1)}, u32[]{:S(2)}, u32[]{:S(2)}) collective-permute-start(s16[272,512]{1,0:T(8,128)(2,1)S(1)} %get-tuple-element.83), channel_id=1, source_target_pairs={{8,16},{16,8},{24,32},{32,24},{40,48},{48,40},{56,64},{64,56},{72,... | collective-permute-start | bytes 835592 | tf_op jit(solution)/shard_map/ppermute | solution.py:495
  74.6 9.8 %collective-permute-start.18 = (s16[272,512]{1,0:T(8,128)(2,1)S(1)}, s16[272,512]{1,0:T(8,128)(2,1)S(1)}, u32[]{:S(2)}, u32[]{:S(2)}) collective-permute-start(s16[272,512]{1,0:T(8,128)(2,1)S(1)} %get-tuple-element.84), channel_id=1, source_target_pairs={{0,8},{8,0},{16,24},{24,16},{32,40},{40,32},{48,56},{56,48},{64,72... | collective-permute-start | bytes 835592 | tf_op jit(solution)/shard_map/ppermute | solution.py:495
  78.4 1.3 %collective-permute-start.14 = (f32[64,256]{1,0:T(8,128)S(1)}, f32[64,256]{1,0:T(8,128)S(1)}, u32[]{:S(2)}, u32[]{:S(2)}) collective-permute-start(f32[64,256]{1,0:T(8,128)S(1)} %get-tuple-element.79), channel_id=1, source_target_pairs={{0,1},{1,0},{2,3},{3,2},{4,5},{5,4},{6,7},{7,6},{8,9},{9,8},{10,11... | collective-permute-start | bytes 196616 | tf_op jit(solution)/shard_map/ppermute | solution.py:470
  80.3 9.9 %collective-permute-start.15 = (s16[144,512]{1,0:T(8,128)(2,1)S(1)}, s16[144,512]{1,0:T(8,128)(2,1)S(1)}, u32[]{:S(2)}, u32[]{:S(2)}) collective-permute-start(s16[144,512]{1,0:T(8,128)(2,1)S(1)} %get-tuple-element.81), channel_id=1, source_target_pairs={{8,16},{16,8},{24,32},{32,24},{40,48},{48,40},{56,64},{64,56},{72,... | collective-permute-start | bytes 442376 | tf_op jit(solution)/shard_map/ppermute | solution.py:495
  84.3 6.0 %collective-permute-start.16 = (s16[144,512]{1,0:T(8,128)(2,1)S(1)}, s16[144,512]{1,0:T(8,128)(2,1)S(1)}, u32[]{:S(2)}, u32[]{:S(2)}) collective-permute-start(s16[144,512]{1,0:T(8,128)(2,1)S(1)} %get-tuple-element.82), channel_id=1, source_target_pairs={{0,8},{8,0},{16,24},{24,16},{32,40},{40,32},{48,56},{56,48},{64,72... | collective-permute-start | bytes 442376 | tf_op jit(solution)/shard_map/ppermute | solution.py:495

commit v4 on v3

--- a/solution.py
+++ b/solution.py
@@ -303,13 +303,13 @@
     mask_ref, refs = refs[0], refs[1:]
     if lined:
         lines_ref, refs = refs[0], refs[1:]
-    if not first:
-        refs = refs[2:]
-    (f_ref, b_ref), refs = refs[:2], refs[2:]
-    messages, refs = refs[: len(sizes)], refs[len(sizes) :]
     if halves:
-        (kept_ref, swap_ref), refs = refs[:2], refs[2:]
-    sums, sems = refs
+        messages, (sums, kept_ref, swap_ref) = refs[: len(sizes)], refs[len(sizes) :]
+    else:
+        if not first:
+            refs = refs[2:]
+        (f_ref, b_ref), refs = refs[:2], refs[2:]
+        messages, (sums, sems) = refs[: len(sizes)], refs[len(sizes) :]
     held = [[] for _ in sizes]
     writes = []
     n = len(places)
@@ -338,6 +338,8 @@
                 low, high = total[:, :HALF], total[:, HALF:]
                 kept_ref[...] = jnp.where(first_core, low, high)
                 swap_ref[...] = jnp.where(first_core, high, low)
+            elif kind == "kept":
+                sums[goal[0]] = total
             else:
                 sums[p] = total
                 writes.append((p, (f_ref if kind == "f" else b_ref).at[goal[0], goal[1]]))
@@ -352,75 +354,84 @@
         copy.wait()
 
 
-def add_parts(place, gots, masks, outs, places, sizes=(), halves=False):
+def add_parts(place, gots, masks, outs, places, sizes=(), kept=None):
     n = len(places)
-    first = outs is None
-    earlier = [] if first else list(outs)
-    at = 1 + len(gots) + len(masks)
-    shapes = OUTS + [jax.ShapeDtypeStruct((coded_rows(max(sizes, default=0)), BF), jnp.int16) for _ in sizes]
-    if halves:
+    ins = [place, *gots, *masks]
+    messages = [jax.ShapeDtypeStruct((coded_rows(max(sizes, default=0)), BF), jnp.int16)] * len(sizes)
+    in_specs = [SMEM] + [VMEM] * len(gots) + [SMEM, VMEM][: len(masks)]
+    scratch, aliases = [], {}
+    if kept is not None:
+        shapes = messages + [jax.ShapeDtypeStruct((kept, SLICE, BF), jnp.float32)]
         shapes += [jax.ShapeDtypeStruct((SLICE, HALF), jnp.float32)] * 2
+        out_specs = [VMEM] * len(shapes)
+    else:
+        shapes = OUTS + messages
+        out_specs = [HBM] * 2 + [VMEM] * len(messages)
+        scratch = [pltpu.VMEM((n, SLICE, BF), jnp.float32), pltpu.SemaphoreType.DMA((2 * n,))]
+        if outs is not None:
+            aliases = {len(ins): 0, len(ins) + 1: 1}
+            ins += outs
+            in_specs += [HBM] * 2
+    kernel = functools.partial(
+        add_kernel, places, outs is None, sizes, kept is not None, len(gots), len(masks) > 1
+    )
     return pl.pallas_call(
-        functools.partial(add_kernel, places, first, sizes, halves, len(gots), len(masks) > 1),
+        kernel,
         out_shape=shapes,
-        in_specs=[SMEM] + [VMEM] * len(gots) + [SMEM, VMEM][: len(masks)] + [HBM] * len(earlier),
-        out_specs=[HBM] * 2 + [VMEM] * (len(shapes) - 2),
-        scratch_shapes=[
-            pltpu.VMEM((n, SLICE, BF), jnp.float32),
-            pltpu.SemaphoreType.DMA((2 * n,)),
-        ],
-        input_output_aliases={} if first else {at: 0, at + 1: 1},
+        in_specs=in_specs,
+        out_specs=out_specs,
+        scratch_shapes=scratch,
+        input_output_aliases=aliases,
         compiler_params=PARAMS,
         cost_estimate=pl.CostEstimate(flops=1 << 20, bytes_accessed=1 << 16, transcendentals=0),
-    )(place, *gots, *masks, *earlier)
-
-
-def place_kernel(below_places, above_places, block_places, place_ref, first_ref, second_ref, *refs):
-    blocks, refs = refs[: len(block_places)], refs[len(block_places) + 2 :]
+    )(*ins)
+
+
+def place_kernel(below_places, above_places, block_places, n, place_ref, first_ref, second_ref, *refs):
+    blocks, refs = refs[:n], refs[n + 2 :]
     f_ref, b_ref, sums, sems = refs
-    goals = below_places + above_places + block_places
-
-    def take(*messages):
-        k = 0
-        for ref, count in zip(messages, (len(below_places), len(above_places))):
-            end = ref.shape[0] - 16
-            scales = scales_of(ref[end : end + 16, :])
-            for p in range(count):
-                part = ref[p * SLICE : (p + 1) * SLICE, :].astype(jnp.float32)
-                sums[k] = part * scales[p : p + 1]
+    odd = place_ref[2] == 1
+    end = first_ref.shape[0] - 16
+    scales = [scales_of(ref[end : end + 16, :]) for ref in (first_ref, second_ref)]
+    writes = []
+
+    def write(source, goal):
+        kind, block, slot = goal
+        target = (f_ref if kind == "f" else b_ref).at[block, slot]
+        writes.append(pltpu.make_async_copy(source, target, sems.at[len(writes)]))
+        writes[-1].start()
+
+    goals = iter(block_places)
+    for ref in blocks:
+        for source in [ref] if len(ref.shape) == 2 else [ref.at[k] for k in range(ref.shape[0])]:
+            write(source, next(goals))
+    k = 0
+    for p in range(max(len(below_places), len(above_places))):
+        rows = slice(p * SLICE, (p + 1) * SLICE)
+        first, second = (
+            ref[rows, :].astype(jnp.float32) * scale[p : p + 1]
+            for ref, scale in zip((first_ref, second_ref), scales)
+        )
+        for places, values in ((below_places, (second, first)), (above_places, (first, second))):
+            if p < len(places):
+                sums[k] = jnp.where(odd, *values)
+                write(sums.at[k], places[p])
                 k += 1
-
-    @pl.when(place_ref[2] == 1)
-    def _():
-        take(second_ref, first_ref)
-
-    @pl.when(place_ref[2] == 0)
-    def _():
-        take(first_ref, second_ref)
-
-    for k, block in enumerate(blocks):
-        sums[len(goals) - len(blocks) + k] = block[...]
-    writes = []
-    for k, (kind, block, slot) in enumerate(goals):
-        target = (f_ref if kind == "f" else b_ref).at[block, slot]
-        writes.append(pltpu.make_async_copy(sums.at[k], target, sems.at[k]))
-    for copy in writes:
-        copy.start()
     for copy in writes:
         copy.wait()
 
 
 def place_results(place, first, second, outs, below_places, above_places, blocks=(), block_places=()):
-    total = len(below_places) + len(above_places) + len(blocks)
+    total = len(below_places) + len(above_places)
     n = 3 + len(blocks)
     return pl.pallas_call(
-        functools.partial(place_kernel, below_places, above_places, list(block_places)),
+        functools.partial(place_kernel, below_places, above_places, block_places, len(blocks)),
         out_shape=OUTS,
         in_specs=[SMEM] + [VMEM] * (n - 1) + [HBM] * 2,
         out_specs=[HBM] * 2,
         scratch_shapes=[
             pltpu.VMEM((total, SLICE, BF), jnp.float32),
-            pltpu.SemaphoreType.DMA((total,)),
+            pltpu.SemaphoreType.DMA((total + len(block_places),)),
         ],
         input_output_aliases={n: 0, n + 1: 1},
         compiler_params=PARAMS,
@@ -513,11 +524,12 @@
     low_as, low_bs, high_sib = swap((low_a, low_b, other))
     blocks["L"] = [("low_a", 0), ("low_b", 0)], [("low_as", 0), ("low_bs", 0)]
     blocks["H"] = [("high", 0)], [("high_sib", 0)]
+    near, _ = lax.optimization_barrier((own_sib, low_a))
     coded1 = pair_products(
         place,
         [("L", 0), ("L", 1), ("L", 2), (0, "H"), (1, "H"), ("L", "H")],
         blocks,
-        mine
+        {"own": own, "sib": bring(near)}
         | {"low_a": low_a, "low_b": low_b, "low_as": low_as, "low_bs": low_bs}
         | {"high": high, "high_sib": high_sib},
     )
@@ -563,18 +575,18 @@
         (3, 4),
     )
     first3, second3 = pairwise(up1, down1)
-    *outs, up2, mine_half, other_half = add_parts(
+    up2, kept, mine_half, other_half = add_parts(
         place,
         got2,
         [mask, lines],
-        outs,
+        None,
         [
-            ((0, 0, 3), [("f", 0, 3), ("m", 0, 0)]),
-            ((0, 1, 2), [("f", 1, 2), ("m", 0, 1)]),
+            ((0, 0, 3), [("kept", 0), ("m", 0, 0)]),
+            ((0, 1, 2), [("kept", 1), ("m", 0, 1)]),
             ((1, 1, 3), [("halves",)]),
         ],
         (2,),
-        halves=True,
+        kept=2,
     )
     block, first4, second4 = join_halves(place, mine_half, swap(other_half), up2)
     first4, second4 = pairwise(first4, second4)
@@ -585,8 +597,8 @@
         outs,
         [("b", 0, 2), ("b", 0, 1), ("b", 0, 3)],
         [("f", 2, 0), ("f", 2, 1), ("f", 2, 2), ("f", 2, 3)],
-        [block],
-        [("b", 2, 3)],
+        [block, kept],
+        [("b", 2, 3), ("f", 0, 3), ("f", 1, 2)],
     )
     forward, backward = place_results(
         place, first4, second4, outs, [("b", 1, 3), ("b", 1, 2)], [("f", 1, 3)]

time: 92.5 us -> 90.4 us (0.977)
  Pallas kernels: 30.9 us -> 29.3 us
    pallas_call x3, Pallas kernels: 15.3 us -> 12.9 us  [pair_products(): pl.pallas_call(functools.partial(pair_kernel, pairs, blocks, halved, name...]
    ppermute x5, waiting for transfers between devices: 4.05 us -> 1.98 us  [swap(): return lax.ppermute(value, 'occ', [(o, o ^ 1) for o in range(2 * CHIPS)])]
    pallas_call x1 -> x2, Pallas kernels: 1.9 us -> 3.95 us  [bring(): pl.pallas_call(bring_kernel, out_shape=jax.ShapeDtypeStruct(value.shape,...]
    ppermute x8, waiting for transfers between devices: 17.4 us -> 19.4 us  [pairwise(): done.append(lax.ppermute(value, 'space', sorted(pairs)))]
    pallas_call x3, Pallas kernels: 5.93 us -> 4.68 us  [add_parts(): pl.pallas_call(kernel, out_shape=shapes, in_specs=in_specs, out_specs=out...]
  transfers between devices with their start and end apart: 20 -> 20, of which waited for: 11 -> 9; matrix products, arithmetic and copies ran while one was open for 1% -> 1% of each run, Pallas kernels for 32% -> 31%
where the time goes in v4:
time: 90.4 us; the launch traced here: 90 us
  starting transfers between devices  33.8 us (37%)
  Pallas kernels  29.3 us (32%)
  waiting for transfers between devices  25.3 us (28%)
  between operations  1 us (1%)
    ppermute x8, waiting for transfers between devices, pairwise(): done.append(lax.ppermute(value, 'space', sorted(pairs)))  19.4 us
    ppermute x8, starting transfers between devices, pairwise(): done.append(lax.ppermute(value, 'space', sorted(pairs)))  16.6 us
    pallas_call x3, Pallas kernels, pair_products(): pl.pallas_call(functools.partial(pair_kernel, pairs, blocks, halved, name...  12.9 us
    ppermute x6, starting transfers between devices, chips_on(): return lax.ppermute(value, 'occ', pairs)  11.8 us
    pallas_call x3, Pallas kernels, add_parts(): pl.pallas_call(kernel, out_shape=shapes, in_specs=in_specs, out_specs=out...  4.68 us
    all_to_all x1, starting transfers between devices, across(): return lax.all_to_all(value, 'occ', 0, 0, axis_index_groups=groups)  4.59 us
    ppermute x6, waiting for transfers between devices, chips_on(): return lax.ppermute(value, 'occ', pairs)  3.95 us
    pallas_call x2, Pallas kernels, bring(): pl.pallas_call(bring_kernel, out_shape=jax.ShapeDtypeStruct(value.shape,...  3.95 us
  transfers between devices with their start and end apart: 20, of which 9 were waited for; matrix products, arithmetic and copies ran while one was open for 1% of the time, Pallas kernels for 31%

profile of v4, /device:TPU:96, one launch (start us, length us, event | category | flops | bytes accessed | tf_op | source)
XLA Modules:
  0.0 90.0 jit_solution(6693659703207054698)
XLA Ops:
  0.7 2.4 %shard_map.42 = (bf16[1,512,1024]{2,1,0:T(8,128)(2,1)}, bf16[1,512,1024]{2,1,0:T(8,128)(2,1)}) custom-call(bf16[3,512,1024]{2,1,0:T(8,128)(2,1)} %refs_0_.5), custom_call_target="tpu_custom_call" | custom-call | flops 1024 | bytes 1024 | tf_op jit(solution)/shard_map/pallas_call | solution.py:217
  3.1 4.5 %collective-permute-start.3 = (bf16[1,512,1024]{2,1,0:T(8,128)(2,1)}, bf16[1,512,1024]{2,1,0:T(8,128)(2,1)}, u32[]{:S(2)}, u32[]{:S(2)}) collective-permute-start(bf16[1,512,1024]{2,1,0:T(8,128)(2,1)} %get-tuple-element.49), channel_id=1, source_target_pairs={{8,16},{16,8},{24,32},{32,24},{40,48},{48,40},{56,64},{64,56},{72,... | collective-permute-start | bytes 3145736 | tf_op jit(solution)/shard_map/ppermute | solution.py:506
  8.7 6.0 %shard_map.41 = (s16[4,208,512]{2,1,0:T(8,128)(2,1)}, bf16[2,272,1024]{2,1,0:T(8,128)(2,1)}, bf16[2,272,1024]{2,1,0:T(8,128)(2,1)}) custom-call(s32[3]{0:T(128)} %pad_add_fusion.place_ref, bf16[3,512,1024]{2,1,0:T(8,128)(2,1)} %refs_0_.5, bf16[3,512,1024]{2,1,0:T(8,128)(2,1)} %collective-permute-done.refs_1_.ref, s32[3,4]{1,0:T(4,128)} %refs_4_.3), custom_call_target="tpu_custom_call" | custom-call | flops 1048576 | bytes 65536 | tf_op jit(solution)/shard_map/pallas_call | solution.py:183
  14.7 4.6 %all-to-all-start = ((s16[4,208,512]{2,1,0:T(8,128)(2,1)}), s16[4,208,512]{2,1,0:T(8,128)(2,1)S(1)}, u32[]{:S(2)}, u32[]{:S(2)}) async-start(s16[4,208,512]{2,1,0:T(8,128)(2,1)} %get-tuple-element.51), calls=%async_computation | async-start | bytes 1703936 | tf_op jit(solution)/shard_map/all_to_all | solution.py:493
  19.3 3.1 %collective-permute-start.1 = (bf16[2,272,1024]{2,1,0:T(8,128)(2,1)}, bf16[2,272,1024]{2,1,0:T(8,128)(2,1)S(1)}, u32[]{:S(2)}, u32[]{:S(2)}) collective-permute-start(bf16[2,272,1024]{2,1,0:T(8,128)(2,1)} %get-tuple-element.47), channel_id=1, source_target_pairs={{8,16},{16,8},{24,32},{32,24},{40,48},{48,40},{56,64},{64,56},{72,... | collective-permute-start | bytes 3342344 | tf_op jit(solution)/shard_map/ppermute | solution.py:506
  22.9 10.5 %collective-permute-done.3.first_ref = bf16[1,512,1024]{2,1,0:T(8,128)(2,1)} collective-permute-done((bf16[1,512,1024]{2,1,0:T(8,128)(2,1)}, bf16[1,512,1024]{2,1,0:T(8,128)(2,1)}, u32[]{:S(2)}, u32[]{:S(2)}) %collective-permute-start.3) | collective-permute-done | bytes 1048608 | tf_op jit(solution)/shard_map/ppermute | solution.py:506
  33.4 0.6 collective-permute-done.4.second_ref
  34.1 1.7 %shard_map.43 = (bf16[1,256,1024]{2,1,0:T(8,128)(2,1)S(1)}, bf16[1,256,1024]{2,1,0:T(8,128)(2,1)S(1)}, bf16[1,256,1024]{2,1,0:T(8,128)(2,1)S(1)}, bf16[1,256,1024]{2,1,0:T(8,128)(2,1)S(1)}) custom-call(s32[3]{0:T(128)S(1)} %copy-done.1, bf16[1,512,1024]{2,1,0:T(8,128)(2,1)} %collective-permute-done.3.first_ref, ...), custom_call_target="tpu_custom_call" | custom-call | flops 1024 | bytes 1024 | tf_op jit(solution)/shard_map/pallas_call | solution.py:268
  36.4 2.0 %shard_map.44.refs_1_ = bf16[3,512,1024]{2,1,0:T(8,128)(2,1)S(1)} custom-call(bf16[3,512,1024]{2,1,0:T(8,128)(2,1)} %collective-permute-done.refs_1_.ref), custom_call_target="tpu_custom_call" | custom-call | flops 1024 | bytes 1024 | tf_op jit(solution)/shard_map/pallas_call | solution.py:238
  38.5 0.7 collective-permute-done.5.refs_4_
  39.3 4.2 %shard_map.45 = (s16[400,512]{1,0:T(8,128)(2,1)S(1)}, s16[400,512]{1,0:T(8,128)(2,1)S(1)}, s16[400,512]{1,0:T(8,128)(2,1)S(1)}, s16[400,512]{1,0:T(8,128)(2,1)S(1)}) custom-call(s32[3]{0:T(128)S(1)} %copy-done.1, bf16[3,512,1024]{2,1,0:T(8,128)(2,1)S(1)} %copy-done, bf16[3,512,1024]{2,1,0:T(8,128)(2,1)S(1)} %shard_map.44.refs_1_, ...), custom_call_target="tpu_custom_call" | custom-call | flops 1048576 | bytes 65536 | tf_op jit(solution)/shard_map/pallas_call | solution.py:183
  43.5 1.7 %collective-permute-start.14 = (s16[400,512]{1,0:T(8,128)(2,1)S(1)}, s16[400,512]{1,0:T(8,128)(2,1)S(1)}, u32[]{:S(2)}, u32[]{:S(2)}) collective-permute-start(s16[400,512]{1,0:T(8,128)(2,1)S(1)} %get-tuple-element.77), channel_id=1, source_target_pairs={{0,2},{1,3},{2,4},{3,5},{4,6},{5,7},{6,0},{7,1},{8,10},{9,11},{10,... | collective-permute-start | bytes 1228808 | tf_op jit(solution)/shard_map/ppermute | solution.py:488
  45.2 2.9 %collective-permute-start.15 = (s16[400,512]{1,0:T(8,128)(2,1)S(1)}, s16[400,512]{1,0:T(8,128)(2,1)S(1)}, u32[]{:S(2)}, u32[]{:S(2)}) collective-permute-start(s16[400,512]{1,0:T(8,128)(2,1)S(1)} %get-tuple-element.78), channel_id=1, source_target_pairs={{0,4},{1,5},{2,6},{3,7},{4,0},{5,1},{6,2},{7,3},{8,12},{9,13},{10,... | collective-permute-start | bytes 1228808 | tf_op jit(solution)/shard_map/ppermute | solution.py:488
  48.1 1.3 %collective-permute-start.16 = (s16[400,512]{1,0:T(8,128)(2,1)S(1)}, s16[400,512]{1,0:T(8,128)(2,1)S(1)}, u32[]{:S(2)}, u32[]{:S(2)}) collective-permute-start(s16[400,512]{1,0:T(8,128)(2,1)S(1)} %get-tuple-element.79), channel_id=1, source_target_pairs={{0,6},{1,7},{2,0},{3,1},{4,2},{5,3},{6,4},{7,5},{8,14},{9,15},{10,... | collective-permute-start | bytes 1228808 | tf_op jit(solution)/shard_map/ppermute | solution.py:488
  49.4 1.7 %shard_map.46 = (f32[3,4,64,512]{3,2,1,0:T(8,128)}, f32[3,4,64,512]{3,2,1,0:T(8,128)}) custom-call(s32[3]{0:T(128)S(1)} %copy-done.1, s16[4,208,512]{2,1,0:T(8,128)(2,1)S(1)} %all-to-all-done.refs_0_, s32[3,4]{1,0:T(4,128)S(1)} %copy-done.2), custom_call_target="tpu_custom_call" | custom-call | flops 1048576 | bytes 65536 | tf_op jit(solution)/shard_map/pallas_call | solution.py:378
  51.1 1.9 %shard_map.47.refs_1_ = bf16[3,512,1024]{2,1,0:T(8,128)(2,1)S(1)} custom-call(bf16[3,512,1024]{2,1,0:T(8,128)(2,1)} %collective-permute-done.refs_1_.ref), custom_call_target="tpu_custom_call" | custom-call | flops 1024 | bytes 1024 | tf_op jit(solution)/shard_map/pallas_call | solution.py:238
  53.0 3.7 %collective-permute-done.1.refs_2_ = bf16[2,272,1024]{2,1,0:T(8,128)(2,1)S(1)} collective-permute-done((bf16[2,272,1024]{2,1,0:T(8,128)(2,1)}, bf16[2,272,1024]{2,1,0:T(8,128)(2,1)S(1)}, u32[]{:S(2)}, u32[]{:S(2)}) %collective-permute-start.1) | collective-permute-done | bytes 1114144 | tf_op jit(solution)/shard_map/ppermute | solution.py:506
  57.1 2.7 %shard_map.48 = (s16[208,512]{1,0:T(8,128)(2,1)S(1)}, s16[208,512]{1,0:T(8,128)(2,1)S(1)}, s16[208,512]{1,0:T(8,128)(2,1)S(1)}, s16[208,512]{1,0:T(8,128)(2,1)S(1)}, f32[16,512]{1,0:T(8,128)S(1)}) custom-call(s32[3]{0:T(128)S(1)} %copy-done.1, bf16[3,512,1024]{2,1,0:T(8,128)(2,1)S(1)} %copy-done, bf16[3,512,1024]{2,1,0:T(8,128)(2,1)S(1)} %shard_map.47.refs_1_, ...), custom_call_target="tpu_custom_call" | custom-call | flops 1048576 | bytes 65536 | tf_op jit(solution)/shard_map/pallas_call | solution.py:183
  59.8 1.6 %collective-permute-start.8 = (s16[208,512]{1,0:T(8,128)(2,1)S(1)}, s16[208,512]{1,0:T(8,128)(2,1)S(1)}, u32[]{:S(2)}, u32[]{:S(2)}) collective-permute-start(s16[208,512]{1,0:T(8,128)(2,1)S(1)} %get-tuple-element.68), channel_id=1, source_target_pairs={{0,2},{1,3},{2,4},{3,5},{4,6},{5,7},{6,0},{7,1},{8,10},{9,11},{10,... | collective-permute-start | bytes 638984 | tf_op jit(solution)/shard_map/ppermute | solution.py:488
  61.5 2.9 %collective-permute-start.9 = (s16[208,512]{1,0:T(8,128)(2,1)S(1)}, s16[208,512]{1,0:T(8,128)(2,1)S(1)}, u32[]{:S(2)}, u32[]{:S(2)}) collective-permute-start(s16[208,512]{1,0:T(8,128)(2,1)S(1)} %get-tuple-element.69), channel_id=1, source_target_pairs={{0,4},{1,5},{2,6},{3,7},{4,0},{5,1},{6,2},{7,3},{8,12},{9,13},{10,... | collective-permute-start | bytes 638984 | tf_op jit(solution)/shard_map/ppermute | solution.py:488
  64.4 1.3 %collective-permute-start.10 = (s16[208,512]{1,0:T(8,128)(2,1)S(1)}, s16[208,512]{1,0:T(8,128)(2,1)S(1)}, u32[]{:S(2)}, u32[]{:S(2)}) collective-permute-start(s16[208,512]{1,0:T(8,128)(2,1)S(1)} %get-tuple-element.70), channel_id=1, source_target_pairs={{0,6},{1,7},{2,0},{3,1},{4,2},{5,3},{6,4},{7,5},{8,14},{9,15},{10,... | collective-permute-start | bytes 638984 | tf_op jit(solution)/shard_map/ppermute | solution.py:488
  65.7 1.4 %collective-permute-done.15.refs_2_ = s16[400,512]{1,0:T(8,128)(2,1)S(1)} collective-permute-done((s16[400,512]{1,0:T(8,128)(2,1)S(1)}, s16[400,512]{1,0:T(8,128)(2,1)S(1)}, u32[]{:S(2)}, u32[]{:S(2)}) %collective-permute-start.15) | collective-permute-done | bytes 409632 | tf_op jit(solution)/shard_map/ppermute | solution.py:488
  67.1 2.1 %shard_map.51 = (f32[3,4,64,512]{3,2,1,0:T(8,128)}, f32[3,4,64,512]{3,2,1,0:T(8,128)}, s16[272,512]{1,0:T(8,128)(2,1)S(1)}, s16[272,512]{1,0:T(8,128)(2,1)S(1)}) custom-call(s32[3]{0:T(128)S(1)} %copy-done.1, s16[400,512]{1,0:T(8,128)(2,1)S(1)} %get-tuple-element.59.refs_0_, ...), custom_call_target="tpu_custom_call", output_to_operand_aliasing={{0}: (7, {}), {1}: (8, {})} | custom-call | flops 1048576 | bytes 65536 | tf_op jit(solution)/shard_map/pallas_call | solution.py:378
  69.3 3.9 %collective-permute-start.17 = (s16[272,512]{1,0:T(8,128)(2,1)S(1)}, s16[272,512]{1,0:T(8,128)(2,1)S(1)}, u32[]{:S(2)}, u32[]{:S(2)}) collective-permute-start(s16[272,512]{1,0:T(8,128)(2,1)S(1)} %get-tuple-element.82), channel_id=1, source_target_pairs={{8,16},{16,8},{24,32},{32,24},{40,48},{48,40},{56,64},{64,56},{72,... | collective-permute-start | bytes 835592 | tf_op jit(solution)/shard_map/ppermute | solution.py:506
  73.3 2.5 %collective-permute-done.9.refs_2_ = s16[208,512]{1,0:T(8,128)(2,1)S(1)} collective-permute-done((s16[208,512]{1,0:T(8,128)(2,1)S(1)}, s16[208,512]{1,0:T(8,128)(2,1)S(1)}, u32[]{:S(2)}, u32[]{:S(2)}) %collective-permute-start.9) | collective-permute-done | bytes 213024 | tf_op jit(solution)/shard_map/ppermute | solution.py:488
  75.8 0.9 shard_map.49
  76.8 1.2 %collective-permute-done.11.other_ref = f32[64,256]{1,0:T(8,128)S(1)} collective-permute-done((f32[64,256]{1,0:T(8,128)S(1)}, f32[64,256]{1,0:T(8,128)S(1)}, u32[]{:S(2)}, u32[]{:S(2)}) %collective-permute-start.11) | collective-permute-done | bytes 65568 | tf_op jit(solution)/shard_map/ppermute | solution.py:481
  78.0 0.6 shard_map.50
  78.6 3.9 %collective-permute-start.12 = (s16[144,512]{1,0:T(8,128)(2,1)S(1)}, s16[144,512]{1,0:T(8,128)(2,1)S(1)}, u32[]{:S(2)}, u32[]{:S(2)}) collective-permute-start(s16[144,512]{1,0:T(8,128)(2,1)S(1)} %get-tuple-element.75), channel_id=1, source_target_pairs={{8,16},{16,8},{24,32},{32,24},{40,48},{48,40},{56,64},{64,56},{72,... | collective-permute-start | bytes 442376 | tf_op jit(solution)/shard_map/ppermute | solution.py:506
  82.6 1.7 %shard_map.52 = (f32[3,4,64,512]{3,2,1,0:T(8,128)}, f32[3,4,64,512]{3,2,1,0:T(8,128)}) custom-call(s32[3]{0:T(128)S(1)} %copy-done.1, s16[272,512]{1,0:T(8,128)(2,1)S(1)} %collective-permute-done.17.first_ref, s16[272,512]{1,0:T(8,128)(2,1)S(1)} %collective-permute-done.18.second_ref, ...), custom_call_target="tpu_custom_call", output_to_operand_aliasing={{0}: (5, {}), {1}: (6, {})} | custom-call | flops 1048576 | bytes 65536 | tf_op jit(solution)/shard_map/pallas_call | solution.py:427
  84.3 4.2 %collective-permute-done.12.first_ref = s16[144,512]{1,0:T(8,128)(2,1)S(1)} collective-permute-done((s16[144,512]{1,0:T(8,128)(2,1)S(1)}, s16[144,512]{1,0:T(8,128)(2,1)S(1)}, u32[]{:S(2)}, u32[]{:S(2)}) %collective-permute-start.12) | collective-permute-done | bytes 147488 | tf_op jit(solution)/shard_map/ppermute | solution.py:506
  88.5 1.3 %shard_map.53 = (f32[3,4,64,512]{3,2,1,0:T(8,128)}, f32[3,4,64,512]{3,2,1,0:T(8,128)}) custom-call(s32[3]{0:T(128)S(1)} %copy-done.1, s16[144,512]{1,0:T(8,128)(2,1)S(1)} %collective-permute-done.12.first_ref, s16[144,512]{1,0:T(8,128)(2,1)S(1)} %collective-permute-done.13.second_ref, ...), custom_call_target="tpu_custom_call", output_to_operand_aliasing={{0}: (3, {}), {1}: (4, {})} | custom-call | flops 1048576 | bytes 65536 | tf_op jit(solution)/shard_map/pallas_call | solution.py:427
  (28 shorter events, 3.0 us)
Async XLA Ops:
  0.6 8.1 %collective-permute-start = (bf16[3,512,1024]{2,1,0:T(8,128)(2,1)}, bf16[3,512,1024]{2,1,0:T(8,128)(2,1)}, u32[]{:S(2)}, u32[]{:S(2)}) collective-permute-start(bf16[3,512,1024]{2,1,0:T(8,128)(2,1)} %refs_0_.5), channel_id=1, source_target_pairs={{0,1},{1,0},{2,3},{3,2},{4,5},{5,4},{6,7},{7,6},{8,9},{9,8},{10,11... | collective-permute-start | bytes 9437192 | tf_op jit(solution)/shard_map/ppermute | solution.py:481
  3.1 30.3 %collective-permute-start.3 = (bf16[1,512,1024]{2,1,0:T(8,128)(2,1)}, bf16[1,512,1024]{2,1,0:T(8,128)(2,1)}, u32[]{:S(2)}, u32[]{:S(2)}) collective-permute-start(bf16[1,512,1024]{2,1,0:T(8,128)(2,1)} %get-tuple-element.49), channel_id=1, source_target_pairs={{8,16},{16,8},{24,32},{32,24},{40,48},{48,40},{56,64},{64,56},{72,... | collective-permute-start | bytes 3145736 | tf_op jit(solution)/shard_map/ppermute | solution.py:506
  7.7 26.4 %collective-permute-start.4 = (bf16[1,512,1024]{2,1,0:T(8,128)(2,1)}, bf16[1,512,1024]{2,1,0:T(8,128)(2,1)}, u32[]{:S(2)}, u32[]{:S(2)}) collective-permute-start(bf16[1,512,1024]{2,1,0:T(8,128)(2,1)} %get-tuple-element.50), channel_id=1, source_target_pairs={{0,8},{8,0},{16,24},{24,16},{32,40},{40,32},{48,56},{56,48},{64,72... | collective-permute-start | bytes 3145736 | tf_op jit(solution)/shard_map/ppermute | solution.py:506
  14.7 19.4 %copy-start.1 = (s32[3]{0:T(128)S(1)}, s32[3]{0:T(128)}, u32[]{:S(2)}) copy-start(s32[3]{0:T(128)} %pad_add_fusion.place_ref) | copy-start | bytes 40
  14.7 19.4 %all-to-all-start = ((s16[4,208,512]{2,1,0:T(8,128)(2,1)}), s16[4,208,512]{2,1,0:T(8,128)(2,1)S(1)}, u32[]{:S(2)}, u32[]{:S(2)}) async-start(s16[4,208,512]{2,1,0:T(8,128)(2,1)} %get-tuple-element.51), calls=%async_computation | async-start | bytes 1703936 | tf_op jit(solution)/shard_map/all_to_all | solution.py:493
  19.3 37.5 %collective-permute-start.1 = (bf16[2,272,1024]{2,1,0:T(8,128)(2,1)}, bf16[2,272,1024]{2,1,0:T(8,128)(2,1)S(1)}, u32[]{:S(2)}, u32[]{:S(2)}) collective-permute-start(bf16[2,272,1024]{2,1,0:T(8,128)(2,1)} %get-tuple-element.47), channel_id=1, source_target_pairs={{8,16},{16,8},{24,32},{32,24},{40,48},{48,40},{56,64},{64,56},{72,... | collective-permute-start | bytes 3342344 | tf_op jit(solution)/shard_map/ppermute | solution.py:506
  22.4 34.7 %collective-permute-start.2 = (bf16[2,272,1024]{2,1,0:T(8,128)(2,1)}, bf16[2,272,1024]{2,1,0:T(8,128)(2,1)S(1)}, u32[]{:S(2)}, u32[]{:S(2)}) collective-permute-start(bf16[2,272,1024]{2,1,0:T(8,128)(2,1)} %get-tuple-element.48), channel_id=1, source_target_pairs={{0,8},{8,0},{16,24},{24,16},{32,40},{40,32},{48,56},{56,48},{64,72... | collective-permute-start | bytes 3342344 | tf_op jit(solution)/shard_map/ppermute | solution.py:506
  35.8 2.7 %collective-permute-start.7 = (bf16[1,256,1024]{2,1,0:T(8,128)(2,1)S(1)}, bf16[1,256,1024]{2,1,0:T(8,128)(2,1)S(1)}, u32[]{:S(2)}, u32[]{:S(2)}) collective-permute-start(bf16[1,256,1024]{2,1,0:T(8,128)(2,1)S(1)} %get-tuple-element.58), channel_id=1, source_target_pairs={{0,1},{1,0},{2,3},{3,2},{4,5},{5,4},{6,7},{7,6},{8,9},{9,8},{10,11... | collective-permute-start | bytes 1572872 | tf_op jit(solution)/shard_map/ppermute | solution.py:481
  35.9 2.7 %collective-permute-start.6 = (bf16[1,256,1024]{2,1,0:T(8,128)(2,1)S(1)}, bf16[1,256,1024]{2,1,0:T(8,128)(2,1)S(1)}, u32[]{:S(2)}, u32[]{:S(2)}) collective-permute-start(bf16[1,256,1024]{2,1,0:T(8,128)(2,1)S(1)} %get-tuple-element.56.refs_3_), channel_id=1, source_target_pairs={{0,1},{1,0},{2,3},{3,2},{4,5},{5,4},{6,7},{7,6},{8,9},{9,8},{10,11... | collective-permute-start | bytes 1572872 | tf_op jit(solution)/shard_map/ppermute | solution.py:481
  36.4 2.9 %collective-permute-start.5 = (bf16[1,256,1024]{2,1,0:T(8,128)(2,1)S(1)}, bf16[1,256,1024]{2,1,0:T(8,128)(2,1)S(1)}, u32[]{:S(2)}, u32[]{:S(2)}) collective-permute-start(bf16[1,256,1024]{2,1,0:T(8,128)(2,1)S(1)} %get-tuple-element.54.refs_2_), channel_id=1, source_target_pairs={{0,1},{1,0},{2,3},{3,2},{4,5},{5,4},{6,7},{7,6},{8,9},{9,8},{10,11... | collective-permute-start | bytes 1572872 | tf_op jit(solution)/shard_map/ppermute | solution.py:481
  36.4 2.8 %copy-start = (bf16[3,512,1024]{2,1,0:T(8,128)(2,1)S(1)}, bf16[3,512,1024]{2,1,0:T(8,128)(2,1)}, u32[]{:S(2)}) copy-start(bf16[3,512,1024]{2,1,0:T(8,128)(2,1)} %refs_0_.5) | copy-start | bytes 9437188
  39.3 10.1 %copy-start.2 = (s32[3,4]{1,0:T(4,128)S(1)}, s32[3,4]{1,0:T(4,128)}, u32[]{:S(2)}) copy-start(s32[3,4]{1,0:T(4,128)} %refs_4_.3) | copy-start | bytes 148
  43.5 20.9 %collective-permute-start.14 = (s16[400,512]{1,0:T(8,128)(2,1)S(1)}, s16[400,512]{1,0:T(8,128)(2,1)S(1)}, u32[]{:S(2)}, u32[]{:S(2)}) collective-permute-start(s16[400,512]{1,0:T(8,128)(2,1)S(1)} %get-tuple-element.77), channel_id=1, source_target_pairs={{0,2},{1,3},{2,4},{3,5},{4,6},{5,7},{6,0},{7,1},{8,10},{9,11},{10,... | collective-permute-start | bytes 1228808 | tf_op jit(solution)/shard_map/ppermute | solution.py:488
  45.2 22.0 %collective-permute-start.15 = (s16[400,512]{1,0:T(8,128)(2,1)S(1)}, s16[400,512]{1,0:T(8,128)(2,1)S(1)}, u32[]{:S(2)}, u32[]{:S(2)}) collective-permute-start(s16[400,512]{1,0:T(8,128)(2,1)S(1)} %get-tuple-element.78), channel_id=1, source_target_pairs={{0,4},{1,5},{2,6},{3,7},{4,0},{5,1},{6,2},{7,3},{8,12},{9,13},{10,... | collective-permute-start | bytes 1228808 | tf_op jit(solution)/shard_map/ppermute | solution.py:488
  48.1 19.1 %collective-permute-start.16 = (s16[400,512]{1,0:T(8,128)(2,1)S(1)}, s16[400,512]{1,0:T(8,128)(2,1)S(1)}, u32[]{:S(2)}, u32[]{:S(2)}) collective-permute-start(s16[400,512]{1,0:T(8,128)(2,1)S(1)} %get-tuple-element.79), channel_id=1, source_target_pairs={{0,6},{1,7},{2,0},{3,1},{4,2},{5,3},{6,4},{7,5},{8,14},{9,15},{10,... | collective-permute-start | bytes 1228808 | tf_op jit(solution)/shard_map/ppermute | solution.py:488
  59.8 13.4 %collective-permute-start.8 = (s16[208,512]{1,0:T(8,128)(2,1)S(1)}, s16[208,512]{1,0:T(8,128)(2,1)S(1)}, u32[]{:S(2)}, u32[]{:S(2)}) collective-permute-start(s16[208,512]{1,0:T(8,128)(2,1)S(1)} %get-tuple-element.68), channel_id=1, source_target_pairs={{0,2},{1,3},{2,4},{3,5},{4,6},{5,7},{6,0},{7,1},{8,10},{9,11},{10,... | collective-permute-start | bytes 638984 | tf_op jit(solution)/shard_map/ppermute | solution.py:488
  61.5 14.3 %collective-permute-start.9 = (s16[208,512]{1,0:T(8,128)(2,1)S(1)}, s16[208,512]{1,0:T(8,128)(2,1)S(1)}, u32[]{:S(2)}, u32[]{:S(2)}) collective-permute-start(s16[208,512]{1,0:T(8,128)(2,1)S(1)} %get-tuple-element.69), channel_id=1, source_target_pairs={{0,4},{1,5},{2,6},{3,7},{4,0},{5,1},{6,2},{7,3},{8,12},{9,13},{10,... | collective-permute-start | bytes 638984 | tf_op jit(solution)/shard_map/ppermute | solution.py:488
  64.4 11.4 %collective-permute-start.10 = (s16[208,512]{1,0:T(8,128)(2,1)S(1)}, s16[208,512]{1,0:T(8,128)(2,1)S(1)}, u32[]{:S(2)}, u32[]{:S(2)}) collective-permute-start(s16[208,512]{1,0:T(8,128)(2,1)S(1)} %get-tuple-element.70), channel_id=1, source_target_pairs={{0,6},{1,7},{2,0},{3,1},{4,2},{5,3},{6,4},{7,5},{8,14},{9,15},{10,... | collective-permute-start | bytes 638984 | tf_op jit(solution)/shard_map/ppermute | solution.py:488
  69.3 13.4 %collective-permute-start.17 = (s16[272,512]{1,0:T(8,128)(2,1)S(1)}, s16[272,512]{1,0:T(8,128)(2,1)S(1)}, u32[]{:S(2)}, u32[]{:S(2)}) collective-permute-start(s16[272,512]{1,0:T(8,128)(2,1)S(1)} %get-tuple-element.82), channel_id=1, source_target_pairs={{8,16},{16,8},{24,32},{32,24},{40,48},{48,40},{56,64},{64,56},{72,... | collective-permute-start | bytes 835592 | tf_op jit(solution)/shard_map/ppermute | solution.py:506
  73.2 9.5 %collective-permute-start.18 = (s16[272,512]{1,0:T(8,128)(2,1)S(1)}, s16[272,512]{1,0:T(8,128)(2,1)S(1)}, u32[]{:S(2)}, u32[]{:S(2)}) collective-permute-start(s16[272,512]{1,0:T(8,128)(2,1)S(1)} %get-tuple-element.83), channel_id=1, source_target_pairs={{0,8},{8,0},{16,24},{24,16},{32,40},{40,32},{48,56},{56,48},{64,72... | collective-permute-start | bytes 835592 | tf_op jit(solution)/shard_map/ppermute | solution.py:506
  76.7 1.3 %collective-permute-start.11 = (f32[64,256]{1,0:T(8,128)S(1)}, f32[64,256]{1,0:T(8,128)S(1)}, u32[]{:S(2)}, u32[]{:S(2)}) collective-permute-start(f32[64,256]{1,0:T(8,128)S(1)} %get-tuple-element.73), channel_id=1, source_target_pairs={{0,1},{1,0},{2,3},{3,2},{4,5},{5,4},{6,7},{7,6},{8,9},{9,8},{10,11... | collective-permute-start | bytes 196616 | tf_op jit(solution)/shard_map/ppermute | solution.py:481
  78.6 9.9 %collective-permute-start.12 = (s16[144,512]{1,0:T(8,128)(2,1)S(1)}, s16[144,512]{1,0:T(8,128)(2,1)S(1)}, u32[]{:S(2)}, u32[]{:S(2)}) collective-permute-start(s16[144,512]{1,0:T(8,128)(2,1)S(1)} %get-tuple-element.75), channel_id=1, source_target_pairs={{8,16},{16,8},{24,32},{32,24},{40,48},{48,40},{56,64},{64,56},{72,... | collective-permute-start | bytes 442376 | tf_op jit(solution)/shard_map/ppermute | solution.py:506
  82.5 6.0 %collective-permute-start.13 = (s16[144,512]{1,0:T(8,128)(2,1)S(1)}, s16[144,512]{1,0:T(8,128)(2,1)S(1)}, u32[]{:S(2)}, u32[]{:S(2)}) collective-permute-start(s16[144,512]{1,0:T(8,128)(2,1)S(1)} %get-tuple-element.76), channel_id=1, source_target_pairs={{0,8},{8,0},{16,24},{24,16},{32,40},{40,32},{48,56},{56,48},{64,72... | collective-permute-start | bytes 442376 | tf_op jit(solution)/shard_map/ppermute | solution.py:506

commit v5 on v4

--- a/solution.py
+++ b/solution.py
@@ -22,6 +22,11 @@
 PARAMS = pltpu.CompilerParams(vmem_limit_bytes=18 << 20)
 FAR = pltpu.CompilerParams(vmem_limit_bytes=62 << 20)
 OUTS = [jax.ShapeDtypeStruct((3, 4, SLICE, BF), jnp.float32)] * 2
+
+
+def here():
+    member = lax.axis_index("occ")
+    return member & 1, member >> 1, lax.axis_index("space") & 1
 
 
 def coded_rows(count):
@@ -48,12 +53,13 @@
     return jnp.exp(rows.astype(jnp.float32) * (LN2 / STEPS))
 
 
-def pair_kernel(pairs, blocks, halved, names, together, late, with_second, place_ref, *refs):
+def pair_kernel(pairs, blocks, halved, names, together, late, with_second, *refs):
+    place = here()
     ins = dict(zip(names, refs))
     outs = refs[len(names) :]
     if with_second:
         outs, mask_ref, second = outs[1:-2], outs[0], outs[-2:]
-        put_second(place_ref, mask_ref, (ins["own"], ins["sib"]), *second)
+        put_second(place, mask_ref, (ins["own"], ins["sib"]), *second)
     if late:
         *outs, lines_ref = outs
         first_ref, second_ref = ins["first"], ins["second"]
@@ -61,24 +67,24 @@
         def work(low_ref, high_ref):
             ins.update({"low2": low_ref, "high2": high_ref})
             lines_ref[...] = low_ref[0, HALF : HALF + 16, :BF].astype(jnp.float32)
-            pair_work(pairs, blocks, halved, ins, outs, together, place_ref)
-
-        @pl.when(place_ref[2] == 1)
+            pair_work(pairs, blocks, halved, ins, outs, together, place)
+
+        @pl.when(place[2] == 1)
         def _():
             work(second_ref, first_ref)
 
-        @pl.when(place_ref[2] == 0)
+        @pl.when(place[2] == 0)
         def _():
             work(first_ref, second_ref)
 
         return
-    pair_work(pairs, blocks, halved, ins, outs, together, place_ref)
-
-
-def pair_work(pairs, blocks, halved, ins, outs, together, place_ref):
+    pair_work(pairs, blocks, halved, ins, outs, together, place)
+
+
+def pair_work(pairs, blocks, halved, ins, outs, together, place):
     if together:
         outs = [outs[0].at[d] for d in range(CHIPS)]
-    core, chip = place_ref[0], place_ref[1]
+    core, chip = place[0], place[1]
     order = [d if together else (chip + d) % CHIPS for d in range(CHIPS)]
 
     def read(piece, start, rows):
@@ -132,16 +138,29 @@
         else:
             parts = [acc[d * SLICE : (d + 1) * SLICE] for d in range(CHIPS)]
         coded, level = code(parts)
+        if shared:
+            for k in range(2):
+
+                @pl.when(core == k)
+                def _():
+                    for d in range(CHIPS):
+                        row = level_rows([level[d : d + 1]])
+                        for ref, j in zip(outs[CHIPS:], (k, 1 - k)):
+                            lanes = slice(j * HALF, (j + 1) * HALF)
+                            ref[d, :SLICE, :] = coded[d][:, lanes]
+                            ref[d, SLICE:, :] = row[:, lanes]
+
+            continue
         for d in range(CHIPS):
             outs[d][p * SLICE : (p + 1) * SLICE, :] = coded[d]
         levels.append(level)
-    end = len(pairs) * SLICE
+    end = len(levels) * SLICE
     for d in range(CHIPS):
         outs[d][end : end + 16, :] = level_rows([v[d : d + 1] for v in levels])
 
 
-def put_second(place_ref, mask_ref, sources, first_ref, second_ref):
-    core = place_ref[0]
+def put_second(place, mask_ref, sources, first_ref, second_ref):
+    core = place[0]
     lines = [
         jnp.full((1, COLS), mask_ref[k // 4, k % 4].astype(jnp.float32), jnp.float32)
         for k in range(12)
@@ -159,22 +178,23 @@
                 ]
             down_ref[i, HALF:, :] = lines
 
-    @pl.when(place_ref[2] == 1)
+    @pl.when(place[2] == 1)
     def _():
         put(first_ref, second_ref)
 
-    @pl.when(place_ref[2] == 0)
+    @pl.when(place[2] == 0)
     def _():
         put(second_ref, first_ref)
 
 
-def pair_products(place, pairs, blocks, operands, halved=(), together=False, late=False, mask=None):
+def pair_products(pairs, blocks, operands, halved=(), together=False, late=False, mask=None):
     names = list(operands)
-    n = len(pairs)
-    rows = coded_rows(n)
+    rows = coded_rows(len(pairs) - len(halved))
     shapes = [jax.ShapeDtypeStruct((rows, BF), jnp.int16)] * CHIPS
     if together:
         shapes = [jax.ShapeDtypeStruct((CHIPS, rows, BF), jnp.int16)]
+    if halved:
+        shapes += [jax.ShapeDtypeStruct((CHIPS, SLICE + 16, HALF), jnp.int16)] * 2
     if late:
         shapes.append(jax.ShapeDtypeStruct((16, BF), jnp.float32))
     second = mask is not None
@@ -183,11 +203,43 @@
     return pl.pallas_call(
         functools.partial(pair_kernel, pairs, blocks, halved, names, together, late, second),
         out_shape=shapes,
-        in_specs=[SMEM] + [VMEM] * len(names) + [SMEM] * second,
+        in_specs=[VMEM] * len(names) + [SMEM] * second,
         out_specs=[VMEM] * len(shapes),
         compiler_params=FAR if together else PARAMS,
         cost_estimate=pl.CostEstimate(flops=1 << 20, bytes_accessed=1 << 16, transcendentals=0),
-    )(place, *operands.values(), *([mask] if second else []))
+    )(*operands.values(), *([mask] if second else []))
+
+
+def whole_kernel(*refs):
+    place = here()
+    coded, (mine_ref, other_ref), outs = refs[:CHIPS], refs[CHIPS : CHIPS + 2], refs[CHIPS + 2 :]
+    for d in range(CHIPS):
+        end = coded[d].shape[0] - 16
+        outs[d][:end, :] = coded[d][:end, :]
+        levels = coded[d][end : end + 16, :].astype(jnp.int32)
+        for k in range(2):
+
+            @pl.when(place[0] == k)
+            def _():
+                refs = (mine_ref, other_ref) if k == 0 else (other_ref, mine_ref)
+                block = jnp.concatenate([ref[d, :SLICE, :] for ref in refs], 1)
+                outs[d][end : end + SLICE, :] = block
+                row = [ref[d, SLICE:, :].astype(jnp.int32)[:1] for ref in refs]
+                rows = [levels[i : i + 1] for i in range(end // SLICE)]
+                rows.append(jnp.concatenate(row, 1))
+                outs[d][end + SLICE :, :] = level_rows(rows)
+
+
+def whole(coded, mine, other):
+    rows = coded[0].shape[0] + SLICE
+    return pl.pallas_call(
+        whole_kernel,
+        out_shape=[jax.ShapeDtypeStruct((rows, BF), jnp.int16)] * CHIPS,
+        in_specs=[VMEM] * (CHIPS + 2),
+        out_specs=[VMEM] * CHIPS,
+        compiler_params=PARAMS,
+        cost_estimate=pl.CostEstimate(flops=1 << 10, bytes_accessed=1 << 10, transcendentals=0),
+    )(*coded, mine, other)
 
 
 def first_kernel(own_ref, first_ref, second_ref, held, sems):
@@ -246,36 +298,38 @@
     )(value)
 
 
-def arrived_kernel(place_ref, first_ref, second_ref, low_a_ref, low_b_ref, mine_ref, other_ref):
+def arrived_kernel(first_ref, second_ref, low_a_ref, low_b_ref, mine_ref, other_ref):
+    place = here()
+
     def put(low_ref, high_ref):
         low_a_ref[0] = low_ref[0, :HALF, :]
         low_b_ref[0] = low_ref[0, HALF:, :]
-        for core, target in ((place_ref[0], mine_ref), (1 - place_ref[0], other_ref)):
+        for core, target in ((place[0], mine_ref), (1 - place[0], other_ref)):
             for y in range(CHIPS):
                 start = (2 * y + core) * SLICE
                 target[0, y * SLICE : (y + 1) * SLICE, :] = high_ref[0, pl.ds(start, SLICE), :]
 
-    @pl.when(place_ref[2] == 1)
+    @pl.when(place[2] == 1)
     def _():
         put(second_ref, first_ref)
 
-    @pl.when(place_ref[2] == 0)
+    @pl.when(place[2] == 0)
     def _():
         put(first_ref, second_ref)
 
 
-def arrived(place, first, second):
+def arrived(first, second):
     return pl.pallas_call(
         arrived_kernel,
         out_shape=[jax.ShapeDtypeStruct((1, HALF, COLS), jnp.bfloat16)] * 4,
-        in_specs=[SMEM, VMEM, VMEM],
+        in_specs=[VMEM, VMEM],
         out_specs=[VMEM] * 4,
         compiler_params=PARAMS,
         cost_estimate=pl.CostEstimate(flops=1 << 10, bytes_accessed=1 << 10, transcendentals=0),
-    )(place, first, second)
-
-
-def put_messages(place_ref, refs, held):
+    )(first, second)
+
+
+def put_messages(place, refs, held):
     def put(refs):
         for ref, blocks in zip(refs, held):
             for k, (coded, _) in enumerate(blocks):
@@ -287,24 +341,25 @@
         put(refs)
         return
 
-    @pl.when(place_ref[2] == 1)
+    @pl.when(place[2] == 1)
     def _():
         put(refs)
 
-    @pl.when(place_ref[2] == 0)
+    @pl.when(place[2] == 0)
     def _():
         put(refs[::-1])
 
 
-def add_kernel(places, first, sizes, halves, n_gots, lined, place_ref, *refs):
+def add_kernel(places, first, sizes, keep, n_gots, lined, *refs):
+    place = here()
     gots, refs = refs[:n_gots], refs[n_gots:]
     if n_gots == 1:
         gots = [gots[0].at[d] for d in range(CHIPS)]
     mask_ref, refs = refs[0], refs[1:]
     if lined:
         lines_ref, refs = refs[0], refs[1:]
-    if halves:
-        messages, (sums, kept_ref, swap_ref) = refs[: len(sizes)], refs[len(sizes) :]
+    if keep:
+        messages, sums = refs[: len(sizes)], refs[len(sizes)]
     else:
         if not first:
             refs = refs[2:]
@@ -333,17 +388,12 @@
                     (coded,), level = code([total])
                 assert index == len(held[which])
                 held[which].append((coded, level))
-            elif kind == "halves":
-                first_core = place_ref[0] == 0
-                low, high = total[:, :HALF], total[:, HALF:]
-                kept_ref[...] = jnp.where(first_core, low, high)
-                swap_ref[...] = jnp.where(first_core, high, low)
             elif kind == "kept":
                 sums[goal[0]] = total
             else:
                 sums[p] = total
                 writes.append((p, (f_ref if kind == "f" else b_ref).at[goal[0], goal[1]]))
-    put_messages(place_ref, messages, held)
+    put_messages(place, messages, held)
     writes = [
         pltpu.make_async_copy(sums.at[p], target, sems.at[k])
         for k, (p, target) in enumerate(writes)
@@ -354,15 +404,14 @@
         copy.wait()
 
 
-def add_parts(place, gots, masks, outs, places, sizes=(), kept=None):
+def add_parts(gots, masks, outs, places, sizes=(), kept=None):
     n = len(places)
-    ins = [place, *gots, *masks]
+    ins = [*gots, *masks]
     messages = [jax.ShapeDtypeStruct((coded_rows(max(sizes, default=0)), BF), jnp.int16)] * len(sizes)
-    in_specs = [SMEM] + [VMEM] * len(gots) + [SMEM, VMEM][: len(masks)]
+    in_specs = [VMEM] * len(gots) + [SMEM, VMEM][: len(masks)]
     scratch, aliases = [], {}
     if kept is not None:
         shapes = messages + [jax.ShapeDtypeStruct((kept, SLICE, BF), jnp.float32)]
-        shapes += [jax.ShapeDtypeStruct((SLICE, HALF), jnp.float32)] * 2
         out_specs = [VMEM] * len(shapes)
     else:
         shapes = OUTS + messages
@@ -387,10 +436,10 @@
     )(*ins)
 
 
-def place_kernel(below_places, above_places, block_places, n, place_ref, first_ref, second_ref, *refs):
+def place_kernel(below_places, above_places, block_places, n, first_ref, second_ref, *refs):
     blocks, refs = refs[:n], refs[n + 2 :]
     f_ref, b_ref, sums, sems = refs
-    odd = place_ref[2] == 1
+    odd = here()[2] == 1
     end = first_ref.shape[0] - 16
     scales = [scales_of(ref[end : end + 16, :]) for ref in (first_ref, second_ref)]
     writes = []
@@ -421,13 +470,13 @@
         copy.wait()
 
 
-def place_results(place, first, second, outs, below_places, above_places, blocks=(), block_places=()):
+def place_results(first, second, outs, below_places, above_places, blocks=(), block_places=()):
     total = len(below_places) + len(above_places)
-    n = 3 + len(blocks)
+    n = 2 + len(blocks)
     return pl.pallas_call(
         functools.partial(place_kernel, below_places, above_places, block_places, len(blocks)),
         out_shape=OUTS,
-        in_specs=[SMEM] + [VMEM] * (n - 1) + [HBM] * 2,
+        in_specs=[VMEM] * n + [HBM] * 2,
         out_specs=[HBM] * 2,
         scratch_shapes=[
             pltpu.VMEM((total, SLICE, BF), jnp.float32),
@@ -436,45 +485,7 @@
         input_output_aliases={n: 0, n + 1: 1},
         compiler_params=PARAMS,
         cost_estimate=pl.CostEstimate(flops=1 << 20, bytes_accessed=1 << 16, transcendentals=0),
-    )(place, first, second, *blocks, *outs)
-
-
-def join_kernel(place_ref, mine_ref, other_ref, up_ref, block_ref, *refs):
-    first_core = place_ref[0] == 0
-    mine, other = mine_ref[...], other_ref[...]
-    low, high = jnp.where(first_core, mine, other), jnp.where(first_core, other, mine)
-    total = jnp.concatenate([low, high], 1)
-    block_ref[...] = total
-    (coded,), level = code([total])
-
-    def put(up_to, down_to):
-        up_to[...] = up_ref[...]
-        end = down_to.shape[0] - 16
-        down_to[:SLICE, :] = coded
-        down_to[end:, :] = level_rows([level])
-
-    @pl.when(place_ref[2] == 1)
-    def _():
-        put(*refs)
-
-    @pl.when(place_ref[2] == 0)
-    def _():
-        put(*refs[::-1])
-
-
-def join_halves(place, mine, other, up):
-    return pl.pallas_call(
-        join_kernel,
-        out_shape=[
-            jax.ShapeDtypeStruct((SLICE, BF), jnp.float32),
-            jax.ShapeDtypeStruct(up.shape, jnp.int16),
-            jax.ShapeDtypeStruct(up.shape, jnp.int16),
-        ],
-        in_specs=[SMEM, VMEM, VMEM, VMEM],
-        out_specs=[VMEM] * 3,
-        compiler_params=PARAMS,
-        cost_estimate=pl.CostEstimate(flops=1 << 10, bytes_accessed=1 << 10, transcendentals=0),
-    )(place, mine, other, up)
+    )(first, second, *blocks, *outs)
 
 
 def swap(value):
@@ -508,25 +519,22 @@
 
 
 def on_device(own, mask):
-    index = lax.axis_index("occ")
-    place = jnp.stack([index % 2, index // 2, lax.axis_index("space") % 2]).astype(jnp.int32)
     own_sib = swap(own)
     first, second = pairwise(*first_factors(own))
     mine = {"own": own, "sib": own_sib}
     blocks = {k: ([("own", k)], [("sib", k)]) for k in range(3)}
     coded0, first2, second2 = pair_products(
-        place, [(0, 1), (0, 2), (1, 2)], blocks, mine, together=True, mask=mask
+        [(0, 1), (0, 2), (1, 2)], blocks, mine, together=True, mask=mask
     )
     first2, second2 = pairwise(first2, second2)
     got0 = [across(coded0)]
     first, second, got0 = lax.optimization_barrier((first, second, got0))
-    low_a, low_b, high, other = arrived(place, first, second)
+    low_a, low_b, high, other = arrived(first, second)
     low_as, low_bs, high_sib = swap((low_a, low_b, other))
     blocks["L"] = [("low_a", 0), ("low_b", 0)], [("low_as", 0), ("low_bs", 0)]
     blocks["H"] = [("high", 0)], [("high_sib", 0)]
     near, _ = lax.optimization_barrier((own_sib, low_a))
     coded1 = pair_products(
-        place,
         [("L", 0), ("L", 1), ("L", 2), (0, "H"), (1, "H"), ("L", "H")],
         blocks,
         {"own": own, "sib": bring(near)}
@@ -535,7 +543,6 @@
     )
     got1 = to_chips(coded1)
     outs = add_parts(
-        place,
         got0,
         [mask],
         None,
@@ -550,17 +557,16 @@
     first2, second2, _, outs, near = lax.optimization_barrier((first2, second2, coded1[0], outs, near))
     blocks["H2"] = [("high2", 0)], [("high2", 1)]
     blocks["L2"] = [("low2", 0)], [("low2", 1)]
-    *coded2, lines = pair_products(
-        place,
+    *coded2, mine_half, other_half, lines = pair_products(
         [(0, "H2"), (1, "H2"), ("L2", 2)],
         blocks,
         {"own": own, "sib": near} | {"first": first2, "second": second2},
         halved=("L2",),
         late=True,
     )
+    coded2 = whole(coded2, mine_half, swap(other_half))
     got2 = to_chips(coded2)
     *outs, up1, down1 = add_parts(
-        place,
         got1,
         [mask, lines],
         outs,
@@ -575,33 +581,30 @@
         (3, 4),
     )
     first3, second3 = pairwise(up1, down1)
-    up2, kept, mine_half, other_half = add_parts(
-        place,
+    up2, down2, kept = add_parts(
         got2,
         [mask, lines],
         None,
         [
             ((0, 0, 3), [("kept", 0), ("m", 0, 0)]),
             ((0, 1, 2), [("kept", 1), ("m", 0, 1)]),
-            ((1, 1, 3), [("halves",)]),
+            ((1, 1, 3), [("kept", 2), ("m", 1, 0)]),
         ],
-        (2,),
-        kept=2,
-    )
-    block, first4, second4 = join_halves(place, mine_half, swap(other_half), up2)
-    first4, second4 = pairwise(first4, second4)
+        (2, 1),
+        kept=3,
+    )
+    first4, second4 = pairwise(up2, down2)
     outs = place_results(
-        place,
         first3,
         second3,
         outs,
         [("b", 0, 2), ("b", 0, 1), ("b", 0, 3)],
         [("f", 2, 0), ("f", 2, 1), ("f", 2, 2), ("f", 2, 3)],
-        [block, kept],
-        [("b", 2, 3), ("f", 0, 3), ("f", 1, 2)],
+        [kept],
+        [("f", 0, 3), ("f", 1, 2), ("b", 2, 3)],
     )
     forward, backward = place_results(
-        place, first4, second4, outs, [("b", 1, 3), ("b", 1, 2)], [("f", 1, 3)]
+        first4, second4, outs, [("b", 1, 3), ("b", 1, 2)], [("f", 1, 3)]
     )
     return jnp.swapaxes(forward, 2, 3), backward
 

time: 90.4 us -> 86.8 us (0.960)
  Pallas kernels: 29.3 us -> 26.5 us
    ppermute x6, waiting for transfers between devices: 3.95 us -> 2.05 us  [chips_on(): return lax.ppermute(value, 'occ', pairs)]
    pallas_call x3, Pallas kernels: 12.9 us -> 11.8 us  [pair_products(): pl.pallas_call(functools.partial(pair_kernel, pairs, blocks, halved, name...]
    pallas_call x2, Pallas kernels: 3.02 us -> 1.93 us  [place_results(): pl.pallas_call(functools.partial(place_kernel, below_places, above_places...]
    ppermute x8, waiting for transfers between devices: 19.4 us -> 20.5 us  [pairwise(): done.append(lax.ppermute(value, 'space', sorted(pairs)))]
  transfers between devices with their start and end apart: 20 -> 20, of which waited for: 9 -> 10; matrix products, arithmetic and copies ran while one was open for 1% -> 0% of each run, Pallas kernels for 31% -> 30%
where the time goes in v5:
time: 86.8 us; the launch traced here: 86.5 us
  starting transfers between devices  34.3 us (40%)
  Pallas kernels  26.5 us (31%)
  waiting for transfers between devices  24.6 us (28%)
  between operations  0.98 us (1%)
    ppermute x8, waiting for transfers between devices, pairwise(): done.append(lax.ppermute(value, 'space', sorted(pairs)))  20.5 us
    ppermute x8, starting transfers between devices, pairwise(): done.append(lax.ppermute(value, 'space', sorted(pairs)))  17.2 us
    pallas_call x3, Pallas kernels, pair_products(): pl.pallas_call(functools.partial(pair_kernel, pairs, blocks, halved, name...  11.8 us
    ppermute x6, starting transfers between devices, chips_on(): return lax.ppermute(value, 'occ', pairs)  11.8 us
    pallas_call x3, Pallas kernels, add_parts(): pl.pallas_call(kernel, out_shape=shapes, in_specs=in_specs, out_specs=out...  4.69 us
    all_to_all x1, starting transfers between devices, across(): return lax.all_to_all(value, 'occ', 0, 0, axis_index_groups=groups)  4.47 us
    pallas_call x2, Pallas kernels, bring(): pl.pallas_call(bring_kernel, out_shape=jax.ShapeDtypeStruct(value.shape,...  3.95 us
    pallas_call x1, Pallas kernels, first_factors(): pl.pallas_call(first_kernel, out_shape=[jax.ShapeDtypeStruct((1, BF, COLS...  2.41 us
  transfers between devices with their start and end apart: 20, of which 10 were waited for; matrix products, arithmetic and copies ran while one was open for 0% of the time, Pallas kernels for 30%

profile of v5, /device:TPU:96, one launch (start us, length us, event | category | flops | bytes accessed | tf_op | source)
XLA Modules:
  0.0 86.5 jit_solution(2334596871416364332)
XLA Ops:
  0.7 2.4 %shard_map.42 = (bf16[1,512,1024]{2,1,0:T(8,128)(2,1)}, bf16[1,512,1024]{2,1,0:T(8,128)(2,1)}) custom-call(bf16[3,512,1024]{2,1,0:T(8,128)(2,1)} %refs_0_.5), custom_call_target="tpu_custom_call" | custom-call | flops 1024 | bytes 1024 | tf_op jit(solution)/shard_map/pallas_call | solution.py:269
  3.1 4.5 %collective-permute-start.3 = (bf16[1,512,1024]{2,1,0:T(8,128)(2,1)}, bf16[1,512,1024]{2,1,0:T(8,128)(2,1)}, u32[]{:S(2)}, u32[]{:S(2)}) collective-permute-start(bf16[1,512,1024]{2,1,0:T(8,128)(2,1)} %get-tuple-element.51), channel_id=1, source_target_pairs={{8,16},{16,8},{24,32},{32,24},{40,48},{48,40},{56,64},{64,56},{72,... | collective-permute-start | bytes 3145736 | tf_op jit(solution)/shard_map/ppermute | solution.py:517
  8.1 6.0 %shard_map.41 = (s16[4,208,512]{2,1,0:T(8,128)(2,1)}, bf16[2,272,1024]{2,1,0:T(8,128)(2,1)}, bf16[2,272,1024]{2,1,0:T(8,128)(2,1)}) custom-call(bf16[3,512,1024]{2,1,0:T(8,128)(2,1)} %refs_0_.5, bf16[3,512,1024]{2,1,0:T(8,128)(2,1)} %collective-permute-done.refs_1_.ref, s32[3,4]{1,0:T(4,128)} %refs_4_.3), custom_call_target="tpu_custom_call" | custom-call | flops 1048576 | bytes 65536 | tf_op jit(solution)/shard_map/pallas_call | solution.py:203
  14.1 4.5 %all-to-all-start = ((s16[4,208,512]{2,1,0:T(8,128)(2,1)}), s16[4,208,512]{2,1,0:T(8,128)(2,1)S(1)}, u32[]{:S(2)}, u32[]{:S(2)}) async-start(s16[4,208,512]{2,1,0:T(8,128)(2,1)} %get-tuple-element.53), calls=%async_computation | async-start | bytes 1703936 | tf_op jit(solution)/shard_map/all_to_all | solution.py:504
  18.6 3.1 %collective-permute-start.1 = (bf16[2,272,1024]{2,1,0:T(8,128)(2,1)}, bf16[2,272,1024]{2,1,0:T(8,128)(2,1)S(1)}, u32[]{:S(2)}, u32[]{:S(2)}) collective-permute-start(bf16[2,272,1024]{2,1,0:T(8,128)(2,1)} %get-tuple-element.49), channel_id=1, source_target_pairs={{8,16},{16,8},{24,32},{32,24},{40,48},{48,40},{56,64},{64,56},{72,... | collective-permute-start | bytes 3342344 | tf_op jit(solution)/shard_map/ppermute | solution.py:517
  21.7 0.5 collective-permute-start.2
  22.2 11.2 %collective-permute-done.3.first_ref = bf16[1,512,1024]{2,1,0:T(8,128)(2,1)} collective-permute-done((bf16[1,512,1024]{2,1,0:T(8,128)(2,1)}, bf16[1,512,1024]{2,1,0:T(8,128)(2,1)}, u32[]{:S(2)}, u32[]{:S(2)}) %collective-permute-start.3) | collective-permute-done | bytes 1048608 | tf_op jit(solution)/shard_map/ppermute | solution.py:517
  33.4 0.6 collective-permute-done.4.second_ref
  34.1 1.7 %shard_map.43 = (bf16[1,256,1024]{2,1,0:T(8,128)(2,1)S(1)}, bf16[1,256,1024]{2,1,0:T(8,128)(2,1)S(1)}, bf16[1,256,1024]{2,1,0:T(8,128)(2,1)S(1)}, bf16[1,256,1024]{2,1,0:T(8,128)(2,1)S(1)}) custom-call(bf16[1,512,1024]{2,1,0:T(8,128)(2,1)} %collective-permute-done.3.first_ref, bf16[1,512,1024]{2,1,0:T(8,128)(2,1)} %collective-permute-done.4.second_ref), custom_call_target="tpu_custom_call" | custom-call | flops 1024 | bytes 1024 | tf_op jit(solution)/shard_map/pallas_call | solution.py:322
  35.8 0.5 collective-permute-start.6
  36.4 2.0 %shard_map.44.refs_1_ = bf16[3,512,1024]{2,1,0:T(8,128)(2,1)S(1)} custom-call(bf16[3,512,1024]{2,1,0:T(8,128)(2,1)} %collective-permute-done.refs_1_.ref), custom_call_target="tpu_custom_call" | custom-call | flops 1024 | bytes 1024 | tf_op jit(solution)/shard_map/pallas_call | solution.py:290
  38.5 0.7 collective-permute-done.5.refs_4_
  39.3 3.7 %shard_map.45 = (s16[400,512]{1,0:T(8,128)(2,1)S(1)}, s16[400,512]{1,0:T(8,128)(2,1)S(1)}, s16[400,512]{1,0:T(8,128)(2,1)S(1)}, s16[400,512]{1,0:T(8,128)(2,1)S(1)}) custom-call(bf16[3,512,1024]{2,1,0:T(8,128)(2,1)S(1)} %copy-done, bf16[3,512,1024]{2,1,0:T(8,128)(2,1)S(1)} %shard_map.44.refs_1_, bf16[1,256,1024]{2,1,0:T(8,128)(2,1)S(1)} %get-tuple-element.56.refs_2_, ...), custom_call_target="tpu_custom_call" | custom-call | flops 1048576 | bytes 65536 | tf_op jit(solution)/shard_map/pallas_call | solution.py:203
  42.9 1.6 %collective-permute-start.14 = (s16[400,512]{1,0:T(8,128)(2,1)S(1)}, s16[400,512]{1,0:T(8,128)(2,1)S(1)}, u32[]{:S(2)}, u32[]{:S(2)}) collective-permute-start(s16[400,512]{1,0:T(8,128)(2,1)S(1)} %get-tuple-element.82), channel_id=1, source_target_pairs={{0,2},{1,3},{2,4},{3,5},{4,6},{5,7},{6,0},{7,1},{8,10},{9,11},{10,... | collective-permute-start | bytes 1228808 | tf_op jit(solution)/shard_map/ppermute | solution.py:499
  44.6 2.9 %collective-permute-start.15 = (s16[400,512]{1,0:T(8,128)(2,1)S(1)}, s16[400,512]{1,0:T(8,128)(2,1)S(1)}, u32[]{:S(2)}, u32[]{:S(2)}) collective-permute-start(s16[400,512]{1,0:T(8,128)(2,1)S(1)} %get-tuple-element.83), channel_id=1, source_target_pairs={{0,4},{1,5},{2,6},{3,7},{4,0},{5,1},{6,2},{7,3},{8,12},{9,13},{10,... | collective-permute-start | bytes 1228808 | tf_op jit(solution)/shard_map/ppermute | solution.py:499
  47.5 1.3 %collective-permute-start.16 = (s16[400,512]{1,0:T(8,128)(2,1)S(1)}, s16[400,512]{1,0:T(8,128)(2,1)S(1)}, u32[]{:S(2)}, u32[]{:S(2)}) collective-permute-start(s16[400,512]{1,0:T(8,128)(2,1)S(1)} %get-tuple-element.84), channel_id=1, source_target_pairs={{0,6},{1,7},{2,0},{3,1},{4,2},{5,3},{6,4},{7,5},{8,14},{9,15},{10,... | collective-permute-start | bytes 1228808 | tf_op jit(solution)/shard_map/ppermute | solution.py:499
  48.8 1.7 %shard_map.46 = (f32[3,4,64,512]{3,2,1,0:T(8,128)}, f32[3,4,64,512]{3,2,1,0:T(8,128)}) custom-call(s16[4,208,512]{2,1,0:T(8,128)(2,1)S(1)} %all-to-all-done.refs_0_, s32[3,4]{1,0:T(4,128)S(1)} %copy-done.1), custom_call_target="tpu_custom_call" | custom-call | flops 1048576 | bytes 65536 | tf_op jit(solution)/shard_map/pallas_call | solution.py:427
  50.5 1.9 %shard_map.47.refs_1_ = bf16[3,512,1024]{2,1,0:T(8,128)(2,1)S(1)} custom-call(bf16[3,512,1024]{2,1,0:T(8,128)(2,1)} %collective-permute-done.refs_1_.ref), custom_call_target="tpu_custom_call" | custom-call | flops 1024 | bytes 1024 | tf_op jit(solution)/shard_map/pallas_call | solution.py:290
  52.4 4.3 %collective-permute-done.1.refs_2_ = bf16[2,272,1024]{2,1,0:T(8,128)(2,1)S(1)} collective-permute-done((bf16[2,272,1024]{2,1,0:T(8,128)(2,1)}, bf16[2,272,1024]{2,1,0:T(8,128)(2,1)S(1)}, u32[]{:S(2)}, u32[]{:S(2)}) %collective-permute-start.1) | collective-permute-done | bytes 1114144 | tf_op jit(solution)/shard_map/ppermute | solution.py:517
  57.1 2.2 %shard_map.48 = (s16[144,512]{1,0:T(8,128)(2,1)S(1)}, s16[144,512]{1,0:T(8,128)(2,1)S(1)}, s16[144,512]{1,0:T(8,128)(2,1)S(1)}, s16[144,512]{1,0:T(8,128)(2,1)S(...) custom-call(bf16[3,512,1024]{2,1,0:T(8,128)(2,1)S(1)} %copy-done, ...), custom_call_target="tpu_custom_call" | custom-call | flops 1048576 | bytes 65536 | tf_op jit(solution)/shard_map/pallas_call | solution.py:203
  59.3 1.4 %collective-permute-done.8.refs_5_ = s16[4,80,256]{2,1,0:T(8,128)(2,1)S(1)} collective-permute-done((s16[4,80,256]{2,1,0:T(8,128)(2,1)S(1)}, s16[4,80,256]{2,1,0:T(8,128)(2,1)S(1)}, u32[]{:S(2)}, u32[]{:S(2)}) %collective-permute-start.8) | collective-permute-done | bytes 163872 | tf_op jit(solution)/shard_map/ppermute | solution.py:492
  60.8 1.6 %collective-permute-start.9 = (s16[208,512]{1,0:T(8,128)(2,1)S(1)}, s16[208,512]{1,0:T(8,128)(2,1)S(1)}, u32[]{:S(2)}, u32[]{:S(2)}) collective-permute-start(s16[208,512]{1,0:T(8,128)(2,1)S(1)} %get-tuple-element.76), channel_id=1, source_target_pairs={{0,2},{1,3},{2,4},{3,5},{4,6},{5,7},{6,0},{7,1},{8,10},{9,11},{10,... | collective-permute-start | bytes 638984 | tf_op jit(solution)/shard_map/ppermute | solution.py:499
  62.5 2.9 %collective-permute-start.10 = (s16[208,512]{1,0:T(8,128)(2,1)S(1)}, s16[208,512]{1,0:T(8,128)(2,1)S(1)}, u32[]{:S(2)}, u32[]{:S(2)}) collective-permute-start(s16[208,512]{1,0:T(8,128)(2,1)S(1)} %get-tuple-element.77), channel_id=1, source_target_pairs={{0,4},{1,5},{2,6},{3,7},{4,0},{5,1},{6,2},{7,3},{8,12},{9,13},{10,... | collective-permute-start | bytes 638984 | tf_op jit(solution)/shard_map/ppermute | solution.py:499
  65.4 1.3 %collective-permute-start.11 = (s16[208,512]{1,0:T(8,128)(2,1)S(1)}, s16[208,512]{1,0:T(8,128)(2,1)S(1)}, u32[]{:S(2)}, u32[]{:S(2)}) collective-permute-start(s16[208,512]{1,0:T(8,128)(2,1)S(1)} %get-tuple-element.78), channel_id=1, source_target_pairs={{0,6},{1,7},{2,0},{3,1},{4,2},{5,3},{6,4},{7,5},{8,14},{9,15},{10,... | collective-permute-start | bytes 638984 | tf_op jit(solution)/shard_map/ppermute | solution.py:499
  66.7 2.1 %shard_map.51 = (f32[3,4,64,512]{3,2,1,0:T(8,128)}, f32[3,4,64,512]{3,2,1,0:T(8,128)}, s16[272,512]{1,0:T(8,128)(2,1)S(1)}, s16[272,512]{1,0:T(8,128)(2,1)S(1)}) custom-call(s16[400,512]{1,0:T(8,128)(2,1)S(1)} %get-tuple-element.61.refs_0_, s16[400,512]{1,0:T(8,128)(2,1)S(1)} %collective-permute-done.14.refs_1_, ...), custom_call_target="tpu_custom_call", output_to_operand_aliasing={{0}: (6, {}), {1}: (7, {})} | custom-call | flops 1048576 | bytes 65536 | tf_op jit(solution)/shard_map/pallas_call | solution.py:427
  68.8 4.2 %collective-permute-start.17 = (s16[272,512]{1,0:T(8,128)(2,1)S(1)}, s16[272,512]{1,0:T(8,128)(2,1)S(1)}, u32[]{:S(2)}, u32[]{:S(2)}) collective-permute-start(s16[272,512]{1,0:T(8,128)(2,1)S(1)} %get-tuple-element.87), channel_id=1, source_target_pairs={{8,16},{16,8},{24,32},{32,24},{40,48},{48,40},{56,64},{64,56},{72,... | collective-permute-start | bytes 835592 | tf_op jit(solution)/shard_map/ppermute | solution.py:517
  73.2 2.0 %collective-permute-done.10.refs_2_ = s16[208,512]{1,0:T(8,128)(2,1)S(1)} collective-permute-done((s16[208,512]{1,0:T(8,128)(2,1)S(1)}, s16[208,512]{1,0:T(8,128)(2,1)S(1)}, u32[]{:S(2)}, u32[]{:S(2)}) %collective-permute-start.10) | collective-permute-done | bytes 213024 | tf_op jit(solution)/shard_map/ppermute | solution.py:499
  75.2 0.9 %shard_map.50 = (s16[144,512]{1,0:T(8,128)(2,1)S(1)}, s16[144,512]{1,0:T(8,128)(2,1)S(1)}, f32[3,64,512]{2,1,0:T(8,128)S(1)}) custom-call(s16[208,512]{1,0:T(8,128)(2,1)S(1)} %get-tuple-element.75.refs_0_, s16[208,512]{1,0:T(8,128)(2,1)S(1)} %collective-permute-done.9.refs_1_, s16[208,512]{1,0:T(8,128)(2,1)S(1)} %collective-permute-done.10.refs_2_, ...), custom_call_target="tpu_custom_call" | custom-call | flops 1048576 | bytes 65536 | tf_op jit(solution)/shard_map/pallas_call | solution.py:427
  76.1 4.2 %collective-permute-start.12 = (s16[144,512]{1,0:T(8,128)(2,1)S(1)}, s16[144,512]{1,0:T(8,128)(2,1)S(1)}, u32[]{:S(2)}, u32[]{:S(2)}) collective-permute-start(s16[144,512]{1,0:T(8,128)(2,1)S(1)} %get-tuple-element.80), channel_id=1, source_target_pairs={{8,16},{16,8},{24,32},{32,24},{40,48},{48,40},{56,64},{64,56},{72,... | collective-permute-start | bytes 442376 | tf_op jit(solution)/shard_map/ppermute | solution.py:517
  80.7 1.1 %shard_map.52 = (f32[3,4,64,512]{3,2,1,0:T(8,128)}, f32[3,4,64,512]{3,2,1,0:T(8,128)}) custom-call(s16[272,512]{1,0:T(8,128)(2,1)S(1)} %collective-permute-done.17.first_ref, s16[272,512]{1,0:T(8,128)(2,1)S(1)} %collective-permute-done.18.second_ref, f32[3,64,512]{2,1,0:T(8,128)S(1)} %get-tuple-element.89.refs_0_, ...), custom_call_target="tpu_custom_call", output_to_operand_aliasing={{0}: (3, {}), {1}: (4, {})} | custom-call | flops 1048576 | bytes 65536 | tf_op jit(solution)/shard_map/pallas_call | solution.py:476
  81.8 3.4 %collective-permute-done.12.first_ref = s16[144,512]{1,0:T(8,128)(2,1)S(1)} collective-permute-done((s16[144,512]{1,0:T(8,128)(2,1)S(1)}, s16[144,512]{1,0:T(8,128)(2,1)S(1)}, u32[]{:S(2)}, u32[]{:S(2)}) %collective-permute-start.12) | collective-permute-done | bytes 147488 | tf_op jit(solution)/shard_map/ppermute | solution.py:517
  85.5 0.8 shard_map.53
  (25 shorter events, 2.0 us)
Async XLA Ops:
  0.6 7.5 %collective-permute-start = (bf16[3,512,1024]{2,1,0:T(8,128)(2,1)}, bf16[3,512,1024]{2,1,0:T(8,128)(2,1)}, u32[]{:S(2)}, u32[]{:S(2)}) collective-permute-start(bf16[3,512,1024]{2,1,0:T(8,128)(2,1)} %refs_0_.5), channel_id=1, source_target_pairs={{0,1},{1,0},{2,3},{3,2},{4,5},{5,4},{6,7},{7,6},{8,9},{9,8},{10,11... | collective-permute-start | bytes 9437192 | tf_op jit(solution)/shard_map/ppermute | solution.py:492
  3.1 30.3 %collective-permute-start.3 = (bf16[1,512,1024]{2,1,0:T(8,128)(2,1)}, bf16[1,512,1024]{2,1,0:T(8,128)(2,1)}, u32[]{:S(2)}, u32[]{:S(2)}) collective-permute-start(bf16[1,512,1024]{2,1,0:T(8,128)(2,1)} %get-tuple-element.51), channel_id=1, source_target_pairs={{8,16},{16,8},{24,32},{32,24},{40,48},{48,40},{56,64},{64,56},{72,... | collective-permute-start | bytes 3145736 | tf_op jit(solution)/shard_map/ppermute | solution.py:517
  7.7 26.4 %collective-permute-start.4 = (bf16[1,512,1024]{2,1,0:T(8,128)(2,1)}, bf16[1,512,1024]{2,1,0:T(8,128)(2,1)}, u32[]{:S(2)}, u32[]{:S(2)}) collective-permute-start(bf16[1,512,1024]{2,1,0:T(8,128)(2,1)} %get-tuple-element.52), channel_id=1, source_target_pairs={{0,8},{8,0},{16,24},{24,16},{32,40},{40,32},{48,56},{56,48},{64,72... | collective-permute-start | bytes 3145736 | tf_op jit(solution)/shard_map/ppermute | solution.py:517
  14.1 19.9 %all-to-all-start = ((s16[4,208,512]{2,1,0:T(8,128)(2,1)}), s16[4,208,512]{2,1,0:T(8,128)(2,1)S(1)}, u32[]{:S(2)}, u32[]{:S(2)}) async-start(s16[4,208,512]{2,1,0:T(8,128)(2,1)} %get-tuple-element.53), calls=%async_computation | async-start | bytes 1703936 | tf_op jit(solution)/shard_map/all_to_all | solution.py:504
  18.6 38.2 %collective-permute-start.1 = (bf16[2,272,1024]{2,1,0:T(8,128)(2,1)}, bf16[2,272,1024]{2,1,0:T(8,128)(2,1)S(1)}, u32[]{:S(2)}, u32[]{:S(2)}) collective-permute-start(bf16[2,272,1024]{2,1,0:T(8,128)(2,1)} %get-tuple-element.49), channel_id=1, source_target_pairs={{8,16},{16,8},{24,32},{32,24},{40,48},{48,40},{56,64},{64,56},{72,... | collective-permute-start | bytes 3342344 | tf_op jit(solution)/shard_map/ppermute | solution.py:517
  21.7 35.4 %collective-permute-start.2 = (bf16[2,272,1024]{2,1,0:T(8,128)(2,1)}, bf16[2,272,1024]{2,1,0:T(8,128)(2,1)S(1)}, u32[]{:S(2)}, u32[]{:S(2)}) collective-permute-start(bf16[2,272,1024]{2,1,0:T(8,128)(2,1)} %get-tuple-element.50), channel_id=1, source_target_pairs={{0,8},{8,0},{16,24},{24,16},{32,40},{40,32},{48,56},{56,48},{64,72... | collective-permute-start | bytes 3342344 | tf_op jit(solution)/shard_map/ppermute | solution.py:517
  35.7 2.7 %collective-permute-start.7 = (bf16[1,256,1024]{2,1,0:T(8,128)(2,1)S(1)}, bf16[1,256,1024]{2,1,0:T(8,128)(2,1)S(1)}, u32[]{:S(2)}, u32[]{:S(2)}) collective-permute-start(bf16[1,256,1024]{2,1,0:T(8,128)(2,1)S(1)} %get-tuple-element.60), channel_id=1, source_target_pairs={{0,1},{1,0},{2,3},{3,2},{4,5},{5,4},{6,7},{7,6},{8,9},{9,8},{10,11... | collective-permute-start | bytes 1572872 | tf_op jit(solution)/shard_map/ppermute | solution.py:492
  35.8 2.7 %collective-permute-start.6 = (bf16[1,256,1024]{2,1,0:T(8,128)(2,1)S(1)}, bf16[1,256,1024]{2,1,0:T(8,128)(2,1)S(1)}, u32[]{:S(2)}, u32[]{:S(2)}) collective-permute-start(bf16[1,256,1024]{2,1,0:T(8,128)(2,1)S(1)} %get-tuple-element.58.refs_3_), channel_id=1, source_target_pairs={{0,1},{1,0},{2,3},{3,2},{4,5},{5,4},{6,7},{7,6},{8,9},{9,8},{10,11... | collective-permute-start | bytes 1572872 | tf_op jit(solution)/shard_map/ppermute | solution.py:492
  36.3 2.9 %collective-permute-start.5 = (bf16[1,256,1024]{2,1,0:T(8,128)(2,1)S(1)}, bf16[1,256,1024]{2,1,0:T(8,128)(2,1)S(1)}, u32[]{:S(2)}, u32[]{:S(2)}) collective-permute-start(bf16[1,256,1024]{2,1,0:T(8,128)(2,1)S(1)} %get-tuple-element.56.refs_2_), channel_id=1, source_target_pairs={{0,1},{1,0},{2,3},{3,2},{4,5},{5,4},{6,7},{7,6},{8,9},{9,8},{10,11... | collective-permute-start | bytes 1572872 | tf_op jit(solution)/shard_map/ppermute | solution.py:492
  36.4 2.8 %copy-start = (bf16[3,512,1024]{2,1,0:T(8,128)(2,1)S(1)}, bf16[3,512,1024]{2,1,0:T(8,128)(2,1)}, u32[]{:S(2)}) copy-start(bf16[3,512,1024]{2,1,0:T(8,128)(2,1)} %refs_0_.5) | copy-start | bytes 9437188
  39.3 9.6 %copy-start.1 = (s32[3,4]{1,0:T(4,128)S(1)}, s32[3,4]{1,0:T(4,128)}, u32[]{:S(2)}) copy-start(s32[3,4]{1,0:T(4,128)} %refs_4_.3) | copy-start | bytes 148
  42.9 22.4 %collective-permute-start.14 = (s16[400,512]{1,0:T(8,128)(2,1)S(1)}, s16[400,512]{1,0:T(8,128)(2,1)S(1)}, u32[]{:S(2)}, u32[]{:S(2)}) collective-permute-start(s16[400,512]{1,0:T(8,128)(2,1)S(1)} %get-tuple-element.82), channel_id=1, source_target_pairs={{0,2},{1,3},{2,4},{3,5},{4,6},{5,7},{6,0},{7,1},{8,10},{9,11},{10,... | collective-permute-start | bytes 1228808 | tf_op jit(solution)/shard_map/ppermute | solution.py:499
  44.6 22.2 %collective-permute-start.15 = (s16[400,512]{1,0:T(8,128)(2,1)S(1)}, s16[400,512]{1,0:T(8,128)(2,1)S(1)}, u32[]{:S(2)}, u32[]{:S(2)}) collective-permute-start(s16[400,512]{1,0:T(8,128)(2,1)S(1)} %get-tuple-element.83), channel_id=1, source_target_pairs={{0,4},{1,5},{2,6},{3,7},{4,0},{5,1},{6,2},{7,3},{8,12},{9,13},{10,... | collective-permute-start | bytes 1228808 | tf_op jit(solution)/shard_map/ppermute | solution.py:499
  47.5 19.3 %collective-permute-start.16 = (s16[400,512]{1,0:T(8,128)(2,1)S(1)}, s16[400,512]{1,0:T(8,128)(2,1)S(1)}, u32[]{:S(2)}, u32[]{:S(2)}) collective-permute-start(s16[400,512]{1,0:T(8,128)(2,1)S(1)} %get-tuple-element.84), channel_id=1, source_target_pairs={{0,6},{1,7},{2,0},{3,1},{4,2},{5,3},{6,4},{7,5},{8,14},{9,15},{10,... | collective-permute-start | bytes 1228808 | tf_op jit(solution)/shard_map/ppermute | solution.py:499
  59.3 1.5 %collective-permute-start.8 = (s16[4,80,256]{2,1,0:T(8,128)(2,1)S(1)}, s16[4,80,256]{2,1,0:T(8,128)(2,1)S(1)}, u32[]{:S(2)}, u32[]{:S(2)}) collective-permute-start(s16[4,80,256]{2,1,0:T(8,128)(2,1)S(1)} %get-tuple-element.74), channel_id=1, source_target_pairs={{0,1},{1,0},{2,3},{3,2},{4,5},{5,4},{6,7},{7,6},{8,9},{9,8},{10,11... | collective-permute-start | bytes 491528 | tf_op jit(solution)/shard_map/ppermute | solution.py:492
  60.8 12.3 %collective-permute-start.9 = (s16[208,512]{1,0:T(8,128)(2,1)S(1)}, s16[208,512]{1,0:T(8,128)(2,1)S(1)}, u32[]{:S(2)}, u32[]{:S(2)}) collective-permute-start(s16[208,512]{1,0:T(8,128)(2,1)S(1)} %get-tuple-element.76), channel_id=1, source_target_pairs={{0,2},{1,3},{2,4},{3,5},{4,6},{5,7},{6,0},{7,1},{8,10},{9,11},{10,... | collective-permute-start | bytes 638984 | tf_op jit(solution)/shard_map/ppermute | solution.py:499
  62.5 12.7 %collective-permute-start.10 = (s16[208,512]{1,0:T(8,128)(2,1)S(1)}, s16[208,512]{1,0:T(8,128)(2,1)S(1)}, u32[]{:S(2)}, u32[]{:S(2)}) collective-permute-start(s16[208,512]{1,0:T(8,128)(2,1)S(1)} %get-tuple-element.77), channel_id=1, source_target_pairs={{0,4},{1,5},{2,6},{3,7},{4,0},{5,1},{6,2},{7,3},{8,12},{9,13},{10,... | collective-permute-start | bytes 638984 | tf_op jit(solution)/shard_map/ppermute | solution.py:499
  65.4 9.8 %collective-permute-start.11 = (s16[208,512]{1,0:T(8,128)(2,1)S(1)}, s16[208,512]{1,0:T(8,128)(2,1)S(1)}, u32[]{:S(2)}, u32[]{:S(2)}) collective-permute-start(s16[208,512]{1,0:T(8,128)(2,1)S(1)} %get-tuple-element.78), channel_id=1, source_target_pairs={{0,6},{1,7},{2,0},{3,1},{4,2},{5,3},{6,4},{7,5},{8,14},{9,15},{10,... | collective-permute-start | bytes 638984 | tf_op jit(solution)/shard_map/ppermute | solution.py:499
  68.8 11.9 %collective-permute-start.17 = (s16[272,512]{1,0:T(8,128)(2,1)S(1)}, s16[272,512]{1,0:T(8,128)(2,1)S(1)}, u32[]{:S(2)}, u32[]{:S(2)}) collective-permute-start(s16[272,512]{1,0:T(8,128)(2,1)S(1)} %get-tuple-element.87), channel_id=1, source_target_pairs={{8,16},{16,8},{24,32},{32,24},{40,48},{48,40},{56,64},{64,56},{72,... | collective-permute-start | bytes 835592 | tf_op jit(solution)/shard_map/ppermute | solution.py:517
  73.1 7.7 %collective-permute-start.18 = (s16[272,512]{1,0:T(8,128)(2,1)S(1)}, s16[272,512]{1,0:T(8,128)(2,1)S(1)}, u32[]{:S(2)}, u32[]{:S(2)}) collective-permute-start(s16[272,512]{1,0:T(8,128)(2,1)S(1)} %get-tuple-element.88), channel_id=1, source_target_pairs={{0,8},{8,0},{16,24},{24,16},{32,40},{40,32},{48,56},{56,48},{64,72... | collective-permute-start | bytes 835592 | tf_op jit(solution)/shard_map/ppermute | solution.py:517
  76.1 9.1 %collective-permute-start.12 = (s16[144,512]{1,0:T(8,128)(2,1)S(1)}, s16[144,512]{1,0:T(8,128)(2,1)S(1)}, u32[]{:S(2)}, u32[]{:S(2)}) collective-permute-start(s16[144,512]{1,0:T(8,128)(2,1)S(1)} %get-tuple-element.80), channel_id=1, source_target_pairs={{8,16},{16,8},{24,32},{32,24},{40,48},{48,40},{56,64},{64,56},{72,... | collective-permute-start | bytes 442376 | tf_op jit(solution)/shard_map/ppermute | solution.py:517
  80.3 5.2 %collective-permute-start.13 = (s16[144,512]{1,0:T(8,128)(2,1)S(1)}, s16[144,512]{1,0:T(8,128)(2,1)S(1)}, u32[]{:S(2)}, u32[]{:S(2)}) collective-permute-start(s16[144,512]{1,0:T(8,128)(2,1)S(1)} %get-tuple-element.81), channel_id=1, source_target_pairs={{0,8},{8,0},{16,24},{24,16},{32,40},{40,32},{48,56},{56,48},{64,72... | collective-permute-start | bytes 442376 | tf_op jit(solution)/shard_map/ppermute | solution.py:517

commit v6 on v5

--- a/solution.py
+++ b/solution.py
@@ -12,6 +12,7 @@
 HALF = 256
 SLICE = 64
 CHIPS = 4
+AWAY = (0, 1, 3, 2)
 STEPS = 256.0
 TOP = 32700.0
 LN2 = 0.6931471805599453
@@ -66,7 +67,7 @@
 
         def work(low_ref, high_ref):
             ins.update({"low2": low_ref, "high2": high_ref})
-            lines_ref[...] = low_ref[0, HALF : HALF + 16, :BF].astype(jnp.float32)
+            lines_ref[...] = low_ref[0, BF : BF + 16, :BF].astype(jnp.float32)
             pair_work(pairs, blocks, halved, ins, outs, together, place)
 
         @pl.when(place[2] == 1)
@@ -85,10 +86,13 @@
     if together:
         outs = [outs[0].at[d] for d in range(CHIPS)]
     core, chip = place[0], place[1]
-    order = [d if together else (chip + d) % CHIPS for d in range(CHIPS)]
+    stacked = ("low2", "high2")
+    order = [d if together else (chip + AWAY[d]) % CHIPS for d in range(CHIPS)]
 
     def read(piece, start, rows):
         name, index = piece
+        if name in stacked:
+            return ins[name][0, pl.ds(index * HALF + start, rows), :]
         return ins[name][index, pl.ds(start, rows), :]
 
     def slices(pieces):
@@ -98,7 +102,7 @@
                 start = (2 * (o % 2) + core) * SLICE
                 low, high = (read(piece, start, SLICE) for piece in pieces)
                 rows.append(jnp.where(o < 2, low, high))
-            elif ins[pieces[0][0]].shape[1] < BF:
+            elif pieces[0][0] in stacked or ins[pieces[0][0]].shape[1] < BF:
                 rows.append(read(pieces[0], o * SLICE, SLICE))
             else:
                 rows.append(read(pieces[0], (2 * o + core) * SLICE, SLICE))
@@ -170,13 +174,14 @@
 
     def put(up_ref, down_ref):
         for i, source in enumerate(sources):
-            up_ref[i, :HALF, :] = source[1, pl.ds(core * HALF, HALF), :]
-            up_ref[i, HALF:, :] = lines
+            up_ref[0, i * HALF : (i + 1) * HALF, :] = source[1, pl.ds(core * HALF, HALF), :]
             for y in range(CHIPS):
-                down_ref[i, y * SLICE : (y + 1) * SLICE, :] = source[
+                row = i * HALF + y * SLICE
+                down_ref[0, row : row + SLICE, :] = source[
                     1, pl.ds((2 * y + core) * SLICE, SLICE), :
                 ]
-            down_ref[i, HALF:, :] = lines
+        up_ref[0, BF:, :] = lines
+        down_ref[0, BF:, :] = lines
 
     @pl.when(place[2] == 1)
     def _():
@@ -199,7 +204,7 @@
         shapes.append(jax.ShapeDtypeStruct((16, BF), jnp.float32))
     second = mask is not None
     if second:
-        shapes += [jax.ShapeDtypeStruct((2, HALF + 16, COLS), jnp.bfloat16)] * 2
+        shapes += [jax.ShapeDtypeStruct((1, BF + 16, COLS), jnp.bfloat16)] * 2
     return pl.pallas_call(
         functools.partial(pair_kernel, pairs, blocks, halved, names, together, late, second),
         out_shape=shapes,
@@ -505,7 +510,7 @@
 
 
 def to_chips(parts):
-    return [parts[0]] + [chips_on(parts[d], d) for d in range(1, CHIPS)]
+    return [parts[0]] + [chips_on(parts[d], AWAY[d]) for d in range(1, CHIPS)]
 
 
 def pairwise(first, second):

time: 86.8 us -> 86.7 us (level)
  starting transfers between devices: 34.3 us -> 33.3 us
  waiting for transfers between devices: 24.6 us -> 25.5 us
where the time goes in v6:
time: 86.7 us; the launch traced here: 86.4 us
  starting transfers between devices  33.3 us (38%)
  Pallas kernels  26.5 us (31%)
  waiting for transfers between devices  25.5 us (29%)
  between operations  0.99 us (1%)
    ppermute x8, waiting for transfers between devices, pairwise(): done.append(lax.ppermute(value, 'space', sorted(pairs)))  20.7 us
    ppermute x8, starting transfers between devices, pairwise(): done.append(lax.ppermute(value, 'space', sorted(pairs)))  16.6 us
    pallas_call x3, Pallas kernels, pair_products(): pl.pallas_call(functools.partial(pair_kernel, pairs, blocks, halved, name...  11.8 us
    ppermute x6, starting transfers between devices, chips_on(): return lax.ppermute(value, 'occ', pairs)  11.4 us
    pallas_call x3, Pallas kernels, add_parts(): pl.pallas_call(kernel, out_shape=shapes, in_specs=in_specs, out_specs=out...  4.69 us
    all_to_all x1, starting transfers between devices, across(): return lax.all_to_all(value, 'occ', 0, 0, axis_index_groups=groups)  4.46 us
    pallas_call x2, Pallas kernels, bring(): pl.pallas_call(bring_kernel, out_shape=jax.ShapeDtypeStruct(value.shape,...  3.95 us
    ppermute x6, waiting for transfers between devices, chips_on(): return lax.ppermute(value, 'occ', pairs)  2.7 us
  transfers between devices with their start and end apart: 20, of which 10 were waited for; matrix products, arithmetic and copies ran while one was open for 0% of the time, Pallas kernels for 30%

profile of v6, /device:TPU:96, one launch (start us, length us, event | category | flops | bytes accessed | tf_op | source)
XLA Modules:
  0.0 86.4 jit_solution(17869403434846460319)
XLA Ops:
  0.7 2.4 %shard_map.42 = (bf16[1,512,1024]{2,1,0:T(8,128)(2,1)}, bf16[1,512,1024]{2,1,0:T(8,128)(2,1)}) custom-call(bf16[3,512,1024]{2,1,0:T(8,128)(2,1)} %refs_0_.5), custom_call_target="tpu_custom_call" | custom-call | flops 1024 | bytes 1024 | tf_op jit(solution)/shard_map/pallas_call | solution.py:274
  3.1 4.5 %collective-permute-start.3 = (bf16[1,512,1024]{2,1,0:T(8,128)(2,1)}, bf16[1,512,1024]{2,1,0:T(8,128)(2,1)}, u32[]{:S(2)}, u32[]{:S(2)}) collective-permute-start(bf16[1,512,1024]{2,1,0:T(8,128)(2,1)} %get-tuple-element.51), channel_id=1, source_target_pairs={{8,16},{16,8},{24,32},{32,24},{40,48},{48,40},{56,64},{64,56},{72,... | collective-permute-start | bytes 3145736 | tf_op jit(solution)/shard_map/ppermute | solution.py:522
  8.1 6.0 %shard_map.41 = (s16[4,208,512]{2,1,0:T(8,128)(2,1)}, bf16[1,528,1024]{2,1,0:T(8,128)(2,1)}, bf16[1,528,1024]{2,1,0:T(8,128)(2,1)}) custom-call(bf16[3,512,1024]{2,1,0:T(8,128)(2,1)} %refs_0_.5, bf16[3,512,1024]{2,1,0:T(8,128)(2,1)} %collective-permute-done.refs_1_.ref, s32[3,4]{1,0:T(4,128)} %refs_4_.3), custom_call_target="tpu_custom_call" | custom-call | flops 1048576 | bytes 65536 | tf_op jit(solution)/shard_map/pallas_call | solution.py:208
  14.1 4.5 %all-to-all-start = ((s16[4,208,512]{2,1,0:T(8,128)(2,1)}), s16[4,208,512]{2,1,0:T(8,128)(2,1)S(1)}, u32[]{:S(2)}, u32[]{:S(2)}) async-start(s16[4,208,512]{2,1,0:T(8,128)(2,1)} %get-tuple-element.53), calls=%async_computation | async-start | bytes 1703936 | tf_op jit(solution)/shard_map/all_to_all | solution.py:509
  18.6 3.1 %collective-permute-start.1 = (bf16[1,528,1024]{2,1,0:T(8,128)(2,1)}, bf16[1,528,1024]{2,1,0:T(8,128)(2,1)S(1)}, u32[]{:S(2)}, u32[]{:S(2)}) collective-permute-start(bf16[1,528,1024]{2,1,0:T(8,128)(2,1)} %get-tuple-element.49), channel_id=1, source_target_pairs={{8,16},{16,8},{24,32},{32,24},{40,48},{48,40},{56,64},{64,56},{72,... | collective-permute-start | bytes 3244040 | tf_op jit(solution)/shard_map/ppermute | solution.py:522
  21.7 0.6 collective-permute-start.2
  22.2 11.2 %collective-permute-done.3.first_ref = bf16[1,512,1024]{2,1,0:T(8,128)(2,1)} collective-permute-done((bf16[1,512,1024]{2,1,0:T(8,128)(2,1)}, bf16[1,512,1024]{2,1,0:T(8,128)(2,1)}, u32[]{:S(2)}, u32[]{:S(2)}) %collective-permute-start.3) | collective-permute-done | bytes 1048608 | tf_op jit(solution)/shard_map/ppermute | solution.py:522
  33.4 0.6 collective-permute-done.4.second_ref
  34.1 1.7 %shard_map.43 = (bf16[1,256,1024]{2,1,0:T(8,128)(2,1)S(1)}, bf16[1,256,1024]{2,1,0:T(8,128)(2,1)S(1)}, bf16[1,256,1024]{2,1,0:T(8,128)(2,1)S(1)}, bf16[1,256,1024]{2,1,0:T(8,128)(2,1)S(1)}) custom-call(bf16[1,512,1024]{2,1,0:T(8,128)(2,1)} %collective-permute-done.3.first_ref, bf16[1,512,1024]{2,1,0:T(8,128)(2,1)} %collective-permute-done.4.second_ref), custom_call_target="tpu_custom_call" | custom-call | flops 1024 | bytes 1024 | tf_op jit(solution)/shard_map/pallas_call | solution.py:327
  35.8 0.5 collective-permute-start.6
  36.4 2.0 %shard_map.44.refs_1_ = bf16[3,512,1024]{2,1,0:T(8,128)(2,1)S(1)} custom-call(bf16[3,512,1024]{2,1,0:T(8,128)(2,1)} %collective-permute-done.refs_1_.ref), custom_call_target="tpu_custom_call" | custom-call | flops 1024 | bytes 1024 | tf_op jit(solution)/shard_map/pallas_call | solution.py:295
  38.5 0.7 collective-permute-done.5.refs_4_
  39.3 3.6 %shard_map.45 = (s16[400,512]{1,0:T(8,128)(2,1)S(1)}, s16[400,512]{1,0:T(8,128)(2,1)S(1)}, s16[400,512]{1,0:T(8,128)(2,1)S(1)}, s16[400,512]{1,0:T(8,128)(2,1)S(1)}) custom-call(bf16[3,512,1024]{2,1,0:T(8,128)(2,1)S(1)} %copy-done, bf16[3,512,1024]{2,1,0:T(8,128)(2,1)S(1)} %shard_map.44.refs_1_, bf16[1,256,1024]{2,1,0:T(8,128)(2,1)S(1)} %get-tuple-element.56.refs_2_, ...), custom_call_target="tpu_custom_call" | custom-call | flops 1048576 | bytes 65536 | tf_op jit(solution)/shard_map/pallas_call | solution.py:208
  42.9 1.6 %collective-permute-start.14 = (s16[400,512]{1,0:T(8,128)(2,1)S(1)}, s16[400,512]{1,0:T(8,128)(2,1)S(1)}, u32[]{:S(2)}, u32[]{:S(2)}) collective-permute-start(s16[400,512]{1,0:T(8,128)(2,1)S(1)} %get-tuple-element.82), channel_id=1, source_target_pairs={{0,2},{1,3},{2,4},{3,5},{4,6},{5,7},{6,0},{7,1},{8,10},{9,11},{10,... | collective-permute-start | bytes 1228808 | tf_op jit(solution)/shard_map/ppermute | solution.py:504
  44.6 1.7 %collective-permute-start.15 = (s16[400,512]{1,0:T(8,128)(2,1)S(1)}, s16[400,512]{1,0:T(8,128)(2,1)S(1)}, u32[]{:S(2)}, u32[]{:S(2)}) collective-permute-start(s16[400,512]{1,0:T(8,128)(2,1)S(1)} %get-tuple-element.83), channel_id=1, source_target_pairs={{0,6},{1,7},{2,0},{3,1},{4,2},{5,3},{6,4},{7,5},{8,14},{9,15},{10,... | collective-permute-start | bytes 1228808 | tf_op jit(solution)/shard_map/ppermute | solution.py:504
  46.2 2.0 %collective-permute-start.16 = (s16[400,512]{1,0:T(8,128)(2,1)S(1)}, s16[400,512]{1,0:T(8,128)(2,1)S(1)}, u32[]{:S(2)}, u32[]{:S(2)}) collective-permute-start(s16[400,512]{1,0:T(8,128)(2,1)S(1)} %get-tuple-element.84), channel_id=1, source_target_pairs={{0,4},{1,5},{2,6},{3,7},{4,0},{5,1},{6,2},{7,3},{8,12},{9,13},{10,... | collective-permute-start | bytes 1228808 | tf_op jit(solution)/shard_map/ppermute | solution.py:504
  48.2 1.7 %shard_map.46 = (f32[3,4,64,512]{3,2,1,0:T(8,128)}, f32[3,4,64,512]{3,2,1,0:T(8,128)}) custom-call(s16[4,208,512]{2,1,0:T(8,128)(2,1)S(1)} %all-to-all-done.refs_0_, s32[3,4]{1,0:T(4,128)S(1)} %copy-done.1), custom_call_target="tpu_custom_call" | custom-call | flops 1048576 | bytes 65536 | tf_op jit(solution)/shard_map/pallas_call | solution.py:432
  49.9 1.9 %shard_map.47.refs_1_ = bf16[3,512,1024]{2,1,0:T(8,128)(2,1)S(1)} custom-call(bf16[3,512,1024]{2,1,0:T(8,128)(2,1)} %collective-permute-done.refs_1_.ref), custom_call_target="tpu_custom_call" | custom-call | flops 1024 | bytes 1024 | tf_op jit(solution)/shard_map/pallas_call | solution.py:295
  51.8 4.2 %collective-permute-done.1.refs_2_ = bf16[1,528,1024]{2,1,0:T(8,128)(2,1)S(1)} collective-permute-done((bf16[1,528,1024]{2,1,0:T(8,128)(2,1)}, bf16[1,528,1024]{2,1,0:T(8,128)(2,1)S(1)}, u32[]{:S(2)}, u32[]{:S(2)}) %collective-permute-start.1) | collective-permute-done | bytes 1081376 | tf_op jit(solution)/shard_map/ppermute | solution.py:522
  56.4 2.2 %shard_map.48 = (s16[144,512]{1,0:T(8,128)(2,1)S(1)}, s16[144,512]{1,0:T(8,128)(2,1)S(1)}, s16[144,512]{1,0:T(8,128)(2,1)S(1)}, s16[144,512]{1,0:T(8,128)(2,1)S(...) custom-call(bf16[3,512,1024]{2,1,0:T(8,128)(2,1)S(1)} %copy-done, ...), custom_call_target="tpu_custom_call" | custom-call | flops 1048576 | bytes 65536 | tf_op jit(solution)/shard_map/pallas_call | solution.py:208
  58.7 1.4 %collective-permute-done.8.refs_5_ = s16[4,80,256]{2,1,0:T(8,128)(2,1)S(1)} collective-permute-done((s16[4,80,256]{2,1,0:T(8,128)(2,1)S(1)}, s16[4,80,256]{2,1,0:T(8,128)(2,1)S(1)}, u32[]{:S(2)}, u32[]{:S(2)}) %collective-permute-start.8) | collective-permute-done | bytes 163872 | tf_op jit(solution)/shard_map/ppermute | solution.py:497
  60.1 1.6 %collective-permute-start.9 = (s16[208,512]{1,0:T(8,128)(2,1)S(1)}, s16[208,512]{1,0:T(8,128)(2,1)S(1)}, u32[]{:S(2)}, u32[]{:S(2)}) collective-permute-start(s16[208,512]{1,0:T(8,128)(2,1)S(1)} %get-tuple-element.76), channel_id=1, source_target_pairs={{0,2},{1,3},{2,4},{3,5},{4,6},{5,7},{6,0},{7,1},{8,10},{9,11},{10,... | collective-permute-start | bytes 638984 | tf_op jit(solution)/shard_map/ppermute | solution.py:504
  61.8 1.7 %collective-permute-start.10 = (s16[208,512]{1,0:T(8,128)(2,1)S(1)}, s16[208,512]{1,0:T(8,128)(2,1)S(1)}, u32[]{:S(2)}, u32[]{:S(2)}) collective-permute-start(s16[208,512]{1,0:T(8,128)(2,1)S(1)} %get-tuple-element.77), channel_id=1, source_target_pairs={{0,6},{1,7},{2,0},{3,1},{4,2},{5,3},{6,4},{7,5},{8,14},{9,15},{10,... | collective-permute-start | bytes 638984 | tf_op jit(solution)/shard_map/ppermute | solution.py:504
  63.4 2.8 %collective-permute-start.11 = (s16[208,512]{1,0:T(8,128)(2,1)S(1)}, s16[208,512]{1,0:T(8,128)(2,1)S(1)}, u32[]{:S(2)}, u32[]{:S(2)}) collective-permute-start(s16[208,512]{1,0:T(8,128)(2,1)S(1)} %get-tuple-element.78), channel_id=1, source_target_pairs={{0,4},{1,5},{2,6},{3,7},{4,0},{5,1},{6,2},{7,3},{8,12},{9,13},{10,... | collective-permute-start | bytes 638984 | tf_op jit(solution)/shard_map/ppermute | solution.py:504
  66.5 2.1 %shard_map.51 = (f32[3,4,64,512]{3,2,1,0:T(8,128)}, f32[3,4,64,512]{3,2,1,0:T(8,128)}, s16[272,512]{1,0:T(8,128)(2,1)S(1)}, s16[272,512]{1,0:T(8,128)(2,1)S(1)}) custom-call(s16[400,512]{1,0:T(8,128)(2,1)S(1)} %get-tuple-element.61.refs_0_, s16[400,512]{1,0:T(8,128)(2,1)S(1)} %collective-permute-done.14.refs_1_, ...), custom_call_target="tpu_custom_call", output_to_operand_aliasing={{0}: (6, {}), {1}: (7, {})} | custom-call | flops 1048576 | bytes 65536 | tf_op jit(solution)/shard_map/pallas_call | solution.py:432
  68.6 3.9 %collective-permute-start.17 = (s16[272,512]{1,0:T(8,128)(2,1)S(1)}, s16[272,512]{1,0:T(8,128)(2,1)S(1)}, u32[]{:S(2)}, u32[]{:S(2)}) collective-permute-start(s16[272,512]{1,0:T(8,128)(2,1)S(1)} %get-tuple-element.87), channel_id=1, source_target_pairs={{8,16},{16,8},{24,32},{32,24},{40,48},{48,40},{56,64},{64,56},{72,... | collective-permute-start | bytes 835592 | tf_op jit(solution)/shard_map/ppermute | solution.py:522
  72.6 2.5 %collective-permute-done.11.refs_3_ = s16[208,512]{1,0:T(8,128)(2,1)S(1)} collective-permute-done((s16[208,512]{1,0:T(8,128)(2,1)S(1)}, s16[208,512]{1,0:T(8,128)(2,1)S(1)}, u32[]{:S(2)}, u32[]{:S(2)}) %collective-permute-start.11) | collective-permute-done | bytes 213024 | tf_op jit(solution)/shard_map/ppermute | solution.py:504
  75.1 0.9 %shard_map.50 = (s16[144,512]{1,0:T(8,128)(2,1)S(1)}, s16[144,512]{1,0:T(8,128)(2,1)S(1)}, f32[3,64,512]{2,1,0:T(8,128)S(1)}) custom-call(s16[208,512]{1,0:T(8,128)(2,1)S(1)} %get-tuple-element.75.refs_0_, s16[208,512]{1,0:T(8,128)(2,1)S(1)} %collective-permute-done.9.refs_1_, s16[208,512]{1,0:T(8,128)(2,1)S(1)} %collective-permute-done.10.refs_2_, ...), custom_call_target="tpu_custom_call" | custom-call | flops 1048576 | bytes 65536 | tf_op jit(solution)/shard_map/pallas_call | solution.py:432
  76.0 3.9 %collective-permute-start.12 = (s16[144,512]{1,0:T(8,128)(2,1)S(1)}, s16[144,512]{1,0:T(8,128)(2,1)S(1)}, u32[]{:S(2)}, u32[]{:S(2)}) collective-permute-start(s16[144,512]{1,0:T(8,128)(2,1)S(1)} %get-tuple-element.80), channel_id=1, source_target_pairs={{8,16},{16,8},{24,32},{32,24},{40,48},{48,40},{56,64},{64,56},{72,... | collective-permute-start | bytes 442376 | tf_op jit(solution)/shard_map/ppermute | solution.py:522
  80.3 1.1 %shard_map.52 = (f32[3,4,64,512]{3,2,1,0:T(8,128)}, f32[3,4,64,512]{3,2,1,0:T(8,128)}) custom-call(s16[272,512]{1,0:T(8,128)(2,1)S(1)} %collective-permute-done.17.first_ref, s16[272,512]{1,0:T(8,128)(2,1)S(1)} %collective-permute-done.18.second_ref, f32[3,64,512]{2,1,0:T(8,128)S(1)} %get-tuple-element.89.refs_0_, ...), custom_call_target="tpu_custom_call", output_to_operand_aliasing={{0}: (3, {}), {1}: (4, {})} | custom-call | flops 1048576 | bytes 65536 | tf_op jit(solution)/shard_map/pallas_call | solution.py:481
  81.5 4.0 %collective-permute-done.12.first_ref = s16[144,512]{1,0:T(8,128)(2,1)S(1)} collective-permute-done((s16[144,512]{1,0:T(8,128)(2,1)S(1)}, s16[144,512]{1,0:T(8,128)(2,1)S(1)}, u32[]{:S(2)}, u32[]{:S(2)}) %collective-permute-start.12) | collective-permute-done | bytes 147488 | tf_op jit(solution)/shard_map/ppermute | solution.py:522
  85.4 0.8 shard_map.53
  (25 shorter events, 1.9 us)
Async XLA Ops:
  0.6 7.5 %collective-permute-start = (bf16[3,512,1024]{2,1,0:T(8,128)(2,1)}, bf16[3,512,1024]{2,1,0:T(8,128)(2,1)}, u32[]{:S(2)}, u32[]{:S(2)}) collective-permute-start(bf16[3,512,1024]{2,1,0:T(8,128)(2,1)} %refs_0_.5), channel_id=1, source_target_pairs={{0,1},{1,0},{2,3},{3,2},{4,5},{5,4},{6,7},{7,6},{8,9},{9,8},{10,11... | collective-permute-start | bytes 9437192 | tf_op jit(solution)/shard_map/ppermute | solution.py:497
  3.1 30.3 %collective-permute-start.3 = (bf16[1,512,1024]{2,1,0:T(8,128)(2,1)}, bf16[1,512,1024]{2,1,0:T(8,128)(2,1)}, u32[]{:S(2)}, u32[]{:S(2)}) collective-permute-start(bf16[1,512,1024]{2,1,0:T(8,128)(2,1)} %get-tuple-element.51), channel_id=1, source_target_pairs={{8,16},{16,8},{24,32},{32,24},{40,48},{48,40},{56,64},{64,56},{72,... | collective-permute-start | bytes 3145736 | tf_op jit(solution)/shard_map/ppermute | solution.py:522
  7.7 26.4 %collective-permute-start.4 = (bf16[1,512,1024]{2,1,0:T(8,128)(2,1)}, bf16[1,512,1024]{2,1,0:T(8,128)(2,1)}, u32[]{:S(2)}, u32[]{:S(2)}) collective-permute-start(bf16[1,512,1024]{2,1,0:T(8,128)(2,1)} %get-tuple-element.52), channel_id=1, source_target_pairs={{0,8},{8,0},{16,24},{24,16},{32,40},{40,32},{48,56},{56,48},{64,72... | collective-permute-start | bytes 3145736 | tf_op jit(solution)/shard_map/ppermute | solution.py:522
  14.1 20.0 %all-to-all-start = ((s16[4,208,512]{2,1,0:T(8,128)(2,1)}), s16[4,208,512]{2,1,0:T(8,128)(2,1)S(1)}, u32[]{:S(2)}, u32[]{:S(2)}) async-start(s16[4,208,512]{2,1,0:T(8,128)(2,1)} %get-tuple-element.53), calls=%async_computation | async-start | bytes 1703936 | tf_op jit(solution)/shard_map/all_to_all | solution.py:509
  18.6 37.5 %collective-permute-start.1 = (bf16[1,528,1024]{2,1,0:T(8,128)(2,1)}, bf16[1,528,1024]{2,1,0:T(8,128)(2,1)S(1)}, u32[]{:S(2)}, u32[]{:S(2)}) collective-permute-start(bf16[1,528,1024]{2,1,0:T(8,128)(2,1)} %get-tuple-element.49), channel_id=1, source_target_pairs={{8,16},{16,8},{24,32},{32,24},{40,48},{48,40},{56,64},{64,56},{72,... | collective-permute-start | bytes 3244040 | tf_op jit(solution)/shard_map/ppermute | solution.py:522
  21.7 34.7 %collective-permute-start.2 = (bf16[1,528,1024]{2,1,0:T(8,128)(2,1)}, bf16[1,528,1024]{2,1,0:T(8,128)(2,1)S(1)}, u32[]{:S(2)}, u32[]{:S(2)}) collective-permute-start(bf16[1,528,1024]{2,1,0:T(8,128)(2,1)} %get-tuple-element.50), channel_id=1, source_target_pairs={{0,8},{8,0},{16,24},{24,16},{32,40},{40,32},{48,56},{56,48},{64,72... | collective-permute-start | bytes 3244040 | tf_op jit(solution)/shard_map/ppermute | solution.py:522
  35.7 2.7 %collective-permute-start.7 = (bf16[1,256,1024]{2,1,0:T(8,128)(2,1)S(1)}, bf16[1,256,1024]{2,1,0:T(8,128)(2,1)S(1)}, u32[]{:S(2)}, u32[]{:S(2)}) collective-permute-start(bf16[1,256,1024]{2,1,0:T(8,128)(2,1)S(1)} %get-tuple-element.60), channel_id=1, source_target_pairs={{0,1},{1,0},{2,3},{3,2},{4,5},{5,4},{6,7},{7,6},{8,9},{9,8},{10,11... | collective-permute-start | bytes 1572872 | tf_op jit(solution)/shard_map/ppermute | solution.py:497
  35.8 2.7 %collective-permute-start.6 = (bf16[1,256,1024]{2,1,0:T(8,128)(2,1)S(1)}, bf16[1,256,1024]{2,1,0:T(8,128)(2,1)S(1)}, u32[]{:S(2)}, u32[]{:S(2)}) collective-permute-start(bf16[1,256,1024]{2,1,0:T(8,128)(2,1)S(1)} %get-tuple-element.58.refs_3_), channel_id=1, source_target_pairs={{0,1},{1,0},{2,3},{3,2},{4,5},{5,4},{6,7},{7,6},{8,9},{9,8},{10,11... | collective-permute-start | bytes 1572872 | tf_op jit(solution)/shard_map/ppermute | solution.py:497
  36.3 2.9 %collective-permute-start.5 = (bf16[1,256,1024]{2,1,0:T(8,128)(2,1)S(1)}, bf16[1,256,1024]{2,1,0:T(8,128)(2,1)S(1)}, u32[]{:S(2)}, u32[]{:S(2)}) collective-permute-start(bf16[1,256,1024]{2,1,0:T(8,128)(2,1)S(1)} %get-tuple-element.56.refs_2_), channel_id=1, source_target_pairs={{0,1},{1,0},{2,3},{3,2},{4,5},{5,4},{6,7},{7,6},{8,9},{9,8},{10,11... | collective-permute-start | bytes 1572872 | tf_op jit(solution)/shard_map/ppermute | solution.py:497
  36.4 2.8 %copy-start = (bf16[3,512,1024]{2,1,0:T(8,128)(2,1)S(1)}, bf16[3,512,1024]{2,1,0:T(8,128)(2,1)}, u32[]{:S(2)}) copy-start(bf16[3,512,1024]{2,1,0:T(8,128)(2,1)} %refs_0_.5) | copy-start | bytes 9437188
  39.3 8.9 %copy-start.1 = (s32[3,4]{1,0:T(4,128)S(1)}, s32[3,4]{1,0:T(4,128)}, u32[]{:S(2)}) copy-start(s32[3,4]{1,0:T(4,128)} %refs_4_.3) | copy-start | bytes 148
  42.9 20.5 %collective-permute-start.14 = (s16[400,512]{1,0:T(8,128)(2,1)S(1)}, s16[400,512]{1,0:T(8,128)(2,1)S(1)}, u32[]{:S(2)}, u32[]{:S(2)}) collective-permute-start(s16[400,512]{1,0:T(8,128)(2,1)S(1)} %get-tuple-element.82), channel_id=1, source_target_pairs={{0,2},{1,3},{2,4},{3,5},{4,6},{5,7},{6,0},{7,1},{8,10},{9,11},{10,... | collective-permute-start | bytes 1228808 | tf_op jit(solution)/shard_map/ppermute | solution.py:504
  44.6 21.7 %collective-permute-start.15 = (s16[400,512]{1,0:T(8,128)(2,1)S(1)}, s16[400,512]{1,0:T(8,128)(2,1)S(1)}, u32[]{:S(2)}, u32[]{:S(2)}) collective-permute-start(s16[400,512]{1,0:T(8,128)(2,1)S(1)} %get-tuple-element.83), channel_id=1, source_target_pairs={{0,6},{1,7},{2,0},{3,1},{4,2},{5,3},{6,4},{7,5},{8,14},{9,15},{10,... | collective-permute-start | bytes 1228808 | tf_op jit(solution)/shard_map/ppermute | solution.py:504
  46.2 20.3 %collective-permute-start.16 = (s16[400,512]{1,0:T(8,128)(2,1)S(1)}, s16[400,512]{1,0:T(8,128)(2,1)S(1)}, u32[]{:S(2)}, u32[]{:S(2)}) collective-permute-start(s16[400,512]{1,0:T(8,128)(2,1)S(1)} %get-tuple-element.84), channel_id=1, source_target_pairs={{0,4},{1,5},{2,6},{3,7},{4,0},{5,1},{6,2},{7,3},{8,12},{9,13},{10,... | collective-permute-start | bytes 1228808 | tf_op jit(solution)/shard_map/ppermute | solution.py:504
  58.6 1.5 %collective-permute-start.8 = (s16[4,80,256]{2,1,0:T(8,128)(2,1)S(1)}, s16[4,80,256]{2,1,0:T(8,128)(2,1)S(1)}, u32[]{:S(2)}, u32[]{:S(2)}) collective-permute-start(s16[4,80,256]{2,1,0:T(8,128)(2,1)S(1)} %get-tuple-element.74), channel_id=1, source_target_pairs={{0,1},{1,0},{2,3},{3,2},{4,5},{5,4},{6,7},{7,6},{8,9},{9,8},{10,11... | collective-permute-start | bytes 491528 | tf_op jit(solution)/shard_map/ppermute | solution.py:497
  60.1 12.5 %collective-permute-start.9 = (s16[208,512]{1,0:T(8,128)(2,1)S(1)}, s16[208,512]{1,0:T(8,128)(2,1)S(1)}, u32[]{:S(2)}, u32[]{:S(2)}) collective-permute-start(s16[208,512]{1,0:T(8,128)(2,1)S(1)} %get-tuple-element.76), channel_id=1, source_target_pairs={{0,2},{1,3},{2,4},{3,5},{4,6},{5,7},{6,0},{7,1},{8,10},{9,11},{10,... | collective-permute-start | bytes 638984 | tf_op jit(solution)/shard_map/ppermute | solution.py:504
  61.8 10.9 %collective-permute-start.10 = (s16[208,512]{1,0:T(8,128)(2,1)S(1)}, s16[208,512]{1,0:T(8,128)(2,1)S(1)}, u32[]{:S(2)}, u32[]{:S(2)}) collective-permute-start(s16[208,512]{1,0:T(8,128)(2,1)S(1)} %get-tuple-element.77), channel_id=1, source_target_pairs={{0,6},{1,7},{2,0},{3,1},{4,2},{5,3},{6,4},{7,5},{8,14},{9,15},{10,... | collective-permute-start | bytes 638984 | tf_op jit(solution)/shard_map/ppermute | solution.py:504
  63.4 11.7 %collective-permute-start.11 = (s16[208,512]{1,0:T(8,128)(2,1)S(1)}, s16[208,512]{1,0:T(8,128)(2,1)S(1)}, u32[]{:S(2)}, u32[]{:S(2)}) collective-permute-start(s16[208,512]{1,0:T(8,128)(2,1)S(1)} %get-tuple-element.78), channel_id=1, source_target_pairs={{0,4},{1,5},{2,6},{3,7},{4,0},{5,1},{6,2},{7,3},{8,12},{9,13},{10,... | collective-permute-start | bytes 638984 | tf_op jit(solution)/shard_map/ppermute | solution.py:504
  68.6 11.7 %collective-permute-start.17 = (s16[272,512]{1,0:T(8,128)(2,1)S(1)}, s16[272,512]{1,0:T(8,128)(2,1)S(1)}, u32[]{:S(2)}, u32[]{:S(2)}) collective-permute-start(s16[272,512]{1,0:T(8,128)(2,1)S(1)} %get-tuple-element.87), channel_id=1, source_target_pairs={{8,16},{16,8},{24,32},{32,24},{40,48},{48,40},{56,64},{64,56},{72,... | collective-permute-start | bytes 835592 | tf_op jit(solution)/shard_map/ppermute | solution.py:522
  72.5 7.8 %collective-permute-start.18 = (s16[272,512]{1,0:T(8,128)(2,1)S(1)}, s16[272,512]{1,0:T(8,128)(2,1)S(1)}, u32[]{:S(2)}, u32[]{:S(2)}) collective-permute-start(s16[272,512]{1,0:T(8,128)(2,1)S(1)} %get-tuple-element.88), channel_id=1, source_target_pairs={{0,8},{8,0},{16,24},{24,16},{32,40},{40,32},{48,56},{56,48},{64,72... | collective-permute-start | bytes 835592 | tf_op jit(solution)/shard_map/ppermute | solution.py:522
  76.0 9.4 %collective-permute-start.12 = (s16[144,512]{1,0:T(8,128)(2,1)S(1)}, s16[144,512]{1,0:T(8,128)(2,1)S(1)}, u32[]{:S(2)}, u32[]{:S(2)}) collective-permute-start(s16[144,512]{1,0:T(8,128)(2,1)S(1)} %get-tuple-element.80), channel_id=1, source_target_pairs={{8,16},{16,8},{24,32},{32,24},{40,48},{48,40},{56,64},{64,56},{72,... | collective-permute-start | bytes 442376 | tf_op jit(solution)/shard_map/ppermute | solution.py:522
  79.9 5.5 %collective-permute-start.13 = (s16[144,512]{1,0:T(8,128)(2,1)S(1)}, s16[144,512]{1,0:T(8,128)(2,1)S(1)}, u32[]{:S(2)}, u32[]{:S(2)}) collective-permute-start(s16[144,512]{1,0:T(8,128)(2,1)S(1)} %get-tuple-element.81), channel_id=1, source_target_pairs={{0,8},{8,0},{16,24},{24,16},{32,40},{40,32},{48,56},{56,48},{64,72... | collective-permute-start | bytes 442376 | tf_op jit(solution)/shard_map/ppermute | solution.py:522

commit v7 on v6

--- a/solution.py
+++ b/solution.py
@@ -562,14 +562,13 @@
     first2, second2, _, outs, near = lax.optimization_barrier((first2, second2, coded1[0], outs, near))
     blocks["H2"] = [("high2", 0)], [("high2", 1)]
     blocks["L2"] = [("low2", 0)], [("low2", 1)]
-    *coded2, mine_half, other_half, lines = pair_products(
-        [(0, "H2"), (1, "H2"), ("L2", 2)],
-        blocks,
-        {"own": own, "sib": near} | {"first": first2, "second": second2},
-        halved=("L2",),
-        late=True,
-    )
-    coded2 = whole(coded2, mine_half, swap(other_half))
+    late = {"own": own, "sib": near, "first": first2, "second": second2}
+    *_, mine_half, other_half, lines = pair_products(
+        [("L2", 2)], blocks, late, halved=("L2",), late=True
+    )
+    other_half = swap(other_half)
+    *coded2, _ = pair_products([(0, "H2"), (1, "H2")], blocks, late, late=True)
+    coded2 = whole(coded2, mine_half, other_half)
     got2 = to_chips(coded2)
     *outs, up1, down1 = add_parts(
         got1,

time: 86.7 us -> 86.8 us (level)
  waiting for transfers between devices: 25.5 us -> 23.8 us
  Pallas kernels: 26.5 us -> 27.8 us
    ppermute x5, waiting for transfers between devices: 2.12 us -> 0.74 us  [swap(): return lax.ppermute(value, 'occ', [(o, o ^ 1) for o in range(2 * CHIPS)])]
    pallas_call x3 -> x4, Pallas kernels: 11.8 us -> 13.1 us  [pair_products(): pl.pallas_call(functools.partial(pair_kernel, pairs, blocks, halved, name...]
  transfers between devices with their start and end apart: 20 -> 20, of which waited for: 10 -> 9; matrix products, arithmetic and copies ran while one was open for 0% -> 0% of each run, Pallas kernels for 30% -> 31%
where the time goes in v7:
time: 86.8 us; the launch traced here: 86.5 us
  starting transfers between devices  33.8 us (39%)
  Pallas kernels  27.8 us (32%)
  waiting for transfers between devices  23.8 us (27%)
  between operations  0.98 us (1%)
    ppermute x8, waiting for transfers between devices, pairwise(): done.append(lax.ppermute(value, 'space', sorted(pairs)))  20.7 us
    ppermute x8, starting transfers between devices, pairwise(): done.append(lax.ppermute(value, 'space', sorted(pairs)))  17 us
    pallas_call x4, Pallas kernels, pair_products(): pl.pallas_call(functools.partial(pair_kernel, pairs, blocks, halved, name...  13.1 us
    ppermute x6, starting transfers between devices, chips_on(): return lax.ppermute(value, 'occ', pairs)  11.6 us
    pallas_call x3, Pallas kernels, add_parts(): pl.pallas_call(kernel, out_shape=shapes, in_specs=in_specs, out_specs=out...  4.69 us
    all_to_all x1, starting transfers between devices, across(): return lax.all_to_all(value, 'occ', 0, 0, axis_index_groups=groups)  4.46 us
    pallas_call x2, Pallas kernels, bring(): pl.pallas_call(bring_kernel, out_shape=jax.ShapeDtypeStruct(value.shape,...  3.95 us
    pallas_call x1, Pallas kernels, first_factors(): pl.pallas_call(first_kernel, out_shape=[jax.ShapeDtypeStruct((1, BF, COLS...  2.41 us
  transfers between devices with their start and end apart: 20, of which 9 were waited for; matrix products, arithmetic and copies ran while one was open for 0% of the time, Pallas kernels for 31%

profile of v7, /device:TPU:96, one launch (start us, length us, event | category | flops | bytes accessed | tf_op | source)
XLA Modules:
  0.0 86.5 jit_solution(2164907116591260335)
XLA Ops:
  0.7 2.4 %shard_map.42 = (bf16[1,512,1024]{2,1,0:T(8,128)(2,1)}, bf16[1,512,1024]{2,1,0:T(8,128)(2,1)}) custom-call(bf16[3,512,1024]{2,1,0:T(8,128)(2,1)} %refs_0_.7), custom_call_target="tpu_custom_call" | custom-call | flops 1024 | bytes 1024 | tf_op jit(solution)/shard_map/pallas_call | solution.py:274
  3.1 4.5 %collective-permute-start.3 = (bf16[1,512,1024]{2,1,0:T(8,128)(2,1)}, bf16[1,512,1024]{2,1,0:T(8,128)(2,1)}, u32[]{:S(2)}, u32[]{:S(2)}) collective-permute-start(bf16[1,512,1024]{2,1,0:T(8,128)(2,1)} %get-tuple-element.51), channel_id=1, source_target_pairs={{8,16},{16,8},{24,32},{32,24},{40,48},{48,40},{56,64},{64,56},{72,... | collective-permute-start | bytes 3145736 | tf_op jit(solution)/shard_map/ppermute | solution.py:522
  8.1 6.0 %shard_map.41 = (s16[4,208,512]{2,1,0:T(8,128)(2,1)}, bf16[1,528,1024]{2,1,0:T(8,128)(2,1)}, bf16[1,528,1024]{2,1,0:T(8,128)(2,1)}) custom-call(bf16[3,512,1024]{2,1,0:T(8,128)(2,1)} %refs_0_.7, bf16[3,512,1024]{2,1,0:T(8,128)(2,1)} %collective-permute-done.refs_1_.ref, s32[3,4]{1,0:T(4,128)} %refs_4_.3), custom_call_target="tpu_custom_call" | custom-call | flops 1048576 | bytes 65536 | tf_op jit(solution)/shard_map/pallas_call | solution.py:208
  14.1 4.5 %all-to-all-start = ((s16[4,208,512]{2,1,0:T(8,128)(2,1)}), s16[4,208,512]{2,1,0:T(8,128)(2,1)S(1)}, u32[]{:S(2)}, u32[]{:S(2)}) async-start(s16[4,208,512]{2,1,0:T(8,128)(2,1)} %get-tuple-element.53), calls=%async_computation | async-start | bytes 1703936 | tf_op jit(solution)/shard_map/all_to_all | solution.py:509
  18.6 3.1 %collective-permute-start.1 = (bf16[1,528,1024]{2,1,0:T(8,128)(2,1)}, bf16[1,528,1024]{2,1,0:T(8,128)(2,1)S(1)}, u32[]{:S(2)}, u32[]{:S(2)}) collective-permute-start(bf16[1,528,1024]{2,1,0:T(8,128)(2,1)} %get-tuple-element.49), channel_id=1, source_target_pairs={{8,16},{16,8},{24,32},{32,24},{40,48},{48,40},{56,64},{64,56},{72,... | collective-permute-start | bytes 3244040 | tf_op jit(solution)/shard_map/ppermute | solution.py:522
  21.7 0.6 collective-permute-start.2
  22.2 11.2 %collective-permute-done.3.first_ref = bf16[1,512,1024]{2,1,0:T(8,128)(2,1)} collective-permute-done((bf16[1,512,1024]{2,1,0:T(8,128)(2,1)}, bf16[1,512,1024]{2,1,0:T(8,128)(2,1)}, u32[]{:S(2)}, u32[]{:S(2)}) %collective-permute-start.3) | collective-permute-done | bytes 1048608 | tf_op jit(solution)/shard_map/ppermute | solution.py:522
  33.4 0.6 collective-permute-done.4.second_ref
  34.1 1.7 %shard_map.43 = (bf16[1,256,1024]{2,1,0:T(8,128)(2,1)S(1)}, bf16[1,256,1024]{2,1,0:T(8,128)(2,1)S(1)}, bf16[1,256,1024]{2,1,0:T(8,128)(2,1)S(1)}, bf16[1,256,1024]{2,1,0:T(8,128)(2,1)S(1)}) custom-call(bf16[1,512,1024]{2,1,0:T(8,128)(2,1)} %collective-permute-done.3.first_ref, bf16[1,512,1024]{2,1,0:T(8,128)(2,1)} %collective-permute-done.4.second_ref), custom_call_target="tpu_custom_call" | custom-call | flops 1024 | bytes 1024 | tf_op jit(solution)/shard_map/pallas_call | solution.py:327
  35.8 0.5 collective-permute-start.6
  36.4 2.0 %shard_map.44.refs_1_ = bf16[3,512,1024]{2,1,0:T(8,128)(2,1)S(1)} custom-call(bf16[3,512,1024]{2,1,0:T(8,128)(2,1)} %collective-permute-done.refs_1_.ref), custom_call_target="tpu_custom_call" | custom-call | flops 1024 | bytes 1024 | tf_op jit(solution)/shard_map/pallas_call | solution.py:295
  38.5 0.7 collective-permute-done.5.refs_4_
  39.3 3.6 %shard_map.45 = (s16[400,512]{1,0:T(8,128)(2,1)S(1)}, s16[400,512]{1,0:T(8,128)(2,1)S(1)}, s16[400,512]{1,0:T(8,128)(2,1)S(1)}, s16[400,512]{1,0:T(8,128)(2,1)S(1)}) custom-call(bf16[3,512,1024]{2,1,0:T(8,128)(2,1)S(1)} %copy-done, bf16[3,512,1024]{2,1,0:T(8,128)(2,1)S(1)} %shard_map.44.refs_1_, bf16[1,256,1024]{2,1,0:T(8,128)(2,1)S(1)} %get-tuple-element.56.refs_2_, ...), custom_call_target="tpu_custom_call" | custom-call | flops 1048576 | bytes 65536 | tf_op jit(solution)/shard_map/pallas_call | solution.py:208
  42.9 1.6 %collective-permute-start.14 = (s16[400,512]{1,0:T(8,128)(2,1)S(1)}, s16[400,512]{1,0:T(8,128)(2,1)S(1)}, u32[]{:S(2)}, u32[]{:S(2)}) collective-permute-start(s16[400,512]{1,0:T(8,128)(2,1)S(1)} %get-tuple-element.82), channel_id=1, source_target_pairs={{0,2},{1,3},{2,4},{3,5},{4,6},{5,7},{6,0},{7,1},{8,10},{9,11},{10,... | collective-permute-start | bytes 1228808 | tf_op jit(solution)/shard_map/ppermute | solution.py:504
  44.6 1.7 %collective-permute-start.15 = (s16[400,512]{1,0:T(8,128)(2,1)S(1)}, s16[400,512]{1,0:T(8,128)(2,1)S(1)}, u32[]{:S(2)}, u32[]{:S(2)}) collective-permute-start(s16[400,512]{1,0:T(8,128)(2,1)S(1)} %get-tuple-element.83), channel_id=1, source_target_pairs={{0,6},{1,7},{2,0},{3,1},{4,2},{5,3},{6,4},{7,5},{8,14},{9,15},{10,... | collective-permute-start | bytes 1228808 | tf_op jit(solution)/shard_map/ppermute | solution.py:504
  46.2 2.0 %collective-permute-start.16 = (s16[400,512]{1,0:T(8,128)(2,1)S(1)}, s16[400,512]{1,0:T(8,128)(2,1)S(1)}, u32[]{:S(2)}, u32[]{:S(2)}) collective-permute-start(s16[400,512]{1,0:T(8,128)(2,1)S(1)} %get-tuple-element.84), channel_id=1, source_target_pairs={{0,4},{1,5},{2,6},{3,7},{4,0},{5,1},{6,2},{7,3},{8,12},{9,13},{10,... | collective-permute-start | bytes 1228808 | tf_op jit(solution)/shard_map/ppermute | solution.py:504
  48.2 1.7 %shard_map.46 = (f32[3,4,64,512]{3,2,1,0:T(8,128)}, f32[3,4,64,512]{3,2,1,0:T(8,128)}) custom-call(s16[4,208,512]{2,1,0:T(8,128)(2,1)S(1)} %all-to-all-done.refs_0_, s32[3,4]{1,0:T(4,128)S(1)} %copy-done.1), custom_call_target="tpu_custom_call" | custom-call | flops 1048576 | bytes 65536 | tf_op jit(solution)/shard_map/pallas_call | solution.py:432
  49.9 1.9 %shard_map.47.refs_1_ = bf16[3,512,1024]{2,1,0:T(8,128)(2,1)S(1)} custom-call(bf16[3,512,1024]{2,1,0:T(8,128)(2,1)} %collective-permute-done.refs_1_.ref), custom_call_target="tpu_custom_call" | custom-call | flops 1024 | bytes 1024 | tf_op jit(solution)/shard_map/pallas_call | solution.py:295
  51.8 4.2 %collective-permute-done.1.refs_2_ = bf16[1,528,1024]{2,1,0:T(8,128)(2,1)S(1)} collective-permute-done((bf16[1,528,1024]{2,1,0:T(8,128)(2,1)}, bf16[1,528,1024]{2,1,0:T(8,128)(2,1)S(1)}, u32[]{:S(2)}, u32[]{:S(2)}) %collective-permute-start.1) | collective-permute-done | bytes 1081376 | tf_op jit(solution)/shard_map/ppermute | solution.py:522
  56.4 1.5 %shard_map.49 = (s16[16,512]{1,0:T(8,128)(2,1)}, s16[16,512]{1,0:T(8,128)(2,1)}, s16[16,512]{1,0:T(8,128)(2,1)}, s16[16,512]{1,0:T(8,128)(2,1)}, s16[4,80,256]{2...) custom-call(bf16[3,512,1024]{2,1,0:T(8,128)(2,1)S(1)} %copy-done, ...), custom_call_target="tpu_custom_call" | custom-call | flops 1048576 | bytes 65536 | tf_op jit(solution)/shard_map/pallas_call | solution.py:208
  57.8 2.0 %shard_map.48 = (s16[144,512]{1,0:T(8,128)(2,1)S(1)}, s16[144,512]{1,0:T(8,128)(2,1)S(1)}, s16[144,512]{1,0:T(8,128)(2,1)S(1)}, s16[144,512]{1,0:T(8,128)(2,1)S(1)}, f32[16,512]{1,0:T(8,128)}) custom-call(bf16[3,512,1024]{2,1,0:T(8,128)(2,1)S(1)} %copy-done, bf16[3,512,1024]{2,1,0:T(8,128)(2,1)S(1)} %shard_map.47.refs_1_, ...), custom_call_target="tpu_custom_call" | custom-call | flops 1048576 | bytes 65536 | tf_op jit(solution)/shard_map/pallas_call | solution.py:208
  59.9 1.6 %collective-permute-start.9 = (s16[208,512]{1,0:T(8,128)(2,1)S(1)}, s16[208,512]{1,0:T(8,128)(2,1)S(1)}, u32[]{:S(2)}, u32[]{:S(2)}) collective-permute-start(s16[208,512]{1,0:T(8,128)(2,1)S(1)} %get-tuple-element.76), channel_id=1, source_target_pairs={{0,2},{1,3},{2,4},{3,5},{4,6},{5,7},{6,0},{7,1},{8,10},{9,11},{10,... | collective-permute-start | bytes 638984 | tf_op jit(solution)/shard_map/ppermute | solution.py:504
  61.6 1.7 %collective-permute-start.10 = (s16[208,512]{1,0:T(8,128)(2,1)S(1)}, s16[208,512]{1,0:T(8,128)(2,1)S(1)}, u32[]{:S(2)}, u32[]{:S(2)}) collective-permute-start(s16[208,512]{1,0:T(8,128)(2,1)S(1)} %get-tuple-element.77), channel_id=1, source_target_pairs={{0,6},{1,7},{2,0},{3,1},{4,2},{5,3},{6,4},{7,5},{8,14},{9,15},{10,... | collective-permute-start | bytes 638984 | tf_op jit(solution)/shard_map/ppermute | solution.py:504
  63.3 3.0 %collective-permute-start.11 = (s16[208,512]{1,0:T(8,128)(2,1)S(1)}, s16[208,512]{1,0:T(8,128)(2,1)S(1)}, u32[]{:S(2)}, u32[]{:S(2)}) collective-permute-start(s16[208,512]{1,0:T(8,128)(2,1)S(1)} %get-tuple-element.78), channel_id=1, source_target_pairs={{0,4},{1,5},{2,6},{3,7},{4,0},{5,1},{6,2},{7,3},{8,12},{9,13},{10,... | collective-permute-start | bytes 638984 | tf_op jit(solution)/shard_map/ppermute | solution.py:504
  66.4 2.1 %shard_map.52 = (f32[3,4,64,512]{3,2,1,0:T(8,128)}, f32[3,4,64,512]{3,2,1,0:T(8,128)}, s16[272,512]{1,0:T(8,128)(2,1)S(1)}, s16[272,512]{1,0:T(8,128)(2,1)S(1)}) custom-call(s16[400,512]{1,0:T(8,128)(2,1)S(1)} %get-tuple-element.61.refs_0_, s16[400,512]{1,0:T(8,128)(2,1)S(1)} %collective-permute-done.14.refs_1_, ...), custom_call_target="tpu_custom_call", output_to_operand_aliasing={{0}: (6, {}), {1}: (7, {})} | custom-call | flops 1048576 | bytes 65536 | tf_op jit(solution)/shard_map/pallas_call | solution.py:432
  68.5 4.3 %collective-permute-start.17 = (s16[272,512]{1,0:T(8,128)(2,1)S(1)}, s16[272,512]{1,0:T(8,128)(2,1)S(1)}, u32[]{:S(2)}, u32[]{:S(2)}) collective-permute-start(s16[272,512]{1,0:T(8,128)(2,1)S(1)} %get-tuple-element.87), channel_id=1, source_target_pairs={{8,16},{16,8},{24,32},{32,24},{40,48},{48,40},{56,64},{64,56},{72,... | collective-permute-start | bytes 835592 | tf_op jit(solution)/shard_map/ppermute | solution.py:522
  72.9 2.2 %collective-permute-done.11.refs_3_ = s16[208,512]{1,0:T(8,128)(2,1)S(1)} collective-permute-done((s16[208,512]{1,0:T(8,128)(2,1)S(1)}, s16[208,512]{1,0:T(8,128)(2,1)S(1)}, u32[]{:S(2)}, u32[]{:S(2)}) %collective-permute-start.11) | collective-permute-done | bytes 213024 | tf_op jit(solution)/shard_map/ppermute | solution.py:504
  75.1 0.9 %shard_map.51 = (s16[144,512]{1,0:T(8,128)(2,1)S(1)}, s16[144,512]{1,0:T(8,128)(2,1)S(1)}, f32[3,64,512]{2,1,0:T(8,128)S(1)}) custom-call(s16[208,512]{1,0:T(8,128)(2,1)S(1)} %get-tuple-element.75.refs_0_, s16[208,512]{1,0:T(8,128)(2,1)S(1)} %collective-permute-done.9.refs_1_, s16[208,512]{1,0:T(8,128)(2,1)S(1)} %collective-permute-done.10.refs_2_, ...), custom_call_target="tpu_custom_call" | custom-call | flops 1048576 | bytes 65536 | tf_op jit(solution)/shard_map/pallas_call | solution.py:432
  76.0 3.9 %collective-permute-start.12 = (s16[144,512]{1,0:T(8,128)(2,1)S(1)}, s16[144,512]{1,0:T(8,128)(2,1)S(1)}, u32[]{:S(2)}, u32[]{:S(2)}) collective-permute-start(s16[144,512]{1,0:T(8,128)(2,1)S(1)} %get-tuple-element.80), channel_id=1, source_target_pairs={{8,16},{16,8},{24,32},{32,24},{40,48},{48,40},{56,64},{64,56},{72,... | collective-permute-start | bytes 442376 | tf_op jit(solution)/shard_map/ppermute | solution.py:522
  80.3 1.1 %shard_map.53 = (f32[3,4,64,512]{3,2,1,0:T(8,128)}, f32[3,4,64,512]{3,2,1,0:T(8,128)}) custom-call(s16[272,512]{1,0:T(8,128)(2,1)S(1)} %collective-permute-done.17.first_ref, s16[272,512]{1,0:T(8,128)(2,1)S(1)} %collective-permute-done.18.second_ref, f32[3,64,512]{2,1,0:T(8,128)S(1)} %get-tuple-element.89.refs_0_, ...), custom_call_target="tpu_custom_call", output_to_operand_aliasing={{0}: (3, {}), {1}: (4, {})} | custom-call | flops 1048576 | bytes 65536 | tf_op jit(solution)/shard_map/pallas_call | solution.py:481
  81.5 4.1 %collective-permute-done.12.first_ref = s16[144,512]{1,0:T(8,128)(2,1)S(1)} collective-permute-done((s16[144,512]{1,0:T(8,128)(2,1)S(1)}, s16[144,512]{1,0:T(8,128)(2,1)S(1)}, u32[]{:S(2)}, u32[]{:S(2)}) %collective-permute-start.12) | collective-permute-done | bytes 147488 | tf_op jit(solution)/shard_map/ppermute | solution.py:522
  85.5 0.8 shard_map.54
  (26 shorter events, 1.7 us)
Async XLA Ops:
  0.6 7.5 %collective-permute-start = (bf16[3,512,1024]{2,1,0:T(8,128)(2,1)}, bf16[3,512,1024]{2,1,0:T(8,128)(2,1)}, u32[]{:S(2)}, u32[]{:S(2)}) collective-permute-start(bf16[3,512,1024]{2,1,0:T(8,128)(2,1)} %refs_0_.7), channel_id=1, source_target_pairs={{0,1},{1,0},{2,3},{3,2},{4,5},{5,4},{6,7},{7,6},{8,9},{9,8},{10,11... | collective-permute-start | bytes 9437192 | tf_op jit(solution)/shard_map/ppermute | solution.py:497
  3.1 30.3 %collective-permute-start.3 = (bf16[1,512,1024]{2,1,0:T(8,128)(2,1)}, bf16[1,512,1024]{2,1,0:T(8,128)(2,1)}, u32[]{:S(2)}, u32[]{:S(2)}) collective-permute-start(bf16[1,512,1024]{2,1,0:T(8,128)(2,1)} %get-tuple-element.51), channel_id=1, source_target_pairs={{8,16},{16,8},{24,32},{32,24},{40,48},{48,40},{56,64},{64,56},{72,... | collective-permute-start | bytes 3145736 | tf_op jit(solution)/shard_map/ppermute | solution.py:522
  7.7 26.4 %collective-permute-start.4 = (bf16[1,512,1024]{2,1,0:T(8,128)(2,1)}, bf16[1,512,1024]{2,1,0:T(8,128)(2,1)}, u32[]{:S(2)}, u32[]{:S(2)}) collective-permute-start(bf16[1,512,1024]{2,1,0:T(8,128)(2,1)} %get-tuple-element.52), channel_id=1, source_target_pairs={{0,8},{8,0},{16,24},{24,16},{32,40},{40,32},{48,56},{56,48},{64,72... | collective-permute-start | bytes 3145736 | tf_op jit(solution)/shard_map/ppermute | solution.py:522
  14.1 19.9 %all-to-all-start = ((s16[4,208,512]{2,1,0:T(8,128)(2,1)}), s16[4,208,512]{2,1,0:T(8,128)(2,1)S(1)}, u32[]{:S(2)}, u32[]{:S(2)}) async-start(s16[4,208,512]{2,1,0:T(8,128)(2,1)} %get-tuple-element.53), calls=%async_computation | async-start | bytes 1703936 | tf_op jit(solution)/shard_map/all_to_all | solution.py:509
  18.6 37.5 %collective-permute-start.1 = (bf16[1,528,1024]{2,1,0:T(8,128)(2,1)}, bf16[1,528,1024]{2,1,0:T(8,128)(2,1)S(1)}, u32[]{:S(2)}, u32[]{:S(2)}) collective-permute-start(bf16[1,528,1024]{2,1,0:T(8,128)(2,1)} %get-tuple-element.49), channel_id=1, source_target_pairs={{8,16},{16,8},{24,32},{32,24},{40,48},{48,40},{56,64},{64,56},{72,... | collective-permute-start | bytes 3244040 | tf_op jit(solution)/shard_map/ppermute | solution.py:522
  21.7 34.7 %collective-permute-start.2 = (bf16[1,528,1024]{2,1,0:T(8,128)(2,1)}, bf16[1,528,1024]{2,1,0:T(8,128)(2,1)S(1)}, u32[]{:S(2)}, u32[]{:S(2)}) collective-permute-start(bf16[1,528,1024]{2,1,0:T(8,128)(2,1)} %get-tuple-element.50), channel_id=1, source_target_pairs={{0,8},{8,0},{16,24},{24,16},{32,40},{40,32},{48,56},{56,48},{64,72... | collective-permute-start | bytes 3244040 | tf_op jit(solution)/shard_map/ppermute | solution.py:522
  35.7 2.7 %collective-permute-start.7 = (bf16[1,256,1024]{2,1,0:T(8,128)(2,1)S(1)}, bf16[1,256,1024]{2,1,0:T(8,128)(2,1)S(1)}, u32[]{:S(2)}, u32[]{:S(2)}) collective-permute-start(bf16[1,256,1024]{2,1,0:T(8,128)(2,1)S(1)} %get-tuple-element.60), channel_id=1, source_target_pairs={{0,1},{1,0},{2,3},{3,2},{4,5},{5,4},{6,7},{7,6},{8,9},{9,8},{10,11... | collective-permute-start | bytes 1572872 | tf_op jit(solution)/shard_map/ppermute | solution.py:497
  35.8 2.7 %collective-permute-start.6 = (bf16[1,256,1024]{2,1,0:T(8,128)(2,1)S(1)}, bf16[1,256,1024]{2,1,0:T(8,128)(2,1)S(1)}, u32[]{:S(2)}, u32[]{:S(2)}) collective-permute-start(bf16[1,256,1024]{2,1,0:T(8,128)(2,1)S(1)} %get-tuple-element.58.refs_3_), channel_id=1, source_target_pairs={{0,1},{1,0},{2,3},{3,2},{4,5},{5,4},{6,7},{7,6},{8,9},{9,8},{10,11... | collective-permute-start | bytes 1572872 | tf_op jit(solution)/shard_map/ppermute | solution.py:497
  36.3 2.9 %collective-permute-start.5 = (bf16[1,256,1024]{2,1,0:T(8,128)(2,1)S(1)}, bf16[1,256,1024]{2,1,0:T(8,128)(2,1)S(1)}, u32[]{:S(2)}, u32[]{:S(2)}) collective-permute-start(bf16[1,256,1024]{2,1,0:T(8,128)(2,1)S(1)} %get-tuple-element.56.refs_2_), channel_id=1, source_target_pairs={{0,1},{1,0},{2,3},{3,2},{4,5},{5,4},{6,7},{7,6},{8,9},{9,8},{10,11... | collective-permute-start | bytes 1572872 | tf_op jit(solution)/shard_map/ppermute | solution.py:497
  36.4 2.8 %copy-start = (bf16[3,512,1024]{2,1,0:T(8,128)(2,1)S(1)}, bf16[3,512,1024]{2,1,0:T(8,128)(2,1)}, u32[]{:S(2)}) copy-start(bf16[3,512,1024]{2,1,0:T(8,128)(2,1)} %refs_0_.7) | copy-start | bytes 9437188
  39.3 8.9 %copy-start.1 = (s32[3,4]{1,0:T(4,128)S(1)}, s32[3,4]{1,0:T(4,128)}, u32[]{:S(2)}) copy-start(s32[3,4]{1,0:T(4,128)} %refs_4_.3) | copy-start | bytes 148
  42.9 20.4 %collective-permute-start.14 = (s16[400,512]{1,0:T(8,128)(2,1)S(1)}, s16[400,512]{1,0:T(8,128)(2,1)S(1)}, u32[]{:S(2)}, u32[]{:S(2)}) collective-permute-start(s16[400,512]{1,0:T(8,128)(2,1)S(1)} %get-tuple-element.82), channel_id=1, source_target_pairs={{0,2},{1,3},{2,4},{3,5},{4,6},{5,7},{6,0},{7,1},{8,10},{9,11},{10,... | collective-permute-start | bytes 1228808 | tf_op jit(solution)/shard_map/ppermute | solution.py:504
  44.6 21.7 %collective-permute-start.15 = (s16[400,512]{1,0:T(8,128)(2,1)S(1)}, s16[400,512]{1,0:T(8,128)(2,1)S(1)}, u32[]{:S(2)}, u32[]{:S(2)}) collective-permute-start(s16[400,512]{1,0:T(8,128)(2,1)S(1)} %get-tuple-element.83), channel_id=1, source_target_pairs={{0,6},{1,7},{2,0},{3,1},{4,2},{5,3},{6,4},{7,5},{8,14},{9,15},{10,... | collective-permute-start | bytes 1228808 | tf_op jit(solution)/shard_map/ppermute | solution.py:504
  46.2 20.2 %collective-permute-start.16 = (s16[400,512]{1,0:T(8,128)(2,1)S(1)}, s16[400,512]{1,0:T(8,128)(2,1)S(1)}, u32[]{:S(2)}, u32[]{:S(2)}) collective-permute-start(s16[400,512]{1,0:T(8,128)(2,1)S(1)} %get-tuple-element.84), channel_id=1, source_target_pairs={{0,4},{1,5},{2,6},{3,7},{4,0},{5,1},{6,2},{7,3},{8,12},{9,13},{10,... | collective-permute-start | bytes 1228808 | tf_op jit(solution)/shard_map/ppermute | solution.py:504
  57.8 2.0 %collective-permute-start.8 = (s16[4,80,256]{2,1,0:T(8,128)(2,1)S(1)}, s16[4,80,256]{2,1,0:T(8,128)(2,1)S(1)}, u32[]{:S(2)}, u32[]{:S(2)}) collective-permute-start(s16[4,80,256]{2,1,0:T(8,128)(2,1)S(1)} %get-tuple-element.74), channel_id=1, source_target_pairs={{0,1},{1,0},{2,3},{3,2},{4,5},{5,4},{6,7},{7,6},{8,9},{9,8},{10,11... | collective-permute-start | bytes 491528 | tf_op jit(solution)/shard_map/ppermute | solution.py:497
  59.9 12.9 %collective-permute-start.9 = (s16[208,512]{1,0:T(8,128)(2,1)S(1)}, s16[208,512]{1,0:T(8,128)(2,1)S(1)}, u32[]{:S(2)}, u32[]{:S(2)}) collective-permute-start(s16[208,512]{1,0:T(8,128)(2,1)S(1)} %get-tuple-element.76), channel_id=1, source_target_pairs={{0,2},{1,3},{2,4},{3,5},{4,6},{5,7},{6,0},{7,1},{8,10},{9,11},{10,... | collective-permute-start | bytes 638984 | tf_op jit(solution)/shard_map/ppermute | solution.py:504
  61.6 11.3 %collective-permute-start.10 = (s16[208,512]{1,0:T(8,128)(2,1)S(1)}, s16[208,512]{1,0:T(8,128)(2,1)S(1)}, u32[]{:S(2)}, u32[]{:S(2)}) collective-permute-start(s16[208,512]{1,0:T(8,128)(2,1)S(1)} %get-tuple-element.77), channel_id=1, source_target_pairs={{0,6},{1,7},{2,0},{3,1},{4,2},{5,3},{6,4},{7,5},{8,14},{9,15},{10,... | collective-permute-start | bytes 638984 | tf_op jit(solution)/shard_map/ppermute | solution.py:504
  63.3 11.9 %collective-permute-start.11 = (s16[208,512]{1,0:T(8,128)(2,1)S(1)}, s16[208,512]{1,0:T(8,128)(2,1)S(1)}, u32[]{:S(2)}, u32[]{:S(2)}) collective-permute-start(s16[208,512]{1,0:T(8,128)(2,1)S(1)} %get-tuple-element.78), channel_id=1, source_target_pairs={{0,4},{1,5},{2,6},{3,7},{4,0},{5,1},{6,2},{7,3},{8,12},{9,13},{10,... | collective-permute-start | bytes 638984 | tf_op jit(solution)/shard_map/ppermute | solution.py:504
  68.5 11.8 %collective-permute-start.17 = (s16[272,512]{1,0:T(8,128)(2,1)S(1)}, s16[272,512]{1,0:T(8,128)(2,1)S(1)}, u32[]{:S(2)}, u32[]{:S(2)}) collective-permute-start(s16[272,512]{1,0:T(8,128)(2,1)S(1)} %get-tuple-element.87), channel_id=1, source_target_pairs={{8,16},{16,8},{24,32},{32,24},{40,48},{48,40},{56,64},{64,56},{72,... | collective-permute-start | bytes 835592 | tf_op jit(solution)/shard_map/ppermute | solution.py:522
  72.8 7.5 %collective-permute-start.18 = (s16[272,512]{1,0:T(8,128)(2,1)S(1)}, s16[272,512]{1,0:T(8,128)(2,1)S(1)}, u32[]{:S(2)}, u32[]{:S(2)}) collective-permute-start(s16[272,512]{1,0:T(8,128)(2,1)S(1)} %get-tuple-element.88), channel_id=1, source_target_pairs={{0,8},{8,0},{16,24},{24,16},{32,40},{40,32},{48,56},{56,48},{64,72... | collective-permute-start | bytes 835592 | tf_op jit(solution)/shard_map/ppermute | solution.py:522
  76.0 9.5 %collective-permute-start.12 = (s16[144,512]{1,0:T(8,128)(2,1)S(1)}, s16[144,512]{1,0:T(8,128)(2,1)S(1)}, u32[]{:S(2)}, u32[]{:S(2)}) collective-permute-start(s16[144,512]{1,0:T(8,128)(2,1)S(1)} %get-tuple-element.80), channel_id=1, source_target_pairs={{8,16},{16,8},{24,32},{32,24},{40,48},{48,40},{56,64},{64,56},{72,... | collective-permute-start | bytes 442376 | tf_op jit(solution)/shard_map/ppermute | solution.py:522
  80.0 5.5 %collective-permute-start.13 = (s16[144,512]{1,0:T(8,128)(2,1)S(1)}, s16[144,512]{1,0:T(8,128)(2,1)S(1)}, u32[]{:S(2)}, u32[]{:S(2)}) collective-permute-start(s16[144,512]{1,0:T(8,128)(2,1)S(1)} %get-tuple-element.81), channel_id=1, source_target_pairs={{0,8},{8,0},{16,24},{24,16},{32,40},{40,32},{48,56},{56,48},{64,72... | collective-permute-start | bytes 442376 | tf_op jit(solution)/shard_map/ppermute | solution.py:522
